TPU v7x, 512 devices: a whole 4x4x16 slice. The times are simulated.
512 devices in a mesh: dp: 64 (over z, x), tensor: 8 (over y, core).
Axes of the slice: x: 4, y: 4, z: 16, core: 2. Of those that a mesh axis runs over, the one named last changes fastest.
Arguments:
- partials: bfloat16 [16384, 32768], P('dp', 'tensor'), may hold values from -6 to 6
- resid: bfloat16 [16384, 4096], P('dp', 'tensor'), may hold values from -6 to 6
- low: bfloat16 [16384, 4096], P('dp', 'tensor'), may hold values from -6 to 6
- mid: bfloat16 [16384, 4096], P('dp', 'tensor'), may hold values from -6 to 6
- joining: bfloat16 [3, 4096, 4096], P(None, 'tensor', 'dp'), may hold values from -0.0546875 to 0.0546875
- step_in: bfloat16 [4096, 128], replicated, may hold values from -0.09375 to 0.09375
- step_out: bfloat16 [128, 4096], replicated, may hold values from -0.5 to 0.5
- targets: bfloat16 [16384, 128], P('dp'), may hold values from -6 to 6
- lengths: int32 [64, 8], P('dp'), may hold values from 1 to 128, 256 in all within a row
- loss_mask: int32 [16384], P('dp'), may hold values 0 or 1
- dest: int32 [16384, 1], P('dp'), may hold values from 0 to 63; in each aligned block of 256 rows (0 to 255, 256 to 511, ...) at most 8 rows name the same one
Outputs:
- grad_start: float32 [32768, 4096], P(('dp', 'tensor'))
- final_state: bfloat16 [32768, 4096], P(('dp', 'tensor'))
Inputs may be any that keep to these rules, and one draw needn't show every extreme that they name: `dest`: among the tokens of one sequence group no draft shard is named by more than 8 tokens, a bound that some block reaches. `lengths`: each row sums to 256; the longest is exactly 128.
All inputs are finite; a program needn't handle non-finite values. No bound on the sum of `loss_mask` on one device may be relied on, other than what follows from the above.
Results may differ from a plain program's by a relative error of at most 0.025.
Values may be sent and summed in bfloat16 or wider, within the bound.
No kernel may reach another device: no remote copies, remote signals or barrier semaphores. Data moves between devices by JAX's collectives and lax.ppermute only.
A program may use at most 128 MiB of HBM per device.

v0:
```python
import jax
import jax.numpy as jnp
from jax import lax
from jax.sharding import PartitionSpec as P


def remaining_steps(sizes, mask, count):
    ends = jnp.cumsum(sizes)
    starts = ends - sizes
    place = jnp.arange(count, dtype=jnp.int32)[:, None]
    inside = (place >= starts[None, :]) & (place < ends[None, :])
    offset = jnp.sum(jnp.where(inside, place - starts[None, :], 0), axis=1)
    length = jnp.sum(jnp.where(inside, sizes[None, :], 0), axis=1)
    return (jnp.minimum(length - 1 - offset, 3) * mask).astype(jnp.float32)


def draft_chain(step_in, step_out, start, goal, left):
    state = start
    saved = []
    for step in range(3):
        inv = lax.rsqrt(jnp.mean(state * state, axis=-1, keepdims=True) + 1e-06)
        normed = (state * inv).astype(jnp.bfloat16)
        pre = jnp.dot(normed, step_in, preferred_element_type=jnp.float32)
        active = jax.nn.silu(pre).astype(jnp.bfloat16)
        saved.append((state, inv, pre))
        state = state + jnp.dot(active, step_out, preferred_element_type=jnp.float32)
    target = goal.astype(jnp.float32)
    back = jnp.zeros(start.shape, jnp.float32)
    for step in (2, 1, 0):
        prev, inv, pre = saved[step]
        live = (left > step).astype(jnp.float32)
        dact = jnp.dot(back.astype(jnp.bfloat16), step_out.T, preferred_element_type=jnp.float32)
        sig = jax.nn.sigmoid(pre)
        dpre = (dact * (sig + pre * sig * (1.0 - sig)) + live * (pre - target)).astype(jnp.bfloat16)
        dnorm = jnp.dot(dpre, step_in.T, preferred_element_type=jnp.float32)
        back = back + inv * dnorm - prev * inv**3 * jnp.mean(dnorm * prev, axis=-1, keepdims=True)
    return (state, back)


def per_device(
    partials, resid, low, mid, joining, step_in, step_out, targets, lengths, loss_mask, dest
):
    groups = lax.axis_size("dp")
    shards = lax.axis_size("tensor")
    count = resid.shape[0]
    capacity = 2 * count // groups
    slots = groups * capacity
    share = slots // shards
    first = lax.axis_index("tensor") * share
    summed = lax.psum_scatter(
        partials.astype(jnp.float32).astype(jnp.bfloat16), "tensor", scatter_dimension=1, tiled=True
    ).astype(jnp.float32)
    high = (summed + resid.astype(jnp.float32)).astype(jnp.bfloat16)
    feats = jnp.stack([low, mid, high], axis=1)
    left = remaining_steps(lengths[0], loss_mask, count)
    target = dest[:, 0]
    hits = (target[:, None] == jnp.arange(groups, dtype=jnp.int32)[None, :]).astype(jnp.int32)
    rank = jnp.sum(jnp.cumsum(hits, axis=0) * hits, axis=1) - 1
    slot = target * capacity + rank
    spread = (jnp.arange(slots, dtype=jnp.int32)[:, None] == slot[None, :]).astype(jnp.bfloat16)
    moved_goal = jnp.dot(spread, targets, preferred_element_type=jnp.float32).astype(jnp.bfloat16)
    moved_left = jnp.dot(
        spread, left[:, None].astype(jnp.bfloat16), preferred_element_type=jnp.float32
    ).astype(jnp.bfloat16)
    moved = jnp.dot(spread, feats.reshape(count, -1), preferred_element_type=jnp.float32).astype(
        jnp.bfloat16
    )
    got = (
        lax.all_to_all(
            moved.reshape(groups, capacity, -1), "dp", split_axis=0, concat_axis=0, tiled=True
        ),
        lax.all_to_all(
            moved_goal.reshape(groups, capacity, -1), "dp", split_axis=0, concat_axis=0, tiled=True
        ),
        lax.all_to_all(
            moved_left.reshape(groups, capacity, 1), "dp", split_axis=0, concat_axis=0, tiled=True
        ),
    )
    arrived = got[0].reshape(slots, 3, -1)
    term = jnp.einsum(
        "nlf,lfc->nc",
        arrived,
        lax.all_gather(joining, "dp", axis=2, tiled=True),
        preferred_element_type=jnp.float32,
    )
    start_rows = lax.psum_scatter(
        term.astype(jnp.bfloat16), "tensor", scatter_dimension=0, tiled=True
    )
    goal_rows = lax.dynamic_slice_in_dim(got[1].reshape(slots, -1), first, share, 0)
    left_rows = lax.dynamic_slice_in_dim(got[2].reshape(slots, 1), first, share, 0).astype(
        jnp.float32
    )
    final, grad = draft_chain(
        step_in, step_out, start_rows.astype(jnp.float32), goal_rows, left_rows
    )
    return (grad, final.astype(jnp.bfloat16))


def solution(mesh):
    in_specs = (
        P("dp", "tensor"),
        P("dp", "tensor"),
        P("dp", "tensor"),
        P("dp", "tensor"),
        P(None, "tensor", "dp"),
        P(),
        P(),
        P("dp", None),
        P("dp", None),
        P("dp"),
        P("dp", None),
    )
    out_specs = (P(("dp", "tensor"), None), P(("dp", "tensor"), None))
    return jax.shard_map(
        per_device, mesh=mesh, in_specs=in_specs, out_specs=out_specs, check_vma=False
    )
```

profile of v0, /device:TPU:1, one launch (start us, length us, event | category | flops | bytes accessed | tf_op | source)
XLA Modules:
  0.0 297.8 jit_solution(10201999179466091385)
XLA Ops:
  8.1 4.2 %copy.29 = bf16[256,4096]{0,1:T(8,128)(2,1)} copy(bf16[256,4096]{1,0:T(8,128)(2,1)} %param.11) | data formatting | bytes 4194304 | tf_op args[0]
  12.9 0.6 reduce-window.10
  14.3 43.1 %reduce-scatter.3.cloned.1.call-done = bf16[256,512]{0,1:T(8,128)(2,1)} async-done(((bf16[256,4096]{0,1:T(8,128)(2,1)}), bf16[256,512]{0,1:T(8,128)(2,1)}) %reduce-scatter.3.cloned.1.call-update) | async-done | bytes 262160 | tf_op jit(solution)/shard_map/reduce_scatter | solution.py:50
  57.4 1.0 fusion.30
  58.5 0.6 fusion.1
  59.1 95.6 %all_to_all.15 = bf16[64,8,1536]{2,1,0:T(8,128)(2,1)} all-to-all(bf16[64,8,1536]{2,1,0:T(8,128)(2,1)S(1)} %fusion.1), channel_id=1, replica_groups=mesh['dp'=64,'tensor'=8] {'dp'}, dimensions={0} | all-to-all | bytes 3145728 | tf_op jit(solution)/shard_map/all_to_all | solution.py:69
  154.7 5.6 %reshape.123 = bf16[512,3,512]{2,1,0:T(4,128)(2,1)} reshape(bf16[64,8,1536]{2,1,0:T(8,128)(2,1)} %all_to_all.15) | data formatting | bytes 3145728 | tf_op jit(solution)/shard_map/reshape | solution.py:79
  160.3 51.8 %all-gather.2.cloned.1.call-done = bf16[3,512,4096]{1,2,0:T(8,128)(2,1)} async-done(((bf16[3,512,64]{1,2,0:T(8,128)(2,1)}), bf16[3,512,4096]{1,2,0:T(8,128)(2,1)}) %all-gather.2.cloned.1.call-update) | async-done | bytes 12582928 | tf_op jit(solution)/shard_map/all_gather | solution.py:83
  212.1 13.4 %bitcast_convert_fusion = bf16[512,4096]{1,0:T(8,128)(2,1)} fusion(bf16[3,512,4096]{1,2,0:T(8,128)(2,1)} %all-gather.2.cloned.1.call-done, bf16[512,3,512]{2,1,0:T(4,128)(2,1)} %reshape.123), kind=kOutput, calls=%fused_computation | convolution fusion | flops 6444548096 | bytes 18350080 | tf_op jit(solution)/shard_map/nlf,lfc->nc/dot_general | solution.py:80
  225.6 0.6 copy-done.10
  226.8 0.7 reshape.136
  227.5 12.3 %all-to-all-start.1 = ((bf16[64,8,1]{1,2,0:T(2,128)(2,1)}), bf16[64,8,1]{1,2,0:T(2,128)(2,1)S(1)}, u32[]{:S(2)}, u32[]{:S(2)}) async-start(bf16[64,8,1]{1,2,0:T(2,128)(2,1)} %reshape.136), calls=%async_computation.3 | async-start | bytes 65536 | tf_op jit(solution)/shard_map/all_to_all | solution.py:75
  239.8 0.9 fusion.3
  240.7 12.5 %all-to-all-done.1 = bf16[64,8,1]{1,2,0:T(2,128)(2,1)S(1)} async-done(((bf16[64,8,1]{1,2,0:T(2,128)(2,1)}), bf16[64,8,1]{1,2,0:T(2,128)(2,1)S(1)}, u32[]{:S(2)}, u32[]{:S(2)}) %all-to-all-start.1) | async-done | bytes 1056 | tf_op jit(solution)/shard_map/all_to_all | solution.py:75
  253.2 4.8 %all-to-all-start.2 = ((bf16[64,8,128]{2,1,0:T(8,128)(2,1)}), bf16[64,8,128]{2,1,0:T(8,128)(2,1)S(1)}, u32[]{:S(2)}, u32[]{:S(2)}) async-start(bf16[64,8,128]{2,1,0:T(8,128)(2,1)} %fusion.3), calls=%async_computation.4 | async-start | bytes 262144 | tf_op jit(solution)/shard_map/all_to_all | solution.py:72
  258.3 9.8 %reduce-scatter.5.cloned.1.call-done = bf16[64,4096]{1,0:T(8,128)(2,1)} async-done(((bf16[512,4096]{1,0:T(8,128)(2,1)}), bf16[64,4096]{1,0:T(8,128)(2,1)}) %reduce-scatter.5.cloned.1.call-update) | async-done | bytes 524304 | tf_op jit(solution)/shard_map/reduce_scatter | solution.py:86
  268.1 1.3 fusion.13
  269.5 1.4 fusion.20
  272.7 1.1 fusion
  273.8 2.4 multiply_reduce_fusion.1
  276.2 4.1 %multiply_reduce_fusion = (f32[64]{0:T(128)S(1)}, f32[64,4096]{1,0:T(8,128)}) fusion(f32[64,4096]{1,0:T(8,128)} %copy-done.2, bf16[4096,128]{1,0:T(8,128)(2,1)S(1)} %copy-done.1, bf16[128,4096]{1,0:T(8,128)(2,1)S(1)} %copy-done, f32[64,128]{1,0:T(8,128)S(1)} %fusion.18, f32[64]{0:T(128)S(1)} %get-tuple-element.5, bf16[512,128]{1,0:T(8,128)(2,1)S(1)} %bitcast.65, ...), kind=kOutput, calls=%fused_computation.32 | convolution fusion | flops 136159168 | bytes 6342916 | tf_op jit(solution)/shard_map/dot_general | solution.py:35
  280.3 3.3 %multiply_subtract_fusion = f32[64,4096]{1,0:T(8,128)} fusion(f32[64,4096]{1,0:T(8,128)} %copy-done.2, f32[64,4096]{1,0:T(8,128)} %get-tuple-element.20, f32[64]{0:T(128)S(1)} %broadcast_multiply_fusion.1, f32[64]{0:T(128)S(1)} %get-tuple-element.9, f32[64]{0:T(128)S(1)} %get-tuple-element.10, f32[64]{0:T(128)S(1)} %broadcast_multiply_fusion.2, ...), kind=kLoop, calls=%fused_computation.31 | loop fusion | flops 2359296 | bytes 5244416 | tf_op jit(solution)/shard_map/sub | solution.py:36
  283.7 3.9 %fusion.17 = (f32[64]{0:T(128)S(1)}, f32[64,4096]{1,0:T(8,128)}) fusion(bf16[64,4096]{1,0:T(8,128)(2,1)} %reduce-scatter.5.cloned.1.call-done, bf16[4096,128]{1,0:T(8,128)(2,1)S(1)} %copy-done.1, bf16[128,4096]{1,0:T(8,128)(2,1)S(1)} %copy-done, f32[64,4096]{1,0:T(8,128)} %multiply_subtract_fusion, f32[64,128]{1,0:T(8,128)S(1)} %fusion.20, ...), kind=kOutput, calls=%fused_computation.30 | convolution fusion | flops 135372736 | bytes 4768516 | tf_op jit(solution)/shard_map/dot_general | solution.py:35
  287.6 2.8 fusion.16
  (60 shorter events, 4.1 us)
Async XLA Ops:
  8.0 262.9 %copy-start = (bf16[128,4096]{1,0:T(8,128)(2,1)S(1)}, bf16[128,4096]{1,0:T(8,128)(2,1)}, u32[]{:S(2)}) copy-start(bf16[128,4096]{1,0:T(8,128)(2,1)} %param.17) | copy-start | bytes 3145732
  8.0 49.4 %reduce-scatter.3.cloned.1.call-start = ((), (), s32[]{:S(2)}) async-start(), calls=%async_computation.5 | async-start | bytes 2359296 | tf_op jit(solution)/shard_map/reduce_scatter | solution.py:50
  12.2 0.7 copy-start.8
  12.2 1.5 copy-start.5
  12.2 1.7 copy-start.6
  12.2 1.8 copy-start.7
  12.3 199.9 %all-gather.2.cloned.1.call-start = ((), (), s32[]{:S(2)}) async-start(), calls=%async_computation.6 | async-start | bytes 12779520 | tf_op jit(solution)/shard_map/all_gather | solution.py:83
  12.8 255.3 %reduce-scatter.5.cloned.1.call-start = ((), (), s32[]{:S(2)}) async-start(), calls=%async_computation.7 | async-start | bytes 4718592 | tf_op jit(solution)/shard_map/reduce_scatter | solution.py:86
  225.6 0.7 copy-start.10
  225.6 0.9 copy-start.9
  225.6 14.2 %copy-start.11 = (bf16[256,128]{1,0:T(8,128)(2,1)S(1)}, bf16[256,128]{1,0:T(8,128)(2,1)}, u32[]{:S(2)}) copy-start(bf16[256,128]{1,0:T(8,128)(2,1)} %param.18) | copy-start | bytes 196612
  225.6 43.9 %copy-start.1 = (bf16[4096,128]{1,0:T(8,128)(2,1)S(1)}, bf16[4096,128]{1,0:T(8,128)(2,1)}, u32[]{:S(2)}) copy-start(bf16[4096,128]{1,0:T(8,128)(2,1)} %param.16) | copy-start | bytes 3145732
  227.5 25.8 %all-to-all-start.1 = ((bf16[64,8,1]{1,2,0:T(2,128)(2,1)}), bf16[64,8,1]{1,2,0:T(2,128)(2,1)S(1)}, u32[]{:S(2)}, u32[]{:S(2)}) async-start(bf16[64,8,1]{1,2,0:T(2,128)(2,1)} %reshape.136), calls=%async_computation.3 | async-start | bytes 65536 | tf_op jit(solution)/shard_map/all_to_all | solution.py:75
  253.2 20.5 %all-to-all-start.2 = ((bf16[64,8,128]{2,1,0:T(8,128)(2,1)}), bf16[64,8,128]{2,1,0:T(8,128)(2,1)S(1)}, u32[]{:S(2)}, u32[]{:S(2)}) async-start(bf16[64,8,128]{2,1,0:T(8,128)(2,1)} %fusion.3), calls=%async_computation.4 | async-start | bytes 262144 | tf_op jit(solution)/shard_map/all_to_all | solution.py:72
  268.1 2.8 copy-start.3
  271.3 1.0 copy-start.2
  283.7 3.9 %copy-start.4 = (bf16[64,4096]{1,0:T(8,128)(2,1)S(1)}, bf16[64,4096]{1,0:T(8,128)(2,1)}, u32[]{:S(2)}) copy-start(bf16[64,4096]{1,0:T(8,128)(2,1)} %reduce-scatter.5.cloned.1.call-done) | copy-start | bytes 1572868
Sparse Core Ops, SparseCore 0:
  12.4 44.9 reduce-scatter.2
  225.7 42.3 reduce-scatter.4
Sparse Core Ops, SparseCore 1:
  15.7 196.4 all-gather.1
where the time goes:
time: 300 us; the launch traced here: 298 us
  waiting for transfers between devices  118 us (39%)
  blocking collectives  95.6 us (32%)
  matrix products  29.5 us (10%)
  starting transfers between devices  17.2 us (6%)
  between operations  15.7 us (5%)
  local copies, waits for them, and re-layouts  12 us (4%)
  other arithmetic  9.79 us (3%)
    all_to_all x1, blocking collectives, per_device(): lax.all_to_all(moved.reshape(groups, capacity, -1), 'dp', split_axis=0, c...  95.6 us
    all_gather x1, waiting for transfers between devices, per_device(): lax.all_gather(joining, 'dp', axis=2, tiled=True)  51.8 us
    reduce_scatter x1, waiting for transfers between devices, per_device(): lax.psum_scatter(partials.astype(jnp.float32).astype(jnp.bfloat16), 'tens...  43.1 us
    dot_general x1, matrix products, per_device(): jnp.einsum('nlf,lfc->nc', arrived, lax.all_gather(joining, 'dp', axis=2,...  13.4 us
    all_to_all x1, waiting for transfers between devices, per_device(): lax.all_to_all(moved_left.reshape(groups, capacity, 1), 'dp', split_axis=...  12.5 us
    all_to_all x1, starting transfers between devices, per_device(): lax.all_to_all(moved_left.reshape(groups, capacity, 1), 'dp', split_axis=...  12.3 us
    dot_general x3, matrix products, draft_chain(): dnorm = jnp.dot(dpre, step_in.T, preferred_element_type=jnp.float32)  10.4 us
    reduce_scatter x1, waiting for transfers between devices, per_device(): lax.psum_scatter(term.astype(jnp.bfloat16), 'tensor', scatter_dimension=0...  9.82 us
  transfers between devices with their start and end apart: 5, of which 4 were waited for; matrix products, arithmetic and copies ran while one was open for 5% of the time, Pallas kernels for 0%

commit v1 on v0

v1 whole, which is shorter than its diff:
```python
import jax
import jax.numpy as jnp
from jax import lax
from jax.experimental import pallas as pl
from jax.experimental.pallas import tpu as pltpu
from jax.sharding import Mesh, PartitionSpec as P

BF = jnp.bfloat16
F32 = jnp.float32
NT = (((1,), (1,)), ((), ()))
NN = (((1,), (0,)), ((), ()))
VMEM = pl.BlockSpec(memory_space=pltpu.VMEM)


def dot(a, b, dims=NN):
    return lax.dot_general(a, b, dims, preferred_element_type=F32)


def remaining_steps(sizes, mask, count):
    ends = jnp.cumsum(sizes)
    starts = ends - sizes
    place = jnp.arange(count, dtype=jnp.int32)[:, None]
    inside = (place >= starts[None, :]) & (place < ends[None, :])
    offset = jnp.sum(jnp.where(inside, place - starts[None, :], 0), axis=1)
    length = jnp.sum(jnp.where(inside, sizes[None, :], 0), axis=1)
    return (jnp.minimum(length - 1 - offset, 3) * mask).astype(F32)


def term_kernel(half_ref, pair_ref, high_ref, rows_ref, out_ref):
    weights = [rows_ref[0, :, 0, :, piece].reshape(256, 512) for piece in range(3)]
    for group in range(4):
        total = dot(pair_ref[group, 0:256], weights[0], NT)
        total += dot(pair_ref[group, 256:512], weights[1], NT)
        total += dot(high_ref[group], weights[2], NT)
        total = total.astype(BF)
        for part in range(2):
            out_ref[part, group * 256 : (group + 1) * 256, :] = total[:, part * 128 : (part + 1) * 128]


def term_half(half, pair, high, rows):
    return pl.pallas_call(
        term_kernel,
        grid_spec=pltpu.PrefetchScalarGridSpec(
            num_scalar_prefetch=1,
            grid=(2,),
            in_specs=[
                pl.BlockSpec((4, 528, 512), lambda i, h: (0, 0, 0)),
                pl.BlockSpec((4, 256, 512), lambda i, h: (0, 0, 0)),
                pl.BlockSpec((1, 2, 1, 2, 3, 64, 512), lambda i, h: (i, 0, h[0], 0, 0, 0, 0)),
            ],
            out_specs=pl.BlockSpec((2, 1024, 128), lambda i, h: (i, 0, 0)),
        ),
        out_shape=jax.ShapeDtypeStruct((4, 1024, 128), BF),
        compiler_params=pltpu.CompilerParams(vmem_limit_bytes=40 * 1024 * 1024),
        cost_estimate=pl.CostEstimate(
            flops=2 * 1024 * 1536 * 512, bytes_accessed=6 * 1024 * 1024, transcendentals=0
        ),
        name="term_half",
    )(half, pair, high, rows)


def spread_kernel(terms_ref, pair_ref, out_ref):
    total = terms_ref[0].astype(F32)
    for part in range(1, 4):
        total += terms_ref[part].astype(F32)
    joined = total.astype(BF)
    row = lax.broadcasted_iota(jnp.int32, (1024, 256), 0)
    for two in range(2):
        moved = None
        for group in (2 * two, 2 * two + 1):
            shard = pair_ref[group, 512:513, 0:256].astype(jnp.int32)
            rank = pair_ref[group, 512:513, 256:512].astype(jnp.int32)
            slot = shard * 16 + rank
            hot = jnp.where(row == slot, 1.0, 0.0).astype(BF)
            part = dot(hot, joined[group * 256 : (group + 1) * 256])
            moved = part if moved is None else moved + part
        out_ref[:, two * 16 : (two + 1) * 16, :] = moved.astype(BF).reshape(64, 16, 128)


def spread(terms, pair):
    return pl.pallas_call(
        spread_kernel,
        in_specs=[VMEM, VMEM],
        out_specs=VMEM,
        out_shape=jax.ShapeDtypeStruct((64, 32, 128), BF),
        compiler_params=pltpu.CompilerParams(vmem_limit_bytes=40 * 1024 * 1024),
        name="spread",
    )(terms, pair)


def chain_kernel(rows_ref, side_ref, in_ref, out_ref, grad_ref, final_ref, h0, h1, h2):
    for block in range(8):
        tiles = [
            jnp.concatenate([rows_ref[block, x], rows_ref[block, 4 + x]], axis=0).astype(F32)
            for x in range(4)
        ]
        for k in range(4):
            lane = (k // 2) * 64
            x = 2 * (k % 2)
            h0[:, block * 512 + k * 128 : block * 512 + (k + 1) * 128] = jnp.concatenate(
                [tiles[x][:, lane : lane + 64], tiles[x + 1][:, lane : lane + 64]], axis=1
            )
    side = side_ref[...].astype(F32)
    goal = side[:, 0:8, :].reshape(64, 128)
    left = side[:, 8:16, :].reshape(64, 128)
    states = (h0, h1, h2)
    invs, pres = [], []
    for step in range(3):
        state = states[step][...]
        inv = lax.rsqrt(jnp.sum(state * state, axis=-1, keepdims=True) * (1.0 / 4096) + 1e-06)
        pre = dot((state * inv).astype(BF), in_ref[...])
        active = (pre * jax.nn.sigmoid(pre)).astype(BF)
        invs.append(inv)
        pres.append(pre)
        after = state + dot(active, out_ref[...])
        if step < 2:
            states[step + 1][...] = after
        else:
            final_ref[...] = after.astype(BF)
    for step in (2, 1, 0):
        inv, pre = invs[step], pres[step]
        live = jnp.where(left > step, pre - goal, 0.0)
        if step == 2:
            dpre = live.astype(BF)
        else:
            dact = dot(grad_ref[...].astype(BF), out_ref[...], NT)
            sig = jax.nn.sigmoid(pre)
            dpre = (dact * (sig + pre * sig * (1.0 - sig)) + live).astype(BF)
        dnorm = dot(dpre, in_ref[...], NT)
        state = states[step][...]
        mean = jnp.sum(dnorm * state, axis=-1, keepdims=True) * (1.0 / 4096)
        back = inv * dnorm - state * (inv * inv * inv * mean)
        if step < 2:
            back = grad_ref[...] + back
        grad_ref[...] = back


def chain(rows, side, step_in, step_out):
    return pl.pallas_call(
        chain_kernel,
        in_specs=[VMEM] * 4,
        out_specs=[VMEM] * 2,
        out_shape=[
            jax.ShapeDtypeStruct((64, 4096), F32),
            jax.ShapeDtypeStruct((64, 4096), BF),
        ],
        scratch_shapes=[pltpu.VMEM((64, 4096), F32)] * 3,
        compiler_params=pltpu.CompilerParams(vmem_limit_bytes=40 * 1024 * 1024),
        name="chain",
    )(rows, side, step_in, step_out)


def per_device(
    partials, resid, low, mid, joining, step_in, step_out, targets, lengths, loss_mask, dest
):
    tensor = ("y", "c")
    dp = ("z", "x")
    rows = lax.all_gather(jnp.swapaxes(joining, 1, 2), "z")
    rows = rows.reshape(2, 2, 2, 2, 3, 64, 512)
    split = jnp.swapaxes(partials.reshape(256, 8, 512), 0, 1)
    summed = lax.psum_scatter(split, tensor, scatter_dimension=0, tiled=False).astype(F32)

    shard = dest[:, 0]
    earlier = jnp.arange(256)[:, None] > jnp.arange(256)[None, :]
    rank = jnp.sum(((shard[:, None] == shard[None, :]) & earlier).astype(jnp.int32), axis=1)
    place = lax.rem(lax.axis_index("x"), 2) * 8 + rank
    extra = jnp.concatenate([shard, place]).astype(BF)[None, :]
    extra = jnp.pad(extra, ((0, 15), (0, 0)))
    pair = jnp.concatenate([low, mid, extra], axis=0)
    pair = lax.all_to_all(
        jnp.broadcast_to(pair[None], (4, 528, 512)), "x", split_axis=0, concat_axis=0, tiled=True
    )

    left = remaining_steps(lengths[0], loss_mask, 256).astype(BF)
    side = jnp.concatenate([targets, jnp.broadcast_to(left[:, None], (256, 128))], axis=1)
    slot = jnp.arange(512, dtype=jnp.int32)[:, None] == (shard * 8 + rank)[None, :]
    side = jnp.dot(slot.astype(BF), side, preferred_element_type=F32).astype(BF)
    side = jnp.swapaxes(side.reshape(64, 8, 2, 128), 1, 2).reshape(64, 16, 128)
    side = lax.all_to_all(side, dp, split_axis=0, concat_axis=0, tiled=True)
    me = lax.axis_index("y") * 2 + lax.axis_index("c")
    side = lax.dynamic_slice_in_dim(side, me * 8, 8, 0)

    high = (summed + resid.astype(F32)).astype(BF)
    high = lax.all_to_all(
        jnp.broadcast_to(high[None], (4, 256, 512)), "x", split_axis=0, concat_axis=0, tiled=True
    )

    core = lax.axis_index("c").astype(jnp.int32).reshape(1)
    other = term_half(1 - core, pair, high, rows)
    other = lax.ppermute(other, "c", [(0, 1), (1, 0)])
    own = term_half(core, pair, high, rows)
    terms = (own.astype(F32) + other.astype(F32)).astype(BF)
    terms = lax.all_to_all(terms, "y", split_axis=0, concat_axis=0, tiled=True)
    moved = spread(terms, pair)
    moved = lax.all_to_all(moved, dp, split_axis=0, concat_axis=0, tiled=True)
    moved = lax.all_to_all(
        moved.reshape(8, 256, 128), tensor, split_axis=0, concat_axis=0, tiled=True
    )
    grad, final = chain(moved.reshape(8, 8, 32, 128), side, step_in, step_out)
    return (grad, final)


def solution(mesh):
    fine = Mesh(mesh.devices.reshape(16, 4, 4, 2), ("z", "x", "y", "c"))
    dp, tensor = ("z", "x"), ("y", "c")
    in_specs = (
        P(dp, tensor),
        P(dp, tensor),
        P(dp, tensor),
        P(dp, tensor),
        P(None, tensor, dp),
        P(),
        P(),
        P(dp, None),
        P(dp, None),
        P(dp),
        P(dp, None),
    )
    out_specs = (P(dp + tensor, None), P(dp + tensor, None))
    return jax.shard_map(
        per_device, mesh=fine, in_specs=in_specs, out_specs=out_specs, check_vma=False
    )
```

time: 300 us -> 224 us (0.75)
  blocking collectives: 95.6 us -> 37.5 us
  matrix products: 29.5 us -> 0.94 us
  starting transfers between devices: 17.2 us -> 43 us
  waiting for transfers between devices: 118 us -> 102 us
  Pallas kernels: 0 us -> 12 us
  other arithmetic: 9.79 us -> 2.79 us
    all_to_all x1, blocking collectives: 95.6 us -> 37.5 us  [per_device(): moved = lax.all_to_all(moved, dp, split_axis=0, concat_axis=0, tiled=True)]
    all_gather x1, waiting for transfers between devices: 51.8 us -> 12.2 us  [per_device(): rows = lax.all_gather(jnp.swapaxes(joining, 1, 2), 'z')]
    all_to_all x2 -> x5, waiting for transfers between devices: 12.5 us -> 51.1 us  [the longest x1 16.8 us: per_device(): side = lax.all_to_all(side, dp, split_axis=0, concat_axis=0, tiled=True)]
    dot_general x13 -> x1, matrix products: 29.5 us -> 0.94 us  [per_device(): side = jnp.dot(slot.astype(BF), side, preferred_element_type=F32).astype(BF)]
    reduce_scatter x2 -> x1, waiting for transfers between devices: 52.9 us -> 37.9 us  [per_device(): lax.psum_scatter(split, tensor, scatter_dimension=0, tiled=False)]
    all_to_all x2 -> x5, starting transfers between devices: 17.1 us -> 31.3 us  [the longest x1 10.4 us: per_device(): side = lax.all_to_all(side, dp, split_axis=0, concat_axis=0, tiled=True)]
    pallas_call x0 -> x4, Pallas kernels: none -> 12 us  [the longest x1 6.84 us: chain(): pl.pallas_call(chain_kernel, in_specs=[VMEM] * 4, out_specs=[VMEM] * 2, o...]
    ppermute x0 -> x1, starting transfers between devices: none -> 11.6 us  [per_device(): other = lax.ppermute(other, 'c', [(0, 1), (1, 0)])]
  transfers between devices with their start and end apart: 5 -> 8, of which waited for: 4 -> 6; matrix products, arithmetic and copies ran while one was open for 5% -> 2% of each run, Pallas kernels for 0% -> 1%
where the time goes in v1:
time: 224 us
  waiting for transfers between devices  102 us (46%)
  starting transfers between devices  43 us (19%)
  blocking collectives  37.5 us (17%)
  between operations  15.7 us (7%)
  Pallas kernels  12 us (5%)
  local copies, waits for them, and re-layouts  9.97 us (4%)
  other arithmetic  2.79 us (1%)
    reduce_scatter x1, waiting for transfers between devices, per_device(): lax.psum_scatter(split, tensor, scatter_dimension=0, tiled=False)  37.9 us
    all_to_all x1, blocking collectives, per_device(): moved = lax.all_to_all(moved, dp, split_axis=0, concat_axis=0, tiled=True)  37.5 us
    all_to_all x1, waiting for transfers between devices, per_device(): side = lax.all_to_all(side, dp, split_axis=0, concat_axis=0, tiled=True)  16.8 us
    all_to_all x1, waiting for transfers between devices, per_device(): terms = lax.all_to_all(terms, 'y', split_axis=0, concat_axis=0, tiled=True)  13.2 us
    all_gather x1, waiting for transfers between devices, per_device(): rows = lax.all_gather(jnp.swapaxes(joining, 1, 2), 'z')  12.2 us
    all_to_all x1, waiting for transfers between devices, per_device(): lax.all_to_all(jnp.broadcast_to(high[None], (4, 256, 512)), 'x', split_ax...  11.7 us
    ppermute x1, starting transfers between devices, per_device(): other = lax.ppermute(other, 'c', [(0, 1), (1, 0)])  11.6 us
    all_to_all x1, starting transfers between devices, per_device(): side = lax.all_to_all(side, dp, split_axis=0, concat_axis=0, tiled=True)  10.4 us
  transfers between devices with their start and end apart: 8, of which 6 were waited for; matrix products, arithmetic and copies ran while one was open for 2% of the time, Pallas kernels for 1%

profile of v1, /device:TPU:1, one launch (start us, length us, event | category | flops | bytes accessed | tf_op | source)
XLA Modules:
  0.0 223.6 jit_solution(8534017283683616969)
XLA Ops:
  8.0 4.1 %copy.19 = bf16[256,4096]{0,1:T(8,128)(2,1)} copy(bf16[256,4096]{1,0:T(8,128)(2,1)} %param.11) | data formatting | bytes 4194304 | tf_op args[0]
  13.2 1.5 broadcast_in_dim.22
  14.8 5.0 %all-to-all-start = ((bf16[4,528,512]{2,1,0:T(8,128)(2,1)}), bf16[4,528,512]{2,1,0:T(8,128)(2,1)S(1)}, u32[]{:S(2)}, u32[]{:S(2)}) async-start(bf16[4,528,512]{2,1,0:T(8,128)(2,1)} %broadcast_in_dim.22), calls=%async_computation | async-start | bytes 4325376 | tf_op jit(solution)/shard_map/all_to_all | solution.py:170
  19.9 37.9 %reduce-scatter.2.cloned.1.call-done = bf16[1,256,512]{1,2,0:T(8,128)(2,1)} async-done(((bf16[8,256,512]{1,2,0:T(8,128)(2,1)}), bf16[1,256,512]{1,2,0:T(8,128)(2,1)}) %reduce-scatter.2.cloned.1.call-update) | async-done | bytes 262160 | tf_op jit(solution)/shard_map/reduce_scatter | solution.py:161
  57.7 1.0 fusion.1
  58.9 1.1 broadcast_in_dim.23
  60.0 3.5 %all-to-all-start.1 = ((bf16[4,256,512]{2,1,0:T(8,128)(2,1)}), bf16[4,256,512]{2,1,0:T(8,128)(2,1)S(1)}, u32[]{:S(2)}, u32[]{:S(2)}) async-start(bf16[4,256,512]{2,1,0:T(8,128)(2,1)} %broadcast_in_dim.23), calls=%async_computation.2 | async-start | bytes 2097152 | tf_op jit(solution)/shard_map/all_to_all | solution.py:184
  63.5 11.7 %all-to-all-done.1.high_ref = bf16[4,256,512]{2,1,0:T(8,128)(2,1)S(1)} async-done(((bf16[4,256,512]{2,1,0:T(8,128)(2,1)}), bf16[4,256,512]{2,1,0:T(8,128)(2,1)S(1)}, u32[]{:S(2)}, u32[]{:S(2)}) %all-to-all-start.1) | async-done | bytes 1048608 | tf_op jit(solution)/shard_map/all_to_all | solution.py:184
  75.2 12.2 %all-gather.3.cloned.1.call-done = bf16[48,64,512]{2,1,0:T(8,128)(2,1)} async-done(((bf16[3,64,512]{2,1,0:T(8,128)(2,1)}), bf16[48,64,512]{2,1,0:T(8,128)(2,1)}) %all-gather.3.cloned.1.call-update) | async-done | bytes 3145744 | tf_op jit(solution)/shard_map/all_gather | solution.py:158
  87.4 1.9 copy-done
  89.3 2.2 term_half.3
  91.5 11.6 %collective-permute-start = (bf16[4,1024,128]{2,1,0:T(8,128)(2,1)S(1)}, bf16[4,1024,128]{2,1,0:T(8,128)(2,1)S(1)}, u32[]{:S(2)}, u32[]{:S(2)}) collective-permute-start(bf16[4,1024,128]{2,1,0:T(8,128)(2,1)S(1)} %term_half.3), channel_id=1, source_target_pairs={{0,1},{1,0},{2,3},{3,2},{4,5},{5,4},{6,7},{7,6},{8,9},{9,8},{10,11... | collective-permute-start | bytes 3145736 | tf_op jit(solution)/shard_map/ppermute | solution.py:190
  103.1 2.2 term_half.2
  105.4 1.3 add_convert_fusion
  106.7 4.2 %all-to-all-start.2 = ((bf16[4,1024,128]{2,1,0:T(8,128)(2,1)}), bf16[4,1024,128]{2,1,0:T(8,128)(2,1)S(1)}, u32[]{:S(2)}, u32[]{:S(2)}) async-start(bf16[4,1024,128]{2,1,0:T(8,128)(2,1)} %add_convert_fusion), calls=%async_computation.3 | async-start | bytes 2097152 | tf_op jit(solution)/shard_map/all_to_all | solution.py:193
  111.2 0.9 fusion
  112.2 13.2 %all-to-all-done.2.terms_ref = bf16[4,1024,128]{2,1,0:T(8,128)(2,1)S(1)} async-done(((bf16[4,1024,128]{2,1,0:T(8,128)(2,1)}), bf16[4,1024,128]{2,1,0:T(8,128)(2,1)S(1)}, u32[]{:S(2)}, u32[]{:S(2)}) %all-to-all-start.2) | async-done | bytes 1048608 | tf_op jit(solution)/shard_map/all_to_all | solution.py:193
  125.4 10.4 %all-to-all-start.5 = ((bf16[64,16,128]{2,1,0:T(8,128)(2,1)}), bf16[64,16,128]{2,1,0:T(8,128)(2,1)S(1)}, u32[]{:S(2)}, u32[]{:S(2)}) async-start(bf16[64,16,128]{2,1,0:T(8,128)(2,1)} %fusion), calls=%async_computation.6 | async-start | bytes 524288 | tf_op jit(solution)/shard_map/all_to_all | solution.py:179
  136.6 0.8 copy-done.2
  137.4 16.8 %all-to-all-done.5 = bf16[64,16,128]{2,1,0:T(8,128)(2,1)S(1)} async-done(((bf16[64,16,128]{2,1,0:T(8,128)(2,1)}), bf16[64,16,128]{2,1,0:T(8,128)(2,1)S(1)}, u32[]{:S(2)}, u32[]{:S(2)}) %all-to-all-start.5) | async-done | bytes 262176 | tf_op jit(solution)/shard_map/all_to_all | solution.py:179
  154.2 37.5 %all_to_all.30 = bf16[64,32,128]{2,1,0:T(8,128)(2,1)} all-to-all(bf16[64,32,128]{2,1,0:T(8,128)(2,1)} %copy-done.2), channel_id=1, replica_groups=mesh['z'=16,'x'=4,'y'=4,'c'=2] {'z','x'}, dimensions={0} | all-to-all | bytes 1048576 | tf_op jit(solution)/shard_map/all_to_all | solution.py:195
  191.7 8.2 %all-to-all-start.4 = ((bf16[8,256,128]{2,1,0:T(8,128)(2,1)}), bf16[8,256,128]{2,1,0:T(8,128)(2,1)S(1)}, u32[]{:S(2)}, u32[]{:S(2)}) async-start(bf16[8,256,128]{2,1,0:T(8,128)(2,1)} %bitcast.8), calls=%async_computation.5 | async-start | bytes 1048576 | tf_op jit(solution)/shard_map/all_to_all | solution.py:196
  199.9 9.5 %all-to-all-done.4 = bf16[8,256,128]{2,1,0:T(8,128)(2,1)S(1)} async-done(((bf16[8,256,128]{2,1,0:T(8,128)(2,1)}), bf16[8,256,128]{2,1,0:T(8,128)(2,1)S(1)}, u32[]{:S(2)}, u32[]{:S(2)}) %all-to-all-start.4) | async-done | bytes 524320 | tf_op jit(solution)/shard_map/all_to_all | solution.py:196
  209.4 6.8 %chain.1 = (f32[64,4096]{1,0:T(8,128)}, bf16[64,4096]{1,0:T(8,128)(2,1)}) custom-call(bf16[8,8,32,128]{3,2,1,0:T(8,128)(2,1)S(1)} %bitcast.31, bf16[8,16,128]{2,1,0:T(8,128)(2,1)S(1)} %constant_dynamic-slice_fusion.side_ref, bf16[4096,128]{1,0:T(8,128)(2,1)S(1)} %copy-done.3, bf16[128,4096]{1,0:T(8,128)(2,1)S(1)} %copy-done.4), custom_call_target="tpu_custom_call" | custom-call | tf_op jit(solution)/shard_map/chain/pallas_call | solution.py:139
  (43 shorter events, 2.5 us)
Async XLA Ops:
  8.0 49.7 %reduce-scatter.2.cloned.1.call-start = ((), (), s32[]{:S(2)}) async-start(), calls=%async_computation.7 | async-start | bytes 2359296 | tf_op jit(solution)/shard_map/reduce_scatter | solution.py:161
  12.1 0.7 copy-start.8
  12.1 1.0 copy-start.6
  12.1 1.0 copy-start.7
  12.2 75.3 %all-gather.3.cloned.1.call-start = ((), (), s32[]{:S(2)}) async-start(), calls=%async_computation.8 | async-start | bytes 3342336 | tf_op jit(solution)/shard_map/all_gather | solution.py:158
  14.8 5.0 %copy-start.5 = (bf16[256,512]{1,0:T(8,128)(2,1)S(1)}, bf16[256,512]{1,0:T(8,128)(2,1)}, u32[]{:S(2)}) copy-start(bf16[256,512]{1,0:T(8,128)(2,1)} %param.12) | copy-start | bytes 786436
  14.8 44.2 %all-to-all-start = ((bf16[4,528,512]{2,1,0:T(8,128)(2,1)}), bf16[4,528,512]{2,1,0:T(8,128)(2,1)S(1)}, u32[]{:S(2)}, u32[]{:S(2)}) async-start(bf16[4,528,512]{2,1,0:T(8,128)(2,1)} %broadcast_in_dim.22), calls=%async_computation | async-start | bytes 4325376 | tf_op jit(solution)/shard_map/all_to_all | solution.py:170
  60.0 15.2 %all-to-all-start.1 = ((bf16[4,256,512]{2,1,0:T(8,128)(2,1)}), bf16[4,256,512]{2,1,0:T(8,128)(2,1)S(1)}, u32[]{:S(2)}, u32[]{:S(2)}) async-start(bf16[4,256,512]{2,1,0:T(8,128)(2,1)} %broadcast_in_dim.23), calls=%async_computation.2 | async-start | bytes 2097152 | tf_op jit(solution)/shard_map/all_to_all | solution.py:184
  87.4 1.9 copy-start
  89.3 13.8 %copy-start.1 = (bf16[48,64,512]{2,1,0:T(8,128)(2,1)S(1)}, bf16[48,64,512]{2,1,0:T(8,128)(2,1)}, u32[]{:S(2)}) copy-start(bf16[48,64,512]{2,1,0:T(8,128)(2,1)} %all-gather.3.cloned.1.call-done) | copy-start | bytes 9437188
  91.5 13.9 %collective-permute-start = (bf16[4,1024,128]{2,1,0:T(8,128)(2,1)S(1)}, bf16[4,1024,128]{2,1,0:T(8,128)(2,1)S(1)}, u32[]{:S(2)}, u32[]{:S(2)}) collective-permute-start(bf16[4,1024,128]{2,1,0:T(8,128)(2,1)S(1)} %term_half.3), channel_id=1, source_target_pairs={{0,1},{1,0},{2,3},{3,2},{4,5},{5,4},{6,7},{7,6},{8,9},{9,8},{10,11... | collective-permute-start | bytes 3145736 | tf_op jit(solution)/shard_map/ppermute | solution.py:190
  105.3 5.5 %copy-start.10 = (s32[1,8]{1,0:T(1,128)S(1)}, s32[1,8]{1,0:T(1,128)}, u32[]{:S(2)}) copy-start(s32[1,8]{1,0:T(1,128)} %param.19) | copy-start | bytes 100
  105.4 5.8 %copy-start.9 = (s32[256]{0:T(256)S(1)}, s32[256]{0:T(256)}, u32[]{:S(2)}) copy-start(s32[256]{0:T(256)} %param.20) | copy-start | bytes 3076
  105.4 5.9 %copy-start.11 = (bf16[256,128]{1,0:T(8,128)(2,1)S(1)}, bf16[256,128]{1,0:T(8,128)(2,1)}, u32[]{:S(2)}) copy-start(bf16[256,128]{1,0:T(8,128)(2,1)} %param.18) | copy-start | bytes 196612
  106.7 18.7 %all-to-all-start.2 = ((bf16[4,1024,128]{2,1,0:T(8,128)(2,1)}), bf16[4,1024,128]{2,1,0:T(8,128)(2,1)S(1)}, u32[]{:S(2)}, u32[]{:S(2)}) async-start(bf16[4,1024,128]{2,1,0:T(8,128)(2,1)} %add_convert_fusion), calls=%async_computation.3 | async-start | bytes 2097152 | tf_op jit(solution)/shard_map/all_to_all | solution.py:193
  125.4 28.8 %all-to-all-start.5 = ((bf16[64,16,128]{2,1,0:T(8,128)(2,1)}), bf16[64,16,128]{2,1,0:T(8,128)(2,1)S(1)}, u32[]{:S(2)}, u32[]{:S(2)}) async-start(bf16[64,16,128]{2,1,0:T(8,128)(2,1)} %fusion), calls=%async_computation.6 | async-start | bytes 524288 | tf_op jit(solution)/shard_map/all_to_all | solution.py:179
  136.6 0.8 copy-start.2
  137.4 72.0 %copy-start.3 = (bf16[4096,128]{1,0:T(8,128)(2,1)S(1)}, bf16[4096,128]{1,0:T(8,128)(2,1)}, u32[]{:S(2)}) copy-start(bf16[4096,128]{1,0:T(8,128)(2,1)} %in_ref.1) | copy-start | bytes 3145732
  137.4 72.0 %copy-start.4 = (bf16[128,4096]{1,0:T(8,128)(2,1)S(1)}, bf16[128,4096]{1,0:T(8,128)(2,1)}, u32[]{:S(2)}) copy-start(bf16[128,4096]{1,0:T(8,128)(2,1)} %out_ref.1) | copy-start | bytes 3145732
  191.7 17.7 %all-to-all-start.4 = ((bf16[8,256,128]{2,1,0:T(8,128)(2,1)}), bf16[8,256,128]{2,1,0:T(8,128)(2,1)S(1)}, u32[]{:S(2)}, u32[]{:S(2)}) async-start(bf16[8,256,128]{2,1,0:T(8,128)(2,1)} %bitcast.8), calls=%async_computation.5 | async-start | bytes 1048576 | tf_op jit(solution)/shard_map/all_to_all | solution.py:196
Sparse Core Ops, SparseCore 0:
  12.3 45.4 reduce-scatter.1
Sparse Core Ops, SparseCore 1:
  14.7 72.7 all-gather.2

commit v2 on v1

--- a/solution.py
+++ b/solution.py
@@ -26,31 +26,73 @@
     return (jnp.minimum(length - 1 - offset, 3) * mask).astype(F32)
 
 
-def term_kernel(half_ref, pair_ref, high_ref, rows_ref, out_ref):
-    weights = [rows_ref[0, :, 0, :, piece].reshape(256, 512) for piece in range(3)]
-    for group in range(4):
-        total = dot(pair_ref[group, 0:256], weights[0], NT)
-        total += dot(pair_ref[group, 256:512], weights[1], NT)
-        total += dot(high_ref[group], weights[2], NT)
-        total = total.astype(BF)
-        for part in range(2):
-            out_ref[part, group * 256 : (group + 1) * 256, :] = total[:, part * 128 : (part + 1) * 128]
+def split_kernel(in_ref, out_ref):
+    out_ref[0] = in_ref[...]
+
+
+def split_blocks(partials):
+    return pl.pallas_call(
+        split_kernel,
+        grid=(8,),
+        in_specs=[pl.BlockSpec((256, 512), lambda i: (0, i))],
+        out_specs=pl.BlockSpec((1, 256, 512), lambda i: (i, 0, 0)),
+        out_shape=jax.ShapeDtypeStruct((8, 256, 512), BF),
+        name="split_blocks",
+    )(partials)
+
+
+def high_kernel(summed_ref, resid_ref, out_ref):
+    high = (summed_ref[...].astype(F32) + resid_ref[...].astype(F32)).astype(BF)
+    for x in range(4):
+        out_ref[x] = high
+
+
+def high_copies(summed, resid):
+    return pl.pallas_call(
+        high_kernel,
+        in_specs=[VMEM, VMEM],
+        out_specs=VMEM,
+        out_shape=jax.ShapeDtypeStruct((4, 256, 512), BF),
+        name="high_copies",
+    )(summed, resid)
+
+
+def term_kernel(half_ref, pair_ref, high_ref, rows_ref, out_ref, held, sems):
+    half = half_ref[0]
+    copies = [
+        pltpu.make_async_copy(rows_ref.at[i, :, half], held.at[i], sems.at[i]) for i in range(2)
+    ]
+    for copy in copies:
+        copy.start()
+    for i in range(2):
+        copies[i].wait()
+        weights = [held[i, :, :, piece].reshape(256, 512) for piece in range(3)]
+        for group in range(4):
+            total = dot(pair_ref[group, 0:256], weights[0], NT)
+            total += dot(pair_ref[group, 256:512], weights[1], NT)
+            total += dot(high_ref[group], weights[2], NT)
+            total = total.astype(BF)
+            for part in range(2):
+                out_ref[2 * i + part, group * 256 : (group + 1) * 256, :] = total[
+                    :, part * 128 : (part + 1) * 128
+                ]
 
 
 def term_half(half, pair, high, rows):
     return pl.pallas_call(
         term_kernel,
-        grid_spec=pltpu.PrefetchScalarGridSpec(
-            num_scalar_prefetch=1,
-            grid=(2,),
-            in_specs=[
-                pl.BlockSpec((4, 528, 512), lambda i, h: (0, 0, 0)),
-                pl.BlockSpec((4, 256, 512), lambda i, h: (0, 0, 0)),
-                pl.BlockSpec((1, 2, 1, 2, 3, 64, 512), lambda i, h: (i, 0, h[0], 0, 0, 0, 0)),
-            ],
-            out_specs=pl.BlockSpec((2, 1024, 128), lambda i, h: (i, 0, 0)),
-        ),
+        in_specs=[
+            pl.BlockSpec(memory_space=pltpu.SMEM),
+            VMEM,
+            VMEM,
+            pl.BlockSpec(memory_space=pltpu.HBM),
+        ],
+        out_specs=VMEM,
         out_shape=jax.ShapeDtypeStruct((4, 1024, 128), BF),
+        scratch_shapes=[
+            pltpu.VMEM((2, 2, 2, 3, 64, 512), BF),
+            pltpu.SemaphoreType.DMA((2,)),
+        ],
         compiler_params=pltpu.CompilerParams(vmem_limit_bytes=40 * 1024 * 1024),
         cost_estimate=pl.CostEstimate(
             flops=2 * 1024 * 1536 * 512, bytes_accessed=6 * 1024 * 1024, transcendentals=0
@@ -157,8 +199,9 @@
     dp = ("z", "x")
     rows = lax.all_gather(jnp.swapaxes(joining, 1, 2), "z")
     rows = rows.reshape(2, 2, 2, 2, 3, 64, 512)
-    split = jnp.swapaxes(partials.reshape(256, 8, 512), 0, 1)
-    summed = lax.psum_scatter(split, tensor, scatter_dimension=0, tiled=False).astype(F32)
+    summed = lax.psum_scatter(
+        split_blocks(partials), tensor, scatter_dimension=0, tiled=False
+    )
 
     shard = dest[:, 0]
     earlier = jnp.arange(256)[:, None] > jnp.arange(256)[None, :]
@@ -167,9 +210,7 @@
     extra = jnp.concatenate([shard, place]).astype(BF)[None, :]
     extra = jnp.pad(extra, ((0, 15), (0, 0)))
     pair = jnp.concatenate([low, mid, extra], axis=0)
-    pair = lax.all_to_all(
-        jnp.broadcast_to(pair[None], (4, 528, 512)), "x", split_axis=0, concat_axis=0, tiled=True
-    )
+    pair = jnp.broadcast_to(pair[None], (4, 528, 512))
 
     left = remaining_steps(lengths[0], loss_mask, 256).astype(BF)
     side = jnp.concatenate([targets, jnp.broadcast_to(left[:, None], (256, 128))], axis=1)
@@ -177,12 +218,13 @@
     side = jnp.dot(slot.astype(BF), side, preferred_element_type=F32).astype(BF)
     side = jnp.swapaxes(side.reshape(64, 8, 2, 128), 1, 2).reshape(64, 16, 128)
     side = lax.all_to_all(side, dp, split_axis=0, concat_axis=0, tiled=True)
+    pair, side = lax.optimization_barrier((pair, side))
+    pair = lax.all_to_all(pair, "x", split_axis=0, concat_axis=0, tiled=True)
     me = lax.axis_index("y") * 2 + lax.axis_index("c")
     side = lax.dynamic_slice_in_dim(side, me * 8, 8, 0)
 
-    high = (summed + resid.astype(F32)).astype(BF)
     high = lax.all_to_all(
-        jnp.broadcast_to(high[None], (4, 256, 512)), "x", split_axis=0, concat_axis=0, tiled=True
+        high_copies(summed, resid), "x", split_axis=0, concat_axis=0, tiled=True
     )
 
     core = lax.axis_index("c").astype(jnp.int32).reshape(1)

time: 224 us -> 204 us (0.911)
  waiting for transfers between devices: 102 us -> 61.9 us
  blocking collectives: 37.5 us -> 57 us
  Pallas kernels: 12 us -> 19.6 us
  local copies, waits for them, and re-layouts: 9.97 us -> 3.59 us
    reduce_scatter x1, waiting for transfers between devices: 37.9 us -> 0.01 us  [per_device(): lax.psum_scatter(split_blocks(partials), tensor, scatter_dimension=0, til...]
    all_to_all x0 -> x1, blocking collectives: none -> 18.2 us  [per_device(): terms = lax.all_to_all(terms, 'y', split_axis=0, concat_axis=0, tiled=True)]
    all_gather x1, waiting for transfers between devices: 12.2 us -> 0.01 us  [per_device(): rows = lax.all_gather(jnp.swapaxes(joining, 1, 2), 'z')]
    all_to_all x1, starting transfers between devices: 10.4 us -> 19.1 us  [per_device(): side = lax.all_to_all(side, dp, split_axis=0, concat_axis=0, tiled=True)]
    pallas_call x2 -> x4, Pallas kernels: 4.37 us -> 12 us  [the longest x1 5.66 us: split_blocks(): pl.pallas_call(split_kernel, grid=(8,), in_specs=[pl.BlockSpec((256, 512)...]
    all_to_all x3 -> x2, waiting for transfers between devices: 24.8 us -> 30.7 us  [the longest x1 20.9 us: per_device(): pair = lax.all_to_all(pair, 'x', split_axis=0, concat_axis=0, tiled=True)]
    unnamed x26 -> x20, local copies, waits for them, and re-layouts: 7.13 us -> 1.94 us
    all_to_all x3 -> x2, starting transfers between devices: 12.7 us -> 7.72 us  [the longest x1 4.2 us: per_device(): pair = lax.all_to_all(pair, 'x', split_axis=0, concat_axis=0, tiled=True)]
  transfers between devices with their start and end apart: 8 -> 7, of which waited for: 6 -> 5; matrix products, arithmetic and copies ran while one was open for 2% -> 2% of each run, Pallas kernels for 1% -> 2%
where the time goes in v2:
time: 204 us
  waiting for transfers between devices  61.9 us (30%)
  blocking collectives  57 us (28%)
  starting transfers between devices  44.2 us (22%)
  Pallas kernels  19.6 us (10%)
  between operations  15.7 us (8%)
  local copies, waits for them, and re-layouts  3.59 us (2%)
    all_to_all x1, blocking collectives, per_device(): moved = lax.all_to_all(moved, dp, split_axis=0, concat_axis=0, tiled=True)  38.8 us
    all_to_all x1, waiting for transfers between devices, per_device(): side = lax.all_to_all(side, dp, split_axis=0, concat_axis=0, tiled=True)  21.1 us
    all_to_all x1, waiting for transfers between devices, per_device(): pair = lax.all_to_all(pair, 'x', split_axis=0, concat_axis=0, tiled=True)  20.9 us
    all_to_all x1, starting transfers between devices, per_device(): side = lax.all_to_all(side, dp, split_axis=0, concat_axis=0, tiled=True)  19.1 us
    all_to_all x1, blocking collectives, per_device(): terms = lax.all_to_all(terms, 'y', split_axis=0, concat_axis=0, tiled=True)  18.2 us
    all_to_all x1, waiting for transfers between devices, per_device(): lax.all_to_all(high_copies(summed, resid), 'x', split_axis=0, concat_axis...  9.8 us
    all_to_all x1, waiting for transfers between devices, per_device(): lax.all_to_all(moved.reshape(8, 256, 128), tensor, split_axis=0, concat_a...  9.5 us
    ppermute x1, starting transfers between devices, per_device(): other = lax.ppermute(other, 'c', [(0, 1), (1, 0)])  9.05 us
  transfers between devices with their start and end apart: 7, of which 5 were waited for; matrix products, arithmetic and copies ran while one was open for 2% of the time, Pallas kernels for 2%

profile of v2, /device:TPU:1, one launch (start us, length us, event | category | flops | bytes accessed | tf_op | source)
XLA Modules:
  0.0 203.7 jit_solution(7937517136163124353)
XLA Ops:
  8.0 5.7 %split_blocks.1 = bf16[8,256,512]{2,1,0:T(8,128)(2,1)} custom-call(bf16[256,4096]{1,0:T(8,128)(2,1)} %in_ref.2), custom_call_target="tpu_custom_call" | custom-call | tf_op jit(solution)/shard_map/split_blocks/pallas_call | solution.py:34
  13.8 0.5 all-gather.3.cloned.1.call-update
  14.4 0.2 reduce-window.4
  14.6 0.2 convert_reduce_fusion
  15.0 0.9 fusion
  15.9 19.1 %all-to-all-start = ((bf16[64,16,128]{2,1,0:T(8,128)(2,1)}), bf16[64,16,128]{2,1,0:T(8,128)(2,1)S(1)}, u32[]{:S(2)}, u32[]{:S(2)}) async-start(bf16[64,16,128]{2,1,0:T(8,128)(2,1)} %fusion), calls=%async_computation | async-start | bytes 524288 | tf_op jit(solution)/shard_map/all_to_all | solution.py:220
  35.1 21.1 %all-to-all-done = bf16[64,16,128]{2,1,0:T(8,128)(2,1)S(1)} async-done(((bf16[64,16,128]{2,1,0:T(8,128)(2,1)}), bf16[64,16,128]{2,1,0:T(8,128)(2,1)S(1)}, u32[]{:S(2)}, u32[]{:S(2)}) %all-to-all-start) | async-done | bytes 262176 | tf_op jit(solution)/shard_map/all_to_all | solution.py:220
  56.2 1.5 broadcast_in_dim.16
  57.8 4.2 %all-to-all-start.1 = ((bf16[4,528,512]{2,1,0:T(8,128)(2,1)}), bf16[4,528,512]{2,1,0:T(8,128)(2,1)S(1)}, u32[]{:S(2)}, u32[]{:S(2)}) async-start(bf16[4,528,512]{2,1,0:T(8,128)(2,1)} %broadcast_in_dim.16), calls=%async_computation.1 | async-start | bytes 4325376 | tf_op jit(solution)/shard_map/all_to_all | solution.py:222
  62.0 2.1 %high_copies.1 = bf16[4,256,512]{2,1,0:T(8,128)(2,1)} custom-call(bf16[256,512]{1,0:T(8,128)(2,1)} %bitcast.27, bf16[256,512]{1,0:T(8,128)(2,1)} %resid_ref.1), custom_call_target="tpu_custom_call" | custom-call | tf_op jit(solution)/shard_map/high_copies/pallas_call | solution.py:51
  64.0 20.9 %all-to-all-done.1.pair_ref = bf16[4,528,512]{2,1,0:T(8,128)(2,1)S(1)} async-done(((bf16[4,528,512]{2,1,0:T(8,128)(2,1)}), bf16[4,528,512]{2,1,0:T(8,128)(2,1)S(1)}, u32[]{:S(2)}, u32[]{:S(2)}) %all-to-all-start.1) | async-done | bytes 2162720 | tf_op jit(solution)/shard_map/all_to_all | solution.py:222
  85.0 3.5 %all-to-all-start.2 = ((bf16[4,256,512]{2,1,0:T(8,128)(2,1)}), bf16[4,256,512]{2,1,0:T(8,128)(2,1)S(1)}, u32[]{:S(2)}, u32[]{:S(2)}) async-start(bf16[4,256,512]{2,1,0:T(8,128)(2,1)} %high_copies.1), calls=%async_computation.3 | async-start | bytes 2097152 | tf_op jit(solution)/shard_map/all_to_all | solution.py:226
  88.5 9.8 %all-to-all-done.2.high_ref = bf16[4,256,512]{2,1,0:T(8,128)(2,1)S(1)} async-done(((bf16[4,256,512]{2,1,0:T(8,128)(2,1)}), bf16[4,256,512]{2,1,0:T(8,128)(2,1)S(1)}, u32[]{:S(2)}, u32[]{:S(2)}) %all-to-all-start.2) | async-done | bytes 1048608 | tf_op jit(solution)/shard_map/all_to_all | solution.py:226
  98.3 1.9 copy-done
  100.2 2.1 %term_half.3 = bf16[4,1024,128]{2,1,0:T(8,128)(2,1)S(1)} custom-call(s32[1]{0:T(128)S(6)} %sub.27.half_ref, bf16[4,528,512]{2,1,0:T(8,128)(2,1)S(1)} %all-to-all-done.1.pair_ref, bf16[4,256,512]{2,1,0:T(8,128)(2,1)S(1)} %all-to-all-done.2.high_ref, bf16[2,2,2,2,3,64,512]{6,5,4,3,2,1,0:T(8,128)(2,1)S(1)} %bitcast.24), custom_call_target="tpu_custom_call" | custom-call | flops 1610612736 | bytes 6291456 | tf_op jit(solution)/shard_map/term_half/pallas_call | solution.py:82
  102.3 9.0 %collective-permute-start = (bf16[4,1024,128]{2,1,0:T(8,128)(2,1)S(1)}, bf16[4,1024,128]{2,1,0:T(8,128)(2,1)S(1)}, u32[]{:S(2)}, u32[]{:S(2)}) collective-permute-start(bf16[4,1024,128]{2,1,0:T(8,128)(2,1)S(1)} %term_half.3), channel_id=1, source_target_pairs={{0,1},{1,0},{2,3},{3,2},{4,5},{5,4},{6,7},{7,6},{8,9},{9,8},{10,11... | collective-permute-start | bytes 3145736 | tf_op jit(solution)/shard_map/ppermute | solution.py:232
  111.4 2.2 %term_half.2 = bf16[4,1024,128]{2,1,0:T(8,128)(2,1)S(1)} custom-call(s32[1]{0:T(128)} %bitcast.half_ref, bf16[4,528,512]{2,1,0:T(8,128)(2,1)S(1)} %all-to-all-done.1.pair_ref, bf16[4,256,512]{2,1,0:T(8,128)(2,1)S(1)} %all-to-all-done.2.high_ref, bf16[2,2,2,2,3,64,512]{6,5,4,3,2,1,0:T(8,128)(2,1)S(1)} %bitcast.25), custom_call_target="tpu_custom_call" | custom-call | flops 1610612736 | bytes 6291456 | tf_op jit(solution)/shard_map/term_half/pallas_call | solution.py:82
  113.7 0.3 add_convert_fusion
  114.0 18.2 %all_to_all.30.terms_ref = bf16[4,1024,128]{2,1,0:T(8,128)(2,1)S(1)} all-to-all(bf16[4,1024,128]{2,1,0:T(8,128)(2,1)S(1)} %add_convert_fusion), channel_id=1, replica_groups=mesh['z'=16,'x'=4,'y'=4,'c'=2] {'y'}, dimensions={0} | all-to-all | bytes 2097152 | tf_op jit(solution)/shard_map/all_to_all | solution.py:235
  132.2 0.8 spread.1
  133.0 38.8 %all_to_all.31 = bf16[64,32,128]{2,1,0:T(8,128)(2,1)} all-to-all(bf16[64,32,128]{2,1,0:T(8,128)(2,1)S(1)} %spread.1), channel_id=1, replica_groups=mesh['z'=16,'x'=4,'y'=4,'c'=2] {'z','x'}, dimensions={0} | all-to-all | bytes 1048576 | tf_op jit(solution)/shard_map/all_to_all | solution.py:237
  171.7 8.2 %all-to-all-start.5 = ((bf16[8,256,128]{2,1,0:T(8,128)(2,1)}), bf16[8,256,128]{2,1,0:T(8,128)(2,1)S(1)}, u32[]{:S(2)}, u32[]{:S(2)}) async-start(bf16[8,256,128]{2,1,0:T(8,128)(2,1)} %bitcast.14), calls=%async_computation.6 | async-start | bytes 1048576 | tf_op jit(solution)/shard_map/all_to_all | solution.py:238
  179.9 9.5 %all-to-all-done.5 = bf16[8,256,128]{2,1,0:T(8,128)(2,1)S(1)} async-done(((bf16[8,256,128]{2,1,0:T(8,128)(2,1)}), bf16[8,256,128]{2,1,0:T(8,128)(2,1)S(1)}, u32[]{:S(2)}, u32[]{:S(2)}) %all-to-all-start.5) | async-done | bytes 524320 | tf_op jit(solution)/shard_map/all_to_all | solution.py:238
  189.4 6.8 %chain.1 = (f32[64,4096]{1,0:T(8,128)}, bf16[64,4096]{1,0:T(8,128)(2,1)}) custom-call(bf16[8,8,32,128]{3,2,1,0:T(8,128)(2,1)S(1)} %bitcast.26, bf16[8,16,128]{2,1,0:T(8,128)(2,1)S(1)} %constant_dynamic-slice_fusion.side_ref, bf16[4096,128]{1,0:T(8,128)(2,1)S(1)} %copy-done.2, bf16[128,4096]{1,0:T(8,128)(2,1)S(1)} %copy-done.3), custom_call_target="tpu_custom_call" | custom-call | tf_op jit(solution)/shard_map/chain/pallas_call | solution.py:181
  (35 shorter events, 0.5 us)
Async XLA Ops:
  8.0 54.0 %reduce-scatter.2.cloned.1.call-start = ((), (), s32[]{:S(2)}) async-start(), calls=%async_computation.7 | async-start | bytes 2359296 | tf_op jit(solution)/shard_map/reduce_scatter | solution.py:202
  13.7 0.7 copy-start.8
  13.7 0.9 copy-start.6
  13.7 1.1 copy-start.7
  13.7 1.3 copy-start.9
  13.7 21.4 %copy-start.4 = (bf16[256,512]{1,0:T(8,128)(2,1)S(1)}, bf16[256,512]{1,0:T(8,128)(2,1)}, u32[]{:S(2)}) copy-start(bf16[256,512]{1,0:T(8,128)(2,1)} %param.14) | copy-start | bytes 786436
  13.7 21.4 %copy-start.5 = (bf16[256,512]{1,0:T(8,128)(2,1)S(1)}, bf16[256,512]{1,0:T(8,128)(2,1)}, u32[]{:S(2)}) copy-start(bf16[256,512]{1,0:T(8,128)(2,1)} %param.13) | copy-start | bytes 786436
  13.8 84.5 %all-gather.3.cloned.1.call-start = ((), (), s32[]{:S(2)}) async-start(), calls=%async_computation.8 | async-start | bytes 3342336 | tf_op jit(solution)/shard_map/all_gather | solution.py:200
  15.9 40.3 %all-to-all-start = ((bf16[64,16,128]{2,1,0:T(8,128)(2,1)}), bf16[64,16,128]{2,1,0:T(8,128)(2,1)S(1)}, u32[]{:S(2)}, u32[]{:S(2)}) async-start(bf16[64,16,128]{2,1,0:T(8,128)(2,1)} %fusion), calls=%async_computation | async-start | bytes 524288 | tf_op jit(solution)/shard_map/all_to_all | solution.py:220
  57.8 27.2 %all-to-all-start.1 = ((bf16[4,528,512]{2,1,0:T(8,128)(2,1)}), bf16[4,528,512]{2,1,0:T(8,128)(2,1)S(1)}, u32[]{:S(2)}, u32[]{:S(2)}) async-start(bf16[4,528,512]{2,1,0:T(8,128)(2,1)} %broadcast_in_dim.16), calls=%async_computation.1 | async-start | bytes 4325376 | tf_op jit(solution)/shard_map/all_to_all | solution.py:222
  85.0 13.3 %all-to-all-start.2 = ((bf16[4,256,512]{2,1,0:T(8,128)(2,1)}), bf16[4,256,512]{2,1,0:T(8,128)(2,1)S(1)}, u32[]{:S(2)}, u32[]{:S(2)}) async-start(bf16[4,256,512]{2,1,0:T(8,128)(2,1)} %high_copies.1), calls=%async_computation.3 | async-start | bytes 2097152 | tf_op jit(solution)/shard_map/all_to_all | solution.py:226
  98.3 1.9 copy-start
  100.2 11.2 %copy-start.1 = (bf16[48,64,512]{2,1,0:T(8,128)(2,1)S(1)}, bf16[48,64,512]{2,1,0:T(8,128)(2,1)}, u32[]{:S(2)}) copy-start(bf16[48,64,512]{2,1,0:T(8,128)(2,1)} %all-gather.3.cloned.1.call-done) | copy-start | bytes 9437188
  102.3 11.3 %collective-permute-start = (bf16[4,1024,128]{2,1,0:T(8,128)(2,1)S(1)}, bf16[4,1024,128]{2,1,0:T(8,128)(2,1)S(1)}, u32[]{:S(2)}, u32[]{:S(2)}) collective-permute-start(bf16[4,1024,128]{2,1,0:T(8,128)(2,1)S(1)} %term_half.3), channel_id=1, source_target_pairs={{0,1},{1,0},{2,3},{3,2},{4,5},{5,4},{6,7},{7,6},{8,9},{9,8},{10,11... | collective-permute-start | bytes 3145736 | tf_op jit(solution)/shard_map/ppermute | solution.py:232
  132.2 57.2 %copy-start.2 = (bf16[4096,128]{1,0:T(8,128)(2,1)S(1)}, bf16[4096,128]{1,0:T(8,128)(2,1)}, u32[]{:S(2)}) copy-start(bf16[4096,128]{1,0:T(8,128)(2,1)} %in_ref.3) | copy-start | bytes 3145732
  132.9 56.5 %copy-start.3 = (bf16[128,4096]{1,0:T(8,128)(2,1)S(1)}, bf16[128,4096]{1,0:T(8,128)(2,1)}, u32[]{:S(2)}) copy-start(bf16[128,4096]{1,0:T(8,128)(2,1)} %out_ref.1) | copy-start | bytes 3145732
  171.7 17.7 %all-to-all-start.5 = ((bf16[8,256,128]{2,1,0:T(8,128)(2,1)}), bf16[8,256,128]{2,1,0:T(8,128)(2,1)S(1)}, u32[]{:S(2)}, u32[]{:S(2)}) async-start(bf16[8,256,128]{2,1,0:T(8,128)(2,1)} %bitcast.14), calls=%async_computation.6 | async-start | bytes 1048576 | tf_op jit(solution)/shard_map/all_to_all | solution.py:238
Sparse Core Ops, SparseCore 0:
  13.9 45.3 reduce-scatter.1
Sparse Core Ops, SparseCore 1:
  16.3 80.7 all-gather.2

commit v3 on v2

v3 whole, which is shorter than its diff:
```python
import jax
import jax.numpy as jnp
from jax import lax
from jax.experimental import pallas as pl
from jax.experimental.pallas import tpu as pltpu
from jax.sharding import Mesh, PartitionSpec as P

BF = jnp.bfloat16
F32 = jnp.float32
NT = (((1,), (1,)), ((), ()))
NN = (((1,), (0,)), ((), ()))
VMEM = pl.BlockSpec(memory_space=pltpu.VMEM)
HBM = pl.BlockSpec(memory_space=pltpu.HBM)


def dot(a, b, dims=NN):
    return lax.dot_general(a, b, dims, preferred_element_type=F32)


def remaining_steps(sizes, mask, count):
    ends = jnp.cumsum(sizes)
    starts = ends - sizes
    place = jnp.arange(count, dtype=jnp.int32)[:, None]
    inside = (place >= starts[None, :]) & (place < ends[None, :])
    offset = jnp.sum(jnp.where(inside, place - starts[None, :], 0), axis=1)
    length = jnp.sum(jnp.where(inside, sizes[None, :], 0), axis=1)
    return (jnp.minimum(length - 1 - offset, 3) * mask).astype(F32)


def split_kernel(in_ref, out_ref, sems):
    copies = [
        pltpu.make_async_copy(in_ref.at[:, pl.ds(i * 512, 512)], out_ref.at[i], sems.at[i])
        for i in range(8)
    ]
    for copy in copies:
        copy.start()
    for copy in copies:
        copy.wait()


def split_blocks(partials):
    return pl.pallas_call(
        split_kernel,
        in_specs=[HBM],
        out_specs=HBM,
        out_shape=jax.ShapeDtypeStruct((8, 256, 512), BF),
        scratch_shapes=[pltpu.SemaphoreType.DMA((8,))],
        name="split_blocks",
    )(partials)


def high_kernel(summed_ref, resid_ref, out_ref):
    high = (summed_ref[...].astype(F32) + resid_ref[...].astype(F32)).astype(BF)
    for x in range(4):
        out_ref[x] = high


def high_copies(summed, resid):
    return pl.pallas_call(
        high_kernel,
        in_specs=[VMEM, VMEM],
        out_specs=VMEM,
        out_shape=jax.ShapeDtypeStruct((4, 256, 512), BF),
        name="high_copies",
    )(summed, resid)


def term_kernel(half_ref, p0, p1, p2, p3, high_ref, mine_ref, below_ref, above_ref, out_ref, held, sems):
    half = half_ref[0]
    copies = []
    for i, other in ((0, below_ref), (1, above_ref)):
        copies.append(
            (
                pltpu.make_async_copy(mine_ref.at[i, :, half], held.at[i, 0], sems.at[i, 0]),
                pltpu.make_async_copy(other.at[:, half], held.at[i, 1], sems.at[i, 1]),
            )
        )
    for two in copies:
        for copy in two:
            copy.start()
    for i in range(2):
        for copy in copies[i]:
            copy.wait()
        weights = [
            jnp.concatenate(
                [held[i, 0, 0, piece], held[i, 1, 0, piece], held[i, 0, 1, piece], held[i, 1, 1, piece]],
                axis=0,
            )
            for piece in range(3)
        ]
        for group, pair_ref in enumerate((p0, p1, p2, p3)):
            total = dot(pair_ref[0:256], weights[0], NT)
            total += dot(pair_ref[256:512], weights[1], NT)
            total += dot(high_ref[lax.rem(half_ref[1] + (4 - group), 4)], weights[2], NT)
            total = total.astype(BF)
            for part in range(2):
                out_ref[2 * i + part, group * 256 : (group + 1) * 256, :] = total[
                    :, part * 128 : (part + 1) * 128
                ]


def term_half(half, pairs, high, mine, below, above):
    return pl.pallas_call(
        term_kernel,
        in_specs=[pl.BlockSpec(memory_space=pltpu.SMEM)] + [VMEM] * 5 + [HBM] * 3,
        out_specs=VMEM,
        out_shape=jax.ShapeDtypeStruct((4, 1024, 128), BF),
        scratch_shapes=[
            pltpu.VMEM((2, 2, 2, 3, 64, 512), BF),
            pltpu.SemaphoreType.DMA((2, 2)),
        ],
        compiler_params=pltpu.CompilerParams(vmem_limit_bytes=40 * 1024 * 1024),
        cost_estimate=pl.CostEstimate(
            flops=2 * 1024 * 1536 * 512, bytes_accessed=6 * 1024 * 1024, transcendentals=0
        ),
        name="term_half",
    )(half, *pairs, high, mine, below, above)


def spread_kernel(terms_ref, p0, p1, p2, p3, out_ref):
    total = terms_ref[0].astype(F32)
    for part in range(1, 4):
        total += terms_ref[part].astype(F32)
    joined = total.astype(BF)
    row = lax.broadcasted_iota(jnp.int32, (1024, 256), 0)
    for two in range(2):
        moved = None
        for odd, pair_ref in enumerate(((p0, p1), (p2, p3))[two]):
            group = 2 * two + odd
            shard = pair_ref[512:513, 0:256].astype(jnp.int32)
            rank = pair_ref[512:513, 256:512].astype(jnp.int32)
            slot = shard * 16 + (odd * 8 + rank)
            hot = jnp.where(row == slot, 1.0, 0.0).astype(BF)
            part = dot(hot, joined[group * 256 : (group + 1) * 256])
            moved = part if moved is None else moved + part
        out_ref[:, two * 16 : (two + 1) * 16, :] = moved.astype(BF).reshape(64, 16, 128)


def spread(terms, pairs):
    return pl.pallas_call(
        spread_kernel,
        in_specs=[VMEM] * 5,
        out_specs=VMEM,
        out_shape=jax.ShapeDtypeStruct((64, 32, 128), BF),
        compiler_params=pltpu.CompilerParams(vmem_limit_bytes=40 * 1024 * 1024),
        name="spread",
    )(terms, *pairs)


def source_rows(tile, odd, x):
    tile = tile.astype(F32)
    tile = jnp.concatenate(
        [tile[8 * ((x - group) % 4) : 8 * ((x - group) % 4) + 8] for group in range(4)], axis=0
    )
    if odd:
        tile = jnp.concatenate([tile[:, 64:], tile[:, :64]], axis=1)
    return tile


def chain_kernel(rows_ref, goal_ref, left_ref, in_ref, out_ref, grad_ref, final_ref, h0, h1, h2):
    for block in range(8):
        tiles = [
            jnp.concatenate(
                [source_rows(rows_ref[block, 4 * odd + x], odd, x) for odd in range(2)], axis=0
            )
            for x in range(4)
        ]
        for k in range(4):
            lane = (k // 2) * 64
            x = 2 * (k % 2)
            h0[:, block * 512 + k * 128 : block * 512 + (k + 1) * 128] = jnp.concatenate(
                [tiles[x][:, lane : lane + 64], tiles[x + 1][:, lane : lane + 64]], axis=1
            )
    goal = goal_ref[...].astype(F32)
    left = left_ref[...].astype(F32)
    states = (h0, h1, h2)
    invs, pres = [], []
    for step in range(3):
        state = states[step][...]
        inv = lax.rsqrt(jnp.sum(state * state, axis=-1, keepdims=True) * (1.0 / 4096) + 1e-06)
        pre = dot((state * inv).astype(BF), in_ref[...])
        active = (pre * jax.nn.sigmoid(pre)).astype(BF)
        invs.append(inv)
        pres.append(pre)
        after = state + dot(active, out_ref[...])
        if step < 2:
            states[step + 1][...] = after
        else:
            final_ref[...] = after.astype(BF)
    for step in (2, 1, 0):
        inv, pre = invs[step], pres[step]
        live = jnp.where(left > step, pre - goal, 0.0)
        if step == 2:
            dpre = live.astype(BF)
        else:
            dact = dot(grad_ref[...].astype(BF), out_ref[...], NT)
            sig = jax.nn.sigmoid(pre)
            dpre = (dact * (sig + pre * sig * (1.0 - sig)) + live).astype(BF)
        dnorm = dot(dpre, in_ref[...], NT)
        state = states[step][...]
        mean = jnp.sum(dnorm * state, axis=-1, keepdims=True) * (1.0 / 4096)
        back = inv * dnorm - state * (inv * inv * inv * mean)
        if step < 2:
            back = grad_ref[...] + back
        grad_ref[...] = back


def chain(rows, goal, left, step_in, step_out):
    return pl.pallas_call(
        chain_kernel,
        in_specs=[VMEM] * 5,
        out_specs=[VMEM] * 2,
        out_shape=[
            jax.ShapeDtypeStruct((64, 4096), F32),
            jax.ShapeDtypeStruct((64, 4096), BF),
        ],
        scratch_shapes=[pltpu.VMEM((64, 4096), F32)] * 3,
        compiler_params=pltpu.CompilerParams(vmem_limit_bytes=40 * 1024 * 1024),
        name="chain",
    )(rows, goal, left, step_in, step_out)


def per_device(
    partials, resid, low, mid, joining, step_in, step_out, targets, lengths, loss_mask, dest
):
    tensor, dp, z = ("y", "c"), ("zh", "zl", "x"), ("zh", "zl")
    me = lax.axis_index("y") * 2 + lax.axis_index("c")
    core, along = lax.axis_index("c"), lax.axis_index("x")

    mine = lax.all_gather(jnp.swapaxes(joining, 1, 2), "zh")
    summed = lax.psum_scatter(split_blocks(partials), tensor, scatter_dimension=0, tiled=False)

    shard = dest[:, 0]
    earlier = jnp.arange(256)[:, None] > jnp.arange(256)[None, :]
    rank = jnp.sum(((shard[:, None] == shard[None, :]) & earlier).astype(jnp.int32), axis=1)
    extra = jnp.concatenate([shard, rank]).astype(BF)[None, :]
    extra = jnp.pad(extra, ((0, 15), (0, 0)))
    pair = jnp.concatenate([low, mid, extra], axis=0)
    pairs = [pair] + [lax.ppermute(pair, "x", ring(4, shift)) for shift in range(1, 4)]

    mine, *pairs = lax.optimization_barrier((mine, *pairs))
    below = lax.ppermute(mine[:4], z, ring(16, 1)).reshape(2, 2, 3, 64, 512)
    above = lax.ppermute(mine[4:], z, ring(16, -1)).reshape(2, 2, 3, 64, 512)
    mine = mine.reshape(2, 2, 2, 3, 64, 512)

    left = remaining_steps(lengths[0], loss_mask, 256).astype(BF)
    side = lax.dynamic_slice_in_dim(targets, me * 16, 16, 1)
    side = jnp.concatenate([side, jnp.broadcast_to(left[:, None], (256, 16))], axis=1)
    slot = jnp.arange(512, dtype=jnp.int32)[:, None] == (shard * 8 + rank)[None, :]
    side = jnp.dot(slot.astype(BF), side, preferred_element_type=F32).astype(BF)
    side = lax.all_to_all(side.reshape(64, 2, 128), dp, split_axis=0, concat_axis=0, tiled=True)
    side = lax.all_to_all(
        side.reshape(8, 16, 128), tensor, split_axis=0, concat_axis=0, tiled=True
    ).reshape(8, 64, 32)
    goal = jnp.swapaxes(side[:, :, :16], 0, 1).reshape(64, 128)
    left = jnp.broadcast_to(side[0, :, 16:17], (64, 128))

    high = high_copies(summed, resid)
    high, goal, left = lax.optimization_barrier((high, goal, left))
    high = lax.all_to_all(high, "x", split_axis=0, concat_axis=0, tiled=True)

    other = term_half(jnp.stack([1 - core, along]).astype(jnp.int32), pairs, high, mine, below, above)
    other = lax.ppermute(other, "c", ring(2, 1))
    own = term_half(jnp.stack([core, along]).astype(jnp.int32), pairs, high, mine, below, above)
    terms = (own.astype(F32) + other.astype(F32)).astype(BF)
    terms = lax.all_to_all(terms, "y", split_axis=0, concat_axis=0, tiled=True)
    moved = spread(terms, pairs)
    moved = lax.all_to_all(moved, dp, split_axis=0, concat_axis=0, tiled=True)
    moved = lax.all_to_all(
        moved.reshape(8, 256, 128), tensor, split_axis=0, concat_axis=0, tiled=True
    )
    grad, final = chain(moved.reshape(8, 8, 32, 128), goal, left, step_in, step_out)
    return (grad, final)


def ring(size, shift):
    return [(i, (i + shift) % size) for i in range(size)]


def solution(mesh):
    fine = Mesh(mesh.devices.reshape(8, 2, 4, 4, 2), ("zh", "zl", "x", "y", "c"))
    dp, tensor = ("zh", "zl", "x"), ("y", "c")
    in_specs = (
        P(dp, tensor),
        P(dp, tensor),
        P(dp, tensor),
        P(dp, tensor),
        P(None, tensor, dp),
        P(),
        P(),
        P(dp, None),
        P(dp, None),
        P(dp),
        P(dp, None),
    )
    out_specs = (P(dp + tensor, None), P(dp + tensor, None))
    return jax.shard_map(
        per_device, mesh=fine, in_specs=in_specs, out_specs=out_specs, check_vma=False
    )
```

time: 204 us -> 259 us (1.27)
  Pallas kernels: 19.6 us -> 81.9 us
  blocking collectives: 57 us -> 96.3 us
  waiting for transfers between devices: 61.9 us -> 23.9 us
  starting transfers between devices: 44.2 us -> 31 us
  local copies, waits for them, and re-layouts: 3.59 us -> 8.12 us
    pallas_call x3, Pallas kernels: 13.2 us -> 72.3 us  [the longest x1 64.7 us: split_blocks(): pl.pallas_call(split_kernel, in_specs=[HBM], out_specs=HBM, out_shape=jax...]
    all_to_all x3 -> x1, waiting for transfers between devices: 51.8 us -> 1.31 us  [per_device(): high = lax.all_to_all(high, 'x', split_axis=0, concat_axis=0, tiled=True)]
    all_to_all x0 -> x2, blocking collectives: none -> 42.8 us  [the longest x1 30.9 us: per_device(): lax.all_to_all(side.reshape(64, 2, 128), dp, split_axis=0, concat_axis=0,...]
    all_to_all x3 -> x1, starting transfers between devices: 26.8 us -> 3.52 us  [per_device(): high = lax.all_to_all(high, 'x', split_axis=0, concat_axis=0, tiled=True)]
    ppermute x1 -> x6, waiting for transfers between devices: 0.09 us -> 12.4 us  [the longest x1 9.33 us: per_device(): above = lax.ppermute(mine[4:], z, ring(16, -1)).reshape(2, 2, 3, 64, 512)]
    ppermute x1 -> x6, starting transfers between devices: 9.05 us -> 19.6 us  [the longest x3 10.2 us: per_device(): lax.ppermute(pair, 'x', ring(4, shift))]
    slice x0 -> x2, local copies, waits for them, and re-layouts: none -> 3.39 us  [the longest x1 3.21 us: per_device(): above = lax.ppermute(mine[4:], z, ring(16, -1)).reshape(2, 2, 3, 64, 512)]
    pallas_call x2, Pallas kernels: 4.3 us -> 7.39 us  [term_half(): pl.pallas_call(term_kernel, in_specs=[pl.BlockSpec(memory_space=pltpu.SME...]
  transfers between devices with their start and end apart: 7 -> 10, of which waited for: 5 -> 4; matrix products, arithmetic and copies ran while one was open for 2% -> 2% of each run, Pallas kernels for 2% -> 27%
where the time goes in v3:
time: 259 us; the launch traced here: 258 us
  blocking collectives  96.3 us (37%)
  Pallas kernels  81.9 us (32%)
  starting transfers between devices  31 us (12%)
  waiting for transfers between devices  23.9 us (9%)
  between operations  15.9 us (6%)
  local copies, waits for them, and re-layouts  8.12 us (3%)
    pallas_call x1, Pallas kernels, split_blocks(): pl.pallas_call(split_kernel, in_specs=[HBM], out_specs=HBM, out_shape=jax...  64.7 us
    all_to_all x1, blocking collectives, per_device(): moved = lax.all_to_all(moved, dp, split_axis=0, concat_axis=0, tiled=True)  36.1 us
    all_to_all x1, blocking collectives, per_device(): lax.all_to_all(side.reshape(64, 2, 128), dp, split_axis=0, concat_axis=0,...  30.9 us
    all_to_all x1, blocking collectives, per_device(): terms = lax.all_to_all(terms, 'y', split_axis=0, concat_axis=0, tiled=True)  17.4 us
    all_to_all x1, blocking collectives, per_device(): lax.all_to_all(side.reshape(8, 16, 128), tensor, split_axis=0, concat_axi...  12 us
    ppermute x3, starting transfers between devices, per_device(): lax.ppermute(pair, 'x', ring(4, shift))  10.2 us
    all_to_all x1, waiting for transfers between devices, per_device(): lax.all_to_all(moved.reshape(8, 256, 128), tensor, split_axis=0, concat_a...  9.41 us
    ppermute x1, waiting for transfers between devices, per_device(): above = lax.ppermute(mine[4:], z, ring(16, -1)).reshape(2, 2, 3, 64, 512)  9.33 us
  transfers between devices with their start and end apart: 10, of which 4 were waited for; matrix products, arithmetic and copies ran while one was open for 2% of the time, Pallas kernels for 27%

profile of v3, /device:TPU:1, one launch (start us, length us, event | category | flops | bytes accessed | tf_op | source)
XLA Modules:
  0.0 258.2 jit_solution(4512551879002795102)
XLA Ops:
  8.8 64.7 %split_blocks.1 = bf16[8,256,512]{2,1,0:T(8,128)(2,1)} custom-call(bf16[256,4096]{1,0:T(8,128)(2,1)} %in_ref.2), custom_call_target="tpu_custom_call" | custom-call | tf_op jit(solution)/shard_map/split_blocks/pallas_call | solution.py:42
  74.6 5.2 %collective-permute-start.2 = (bf16[528,512]{1,0:T(8,128)(2,1)S(1)}, bf16[528,512]{1,0:T(8,128)(2,1)S(1)}, u32[]{:S(2)}, u32[]{:S(2)}) collective-permute-start(bf16[528,512]{1,0:T(8,128)(2,1)S(1)} %pad_maximum_fusion.p0), channel_id=1, source_target_pairs={{0,24},{8,0},{16,8},{24,16},{1,25},{9,1},{17,9},{25,17},{2,26},{10... | collective-permute-start | bytes 1622024 | tf_op jit(solution)/shard_map/ppermute | solution.py:239
  79.8 2.4 collective-permute-start.1
  82.3 2.5 collective-permute-start
  85.8 30.9 %all_to_all.30 = bf16[64,2,128]{2,1,0:T(2,128)(2,1)S(1)} all-to-all(bf16[64,2,128]{2,1,0:T(2,128)(2,1)S(1)} %reshape.86), channel_id=1, replica_groups=mesh['zh'=8,'zl'=2,'x'=4,'y'=4,'c'=2] {'zh','zl','x'}, dimensions={0} | all-to-all | bytes 65536 | tf_op jit(solution)/shard_map/all_to_all | solution.py:251
  116.6 12.0 %all_to_all.31 = bf16[8,16,128]{2,1,0:T(8,128)(2,1)S(1)} all-to-all(bf16[8,16,128]{2,1,0:T(8,128)(2,1)S(1)} %bitcast.34), channel_id=1, replica_groups=mesh['zh'=8,'zl'=2,'x'=4,'y'=4,'c'=2] {'y','c'}, dimensions={0} | all-to-all | bytes 65536 | tf_op jit(solution)/shard_map/all_to_all | solution.py:252
  129.1 3.2 %fusion.11 = (bf16[4,3,64,512]{3,2,1,0:T(8,128)(2,1)}, bf16[4,3,64,512]{3,2,1,0:T(8,128)(2,1)}) fusion(bf16[8,3,64,512]{3,2,1,0:T(8,128)(2,1)} %bitcast.27), kind=kLoop, calls=%fused_computation.31 | loop fusion | bytes 3145728 | tf_op jit(solution)/shard_map/slice | solution.py:243
  132.3 2.2 collective-permute-start.4
  134.5 3.1 %collective-permute-start.3 = (bf16[4,3,64,512]{3,2,1,0:T(8,128)(2,1)}, bf16[4,3,64,512]{3,2,1,0:T(8,128)(2,1)}, u32[]{:S(2)}, u32[]{:S(2)}) collective-permute-start(bf16[4,3,64,512]{3,2,1,0:T(8,128)(2,1)} %get-tuple-element.21), channel_id=1, source_target_pairs={{0,32},{32,64},{64,96},{96,128},{128,160},{160,192},{192,224},{224... | collective-permute-start | bytes 2359304 | tf_op jit(solution)/shard_map/ppermute | solution.py:242
  137.7 2.2 high_copies.1
  139.9 3.5 %all-to-all-start.2 = ((bf16[4,256,512]{2,1,0:T(8,128)(2,1)}), bf16[4,256,512]{2,1,0:T(8,128)(2,1)S(1)}, u32[]{:S(2)}, u32[]{:S(2)}) async-start(bf16[4,256,512]{2,1,0:T(8,128)(2,1)} %high_copies.1), calls=%async_computation.3 | async-start | bytes 2097152 | tf_op jit(solution)/shard_map/all_to_all | solution.py:260
  143.5 9.3 %collective-permute-done.4 = bf16[4,3,64,512]{3,2,1,0:T(8,128)(2,1)} collective-permute-done((bf16[4,3,64,512]{3,2,1,0:T(8,128)(2,1)}, bf16[4,3,64,512]{3,2,1,0:T(8,128)(2,1)}, u32[]{:S(2)}, u32[]{:S(2)}) %collective-permute-start.4) | collective-permute-done | bytes 786464 | tf_op jit(solution)/shard_map/ppermute | solution.py:243
  152.9 3.1 %collective-permute-done.3 = bf16[4,3,64,512]{3,2,1,0:T(8,128)(2,1)} collective-permute-done((bf16[4,3,64,512]{3,2,1,0:T(8,128)(2,1)}, bf16[4,3,64,512]{3,2,1,0:T(8,128)(2,1)}, u32[]{:S(2)}, u32[]{:S(2)}) %collective-permute-start.3) | collective-permute-done | bytes 786464 | tf_op jit(solution)/shard_map/ppermute | solution.py:242
  155.9 1.3 all-to-all-done.2.high_ref
  157.3 1.0 copy-done.3
  158.3 1.0 copy-done.6
  160.4 3.7 %term_half.3 = bf16[4,1024,128]{2,1,0:T(8,128)(2,1)S(1)} custom-call(s32[2]{0:T(128)S(1)} %pad_add_fusion.1.half_ref, bf16[528,512]{1,0:T(8,128)(2,1)S(1)} %pad_maximum_fusion.p0, bf16[528,512]{1,0:T(8,128)(2,1)S(1)} %copy-done.8, bf16[528,512]{1,0:T(8,128)(2,1)S(1)} %copy-done.6, bf16[528,512]{1,0:T(8,128)(2,1)S(1)} %copy-done.3, ...), custom_call_target="tpu_custom_call" | custom-call | flops 1610612736 | bytes 6291456 | tf_op jit(solution)/shard_map/term_half/pallas_call | solution.py:103
  164.1 4.1 %collective-permute-start.5 = (bf16[4,1024,128]{2,1,0:T(8,128)(2,1)S(1)}, bf16[4,1024,128]{2,1,0:T(8,128)(2,1)S(1)}, u32[]{:S(2)}, u32[]{:S(2)}) collective-permute-start(bf16[4,1024,128]{2,1,0:T(8,128)(2,1)S(1)} %term_half.3), channel_id=1, source_target_pairs={{0,1},{1,0},{2,3},{3,2},{4,5},{5,4},{6,7},{7,6},{8,9},{9,8},{10,11... | collective-permute-start | bytes 3145736 | tf_op jit(solution)/shard_map/ppermute | solution.py:263
  168.3 3.7 %term_half.2 = bf16[4,1024,128]{2,1,0:T(8,128)(2,1)S(1)} custom-call(s32[2]{0:T(128)S(1)} %pad_add_fusion.half_ref, bf16[528,512]{1,0:T(8,128)(2,1)S(1)} %pad_maximum_fusion.p0, bf16[528,512]{1,0:T(8,128)(2,1)S(1)} %copy-done.8, bf16[528,512]{1,0:T(8,128)(2,1)S(1)} %copy-done.6, bf16[528,512]{1,0:T(8,128)(2,1)S(1)} %copy-done.4, ...), custom_call_target="tpu_custom_call" | custom-call | flops 1610612736 | bytes 6291456 | tf_op jit(solution)/shard_map/term_half/pallas_call | solution.py:103
  172.3 17.4 %all_to_all.32.terms_ref = bf16[4,1024,128]{2,1,0:T(8,128)(2,1)S(1)} all-to-all(bf16[4,1024,128]{2,1,0:T(8,128)(2,1)S(1)} %add_convert_fusion), channel_id=1, replica_groups=mesh['zh'=8,'zl'=2,'x'=4,'y'=4,'c'=2] {'y'}, dimensions={0} | all-to-all | bytes 2097152 | tf_op jit(solution)/shard_map/all_to_all | solution.py:266
  190.5 36.1 %all_to_all.33 = bf16[64,32,128]{2,1,0:T(8,128)(2,1)} all-to-all(bf16[64,32,128]{2,1,0:T(8,128)(2,1)S(1)} %spread.1), channel_id=1, replica_groups=mesh['zh'=8,'zl'=2,'x'=4,'y'=4,'c'=2] {'zh','zl','x'}, dimensions={0} | all-to-all | bytes 1048576 | tf_op jit(solution)/shard_map/all_to_all | solution.py:268
  226.6 7.8 %all-to-all-start.5 = ((bf16[8,256,128]{2,1,0:T(8,128)(2,1)}), bf16[8,256,128]{2,1,0:T(8,128)(2,1)S(1)}, u32[]{:S(2)}, u32[]{:S(2)}) async-start(bf16[8,256,128]{2,1,0:T(8,128)(2,1)} %bitcast.19), calls=%async_computation.6 | async-start | bytes 1048576 | tf_op jit(solution)/shard_map/all_to_all | solution.py:269
  234.5 9.4 %all-to-all-done.5 = bf16[8,256,128]{2,1,0:T(8,128)(2,1)S(1)} async-done(((bf16[8,256,128]{2,1,0:T(8,128)(2,1)}), bf16[8,256,128]{2,1,0:T(8,128)(2,1)S(1)}, u32[]{:S(2)}, u32[]{:S(2)}) %all-to-all-start.5) | async-done | bytes 524320 | tf_op jit(solution)/shard_map/all_to_all | solution.py:269
  243.9 6.9 %chain.1 = (f32[64,4096]{1,0:T(8,128)}, bf16[64,4096]{1,0:T(8,128)(2,1)}) custom-call(bf16[8,8,32,128]{3,2,1,0:T(8,128)(2,1)S(1)} %bitcast.30, bf16[64,128]{1,0:T(8,128)(2,1)S(1)} %copy.27.goal_ref, bf16[64,128]{1,0:T(8,128)(2,1)S(1)} %broadcast_in_dim.43.left_ref, bf16[4096,128]{1,0:T(8,128)(2,1)S(1)} %copy-done.9, bf16[128,4096]{1,0:T(8,128)(2,1)S(1)} %copy-done.10), custom_call_target="tpu_custom_call" | custom-call | tf_op jit(solution)/shard_map/chain/pallas_call | solution.py:209
  (66 shorter events, 5.6 us)
Async XLA Ops:
  8.0 77.0 %copy-start = (bf16[256,128]{1,0:T(8,128)(2,1)S(1)}, bf16[256,128]{1,0:T(8,128)(2,1)}, u32[]{:S(2)}) copy-start(bf16[256,128]{1,0:T(8,128)(2,1)} %param.18) | copy-start | bytes 196612
  8.0 121.1 %all-gather.3.cloned.1.call-start = ((), (), s32[]{:S(2)}) async-start(), calls=%async_computation.8 | async-start | bytes 1769472 | tf_op jit(solution)/shard_map/all_gather | solution.py:230
  8.7 128.9 %reduce-scatter.2.cloned.1.call-start = ((), (), s32[]{:S(2)}) async-start(), calls=%async_computation.7 | async-start | bytes 2359296 | tf_op jit(solution)/shard_map/reduce_scatter | solution.py:231
  73.5 1.0 copy-start.12
  73.5 11.2 %copy-start.15 = (s32[1,8]{1,0:T(1,128)S(1)}, s32[1,8]{1,0:T(1,128)}, u32[]{:S(2)}) copy-start(s32[1,8]{1,0:T(1,128)} %param.19) | copy-start | bytes 100
  73.6 11.7 %copy-start.14 = (s32[256]{0:T(256)S(1)}, s32[256]{0:T(256)}, u32[]{:S(2)}) copy-start(s32[256]{0:T(256)} %param.20) | copy-start | bytes 3076
  74.6 54.4 %collective-permute-start.2 = (bf16[528,512]{1,0:T(8,128)(2,1)S(1)}, bf16[528,512]{1,0:T(8,128)(2,1)S(1)}, u32[]{:S(2)}, u32[]{:S(2)}) collective-permute-start(bf16[528,512]{1,0:T(8,128)(2,1)S(1)} %pad_maximum_fusion.p0), channel_id=1, source_target_pairs={{0,24},{8,0},{16,8},{24,16},{1,25},{9,1},{17,9},{25,17},{2,26},{10... | collective-permute-start | bytes 1622024 | tf_op jit(solution)/shard_map/ppermute | solution.py:239
  79.8 49.2 %collective-permute-start.1 = (bf16[528,512]{1,0:T(8,128)(2,1)S(1)}, bf16[528,512]{1,0:T(8,128)(2,1)S(1)}, u32[]{:S(2)}, u32[]{:S(2)}) collective-permute-start(bf16[528,512]{1,0:T(8,128)(2,1)S(1)} %pad_maximum_fusion.p0), channel_id=1, source_target_pairs={{0,16},{8,24},{16,0},{24,8},{1,17},{9,25},{17,1},{25,9},{2,18},{10... | collective-permute-start | bytes 1622024 | tf_op jit(solution)/shard_map/ppermute | solution.py:239
  82.3 46.8 %collective-permute-start = (bf16[528,512]{1,0:T(8,128)(2,1)S(1)}, bf16[528,512]{1,0:T(8,128)(2,1)S(1)}, u32[]{:S(2)}, u32[]{:S(2)}) collective-permute-start(bf16[528,512]{1,0:T(8,128)(2,1)S(1)} %pad_maximum_fusion.p0), channel_id=1, source_target_pairs={{0,8},{8,16},{16,24},{24,0},{1,9},{9,17},{17,25},{25,1},{2,10},{10... | collective-permute-start | bytes 1622024 | tf_op jit(solution)/shard_map/ppermute | solution.py:239
  129.0 3.3 %copy-start.2 = (bf16[528,512]{1,0:T(8,128)(2,1)}, bf16[528,512]{1,0:T(8,128)(2,1)S(1)}, u32[]{:S(2)}) copy-start(bf16[528,512]{1,0:T(8,128)(2,1)S(1)} %collective-permute-done.2.p3) | copy-start | bytes 1622020
  129.0 3.3 %copy-start.5 = (bf16[528,512]{1,0:T(8,128)(2,1)}, bf16[528,512]{1,0:T(8,128)(2,1)S(1)}, u32[]{:S(2)}) copy-start(bf16[528,512]{1,0:T(8,128)(2,1)S(1)} %collective-permute-done.1.p2) | copy-start | bytes 1622020
  129.1 3.3 %copy-start.7 = (bf16[528,512]{1,0:T(8,128)(2,1)}, bf16[528,512]{1,0:T(8,128)(2,1)S(1)}, u32[]{:S(2)}) copy-start(bf16[528,512]{1,0:T(8,128)(2,1)S(1)} %collective-permute-done.p1) | copy-start | bytes 1622020
  132.3 20.5 %collective-permute-start.4 = (bf16[4,3,64,512]{3,2,1,0:T(8,128)(2,1)}, bf16[4,3,64,512]{3,2,1,0:T(8,128)(2,1)}, u32[]{:S(2)}, u32[]{:S(2)}) collective-permute-start(bf16[4,3,64,512]{3,2,1,0:T(8,128)(2,1)} %get-tuple-element.20), channel_id=1, source_target_pairs={{0,480},{32,0},{64,32},{96,64},{128,96},{160,128},{192,160},{224,1... | collective-permute-start | bytes 2359304 | tf_op jit(solution)/shard_map/ppermute | solution.py:243
  134.5 21.4 %collective-permute-start.3 = (bf16[4,3,64,512]{3,2,1,0:T(8,128)(2,1)}, bf16[4,3,64,512]{3,2,1,0:T(8,128)(2,1)}, u32[]{:S(2)}, u32[]{:S(2)}) collective-permute-start(bf16[4,3,64,512]{3,2,1,0:T(8,128)(2,1)} %get-tuple-element.21), channel_id=1, source_target_pairs={{0,32},{32,64},{64,96},{96,128},{128,160},{160,192},{192,224},{224... | collective-permute-start | bytes 2359304 | tf_op jit(solution)/shard_map/ppermute | solution.py:242
  137.7 19.6 %copy-start.1 = (bf16[24,64,512]{2,1,0:T(8,128)(2,1)S(1)}, bf16[24,64,512]{2,1,0:T(8,128)(2,1)}, u32[]{:S(2)}) copy-start(bf16[24,64,512]{2,1,0:T(8,128)(2,1)} %all-gather.3.cloned.1.call-done) | copy-start | bytes 4718596
  139.9 17.3 %all-to-all-start.2 = ((bf16[4,256,512]{2,1,0:T(8,128)(2,1)}), bf16[4,256,512]{2,1,0:T(8,128)(2,1)S(1)}, u32[]{:S(2)}, u32[]{:S(2)}) async-start(bf16[4,256,512]{2,1,0:T(8,128)(2,1)} %high_copies.1), calls=%async_computation.3 | async-start | bytes 2097152 | tf_op jit(solution)/shard_map/all_to_all | solution.py:260
  157.3 1.0 copy-start.3
  158.3 1.0 copy-start.6
  159.4 1.0 copy-start.8
  160.4 7.9 %copy-start.4 = (bf16[528,512]{1,0:T(8,128)(2,1)S(1)}, bf16[528,512]{1,0:T(8,128)(2,1)}, u32[]{:S(2)}) copy-start(bf16[528,512]{1,0:T(8,128)(2,1)} %copy-done.2) | copy-start | bytes 1622020
  164.1 7.9 %collective-permute-start.5 = (bf16[4,1024,128]{2,1,0:T(8,128)(2,1)S(1)}, bf16[4,1024,128]{2,1,0:T(8,128)(2,1)S(1)}, u32[]{:S(2)}, u32[]{:S(2)}) collective-permute-start(bf16[4,1024,128]{2,1,0:T(8,128)(2,1)S(1)} %term_half.3), channel_id=1, source_target_pairs={{0,1},{1,0},{2,3},{3,2},{4,5},{5,4},{6,7},{7,6},{8,9},{9,8},{10,11... | collective-permute-start | bytes 3145736 | tf_op jit(solution)/shard_map/ppermute | solution.py:263
  190.5 53.4 %copy-start.9 = (bf16[4096,128]{1,0:T(8,128)(2,1)S(1)}, bf16[4096,128]{1,0:T(8,128)(2,1)}, u32[]{:S(2)}) copy-start(bf16[4096,128]{1,0:T(8,128)(2,1)} %in_ref.3) | copy-start | bytes 3145732
  190.5 53.4 %copy-start.10 = (bf16[128,4096]{1,0:T(8,128)(2,1)S(1)}, bf16[128,4096]{1,0:T(8,128)(2,1)}, u32[]{:S(2)}) copy-start(bf16[128,4096]{1,0:T(8,128)(2,1)} %out_ref.1) | copy-start | bytes 3145732
  226.6 17.3 %all-to-all-start.5 = ((bf16[8,256,128]{2,1,0:T(8,128)(2,1)}), bf16[8,256,128]{2,1,0:T(8,128)(2,1)S(1)}, u32[]{:S(2)}, u32[]{:S(2)}) async-start(bf16[8,256,128]{2,1,0:T(8,128)(2,1)} %bitcast.19), calls=%async_computation.6 | async-start | bytes 1048576 | tf_op jit(solution)/shard_map/all_to_all | solution.py:269
  (2 other events, 1.6 us)
Sparse Core Ops, SparseCore 0:
  10.9 68.6 all-gather.2
Sparse Core Ops, SparseCore 1:
  73.7 45.3 reduce-scatter.1

commit v4 on v1

v4 whole, which is shorter than its diff:
```python
import functools

import jax
import jax.numpy as jnp
from jax import lax
from jax.experimental import pallas as pl
from jax.experimental.pallas import tpu as pltpu
from jax.sharding import Mesh, PartitionSpec as P

BF = jnp.bfloat16
F32 = jnp.float32
NT = (((1,), (1,)), ((), ()))
NN = (((1,), (0,)), ((), ()))
VMEM = pl.BlockSpec(memory_space=pltpu.VMEM)


def dot(a, b, dims=NN):
    return lax.dot_general(a, b, dims, preferred_element_type=F32)


def remaining_steps(sizes, mask, count):
    ends = jnp.cumsum(sizes)
    starts = ends - sizes
    place = jnp.arange(count, dtype=jnp.int32)[:, None]
    inside = (place >= starts[None, :]) & (place < ends[None, :])
    offset = jnp.sum(jnp.where(inside, place - starts[None, :], 0), axis=1)
    length = jnp.sum(jnp.where(inside, sizes[None, :], 0), axis=1)
    return (jnp.minimum(length - 1 - offset, 3) * mask).astype(F32)


SMEM = pl.BlockSpec(memory_space=pltpu.SMEM)
PLENTY = pltpu.CompilerParams(vmem_limit_bytes=40 * 1024 * 1024)


def blocks_at(place_ref, core, step):
    block = 2 * lax.rem(place_ref[2] + step, 4) + core
    return pl.ds(pl.multiple_of(block * 512, 512), 512)


def give_kernel(place_ref, partials_ref, out_ref):
    for step in range(4):
        out_ref[step] = partials_ref[:, blocks_at(place_ref, 1 - place_ref[0], step)]


def give_blocks(place, partials):
    return pl.pallas_call(
        give_kernel,
        in_specs=[SMEM, VMEM],
        out_specs=VMEM,
        out_shape=jax.ShapeDtypeStruct((4, 256, 512), BF),
        compiler_params=PLENTY,
        name="give_blocks",
    )(place, partials)


def pair_kernel(place_ref, partials_ref, other_ref, *out_refs):
    for step in range(4):
        own = partials_ref[:, blocks_at(place_ref, place_ref[0], step)].astype(F32)
        out_refs[step][...] = (own + other_ref[step].astype(F32)).astype(BF)


def pair_blocks(place, partials, other):
    return pl.pallas_call(
        pair_kernel,
        in_specs=[SMEM, VMEM, VMEM],
        out_specs=[VMEM] * 4,
        out_shape=[jax.ShapeDtypeStruct((256, 512), BF)] * 4,
        compiler_params=PLENTY,
        name="pair_blocks",
    )(place, partials, other)


def high_kernel(s0, s1, s2, s3, resid_ref, out_ref):
    total = s0[...].astype(F32) + s1[...].astype(F32) + s2[...].astype(F32) + s3[...].astype(F32)
    high = (total + resid_ref[...].astype(F32)).astype(BF)
    for x in range(4):
        out_ref[x] = high


def high_copies(sums, resid):
    return pl.pallas_call(
        high_kernel,
        in_specs=[VMEM] * 5,
        out_specs=VMEM,
        out_shape=jax.ShapeDtypeStruct((4, 256, 512), BF),
        name="high_copies",
    )(*sums, resid)


def term_kernel(other, place_ref, p0, p1, p2, p3, high_ref, rows_ref, out_ref):
    half = 1 - place_ref[0] if other else place_ref[0]
    weights = [
        jnp.concatenate(
            [rows_ref[lax.rem(place_ref[2] + step, 4), half, piece] for step in range(4)], axis=0
        )
        for piece in range(3)
    ]
    pairs = (p0, p1, p2, p3)

    def terms(group):
        pair_ref = pairs[group]
        total = dot(pair_ref[0:256], weights[0], NT)
        total += dot(pair_ref[256:512], weights[1], NT)
        return total + dot(high_ref[lax.rem(place_ref[1] + (4 - group), 4)], weights[2], NT)

    for low in range(2):
        left, right = terms(low), terms(low + 2)
        for step in range(4):
            cut = slice(step * 64, step * 64 + 64)
            out_ref[step, low * 256 : (low + 1) * 256, :] = jnp.concatenate(
                [left[:, cut], right[:, cut]], axis=1
            ).astype(BF)


def term_half(other, place, pairs, high, rows):
    return pl.pallas_call(
        functools.partial(term_kernel, other),
        in_specs=[SMEM] + [VMEM] * 6,
        out_specs=VMEM,
        out_shape=jax.ShapeDtypeStruct((4, 512, 128), BF),
        compiler_params=PLENTY,
        cost_estimate=pl.CostEstimate(
            flops=2 * 1024 * 1536 * 256, bytes_accessed=5 * 1024 * 1024, transcendentals=0
        ),
        name="term_half",
    )(place, *pairs, high, rows)


def spread_kernel(t0, t1, t2, t3, p0, p1, p2, p3, out_ref):
    total = t0[...].astype(F32) + t1[...].astype(F32) + t2[...].astype(F32) + t3[...].astype(F32)
    joined = total.astype(BF)
    row = lax.broadcasted_iota(jnp.int32, (1024, 256), 0)
    parts = []
    for group, pair_ref in enumerate((p0, p1, p2, p3)):
        low = group % 2
        shard = pair_ref[512:513, 0:256].astype(jnp.int32)
        rank = pair_ref[512:513, 256:512].astype(jnp.int32)
        hot = jnp.where(row == shard * 16 + (low * 8 + rank), 1.0, 0.0).astype(BF)
        parts.append(dot(hot, joined[low * 256 : (low + 1) * 256]))
    lane = lax.broadcasted_iota(jnp.int32, (1024, 128), 1)
    moved = jnp.where(lane < 64, parts[0] + parts[1], parts[2] + parts[3])
    out_ref[...] = moved.astype(BF).reshape(64, 16, 128)


def spread(terms, pairs):
    return pl.pallas_call(
        spread_kernel,
        in_specs=[VMEM] * 8,
        out_specs=VMEM,
        out_shape=jax.ShapeDtypeStruct((64, 16, 128), BF),
        compiler_params=PLENTY,
        name="spread",
    )(*terms, *pairs)


def source_rows(rows_ref, block, parity, x):
    pieces = []
    for odd in range(2):
        tile = rows_ref[block, 4 * odd + x].astype(F32)
        for group in range(4):
            came = (x - group) % 4
            low, right = came % 2, came // 2
            at = (parity ^ odd) * 16 + low * 8
            pieces.append(tile[at : at + 8, right * 64 : right * 64 + 64])
    return jnp.concatenate(pieces, axis=0)


def chain_kernel(rows_ref, in_ref, out_ref, grad_ref, final_ref, h0, h1, h2):
    for block in range(8):
        for k in range(4):
            x = 2 * (k % 2)
            h0[:, block * 512 + k * 128 : block * 512 + (k + 1) * 128] = jnp.concatenate(
                [
                    source_rows(rows_ref, block, k // 2, x),
                    source_rows(rows_ref, block, k // 2, x + 1),
                ],
                axis=1,
            )
    goals, lefts = [], []
    for source in range(8):
        sides = [rows_ref[block, source].astype(F32)[32:40] for block in range(8)]
        goals.append(jnp.concatenate([one[:, 0:16] for one in sides], axis=1))
        lefts.append(sides[0][:, 16:17])
    goal = jnp.concatenate(goals, axis=0)
    left = jnp.concatenate(lefts, axis=0)
    states = (h0, h1, h2)
    invs, pres = [], []
    for step in range(3):
        state = states[step][...]
        inv = lax.rsqrt(jnp.sum(state * state, axis=-1, keepdims=True) * (1.0 / 4096) + 1e-06)
        pre = dot((state * inv).astype(BF), in_ref[...])
        active = (pre * jax.nn.sigmoid(pre)).astype(BF)
        invs.append(inv)
        pres.append(pre)
        after = state + dot(active, out_ref[...])
        if step < 2:
            states[step + 1][...] = after
        else:
            final_ref[...] = after.astype(BF)
    for step in (2, 1, 0):
        inv, pre = invs[step], pres[step]
        live = jnp.where(left > step, pre - goal, 0.0)
        if step == 2:
            dpre = live.astype(BF)
        else:
            dact = dot(grad_ref[...].astype(BF), out_ref[...], NT)
            sig = jax.nn.sigmoid(pre)
            dpre = (dact * (sig + pre * sig * (1.0 - sig)) + live).astype(BF)
        dnorm = dot(dpre, in_ref[...], NT)
        state = states[step][...]
        mean = jnp.sum(dnorm * state, axis=-1, keepdims=True) * (1.0 / 4096)
        back = inv * dnorm - state * (inv * inv * inv * mean)
        if step < 2:
            back = grad_ref[...] + back
        grad_ref[...] = back


def chain(rows, step_in, step_out):
    return pl.pallas_call(
        chain_kernel,
        in_specs=[VMEM] * 3,
        out_specs=[VMEM] * 2,
        out_shape=[
            jax.ShapeDtypeStruct((64, 4096), F32),
            jax.ShapeDtypeStruct((64, 4096), BF),
        ],
        scratch_shapes=[pltpu.VMEM((64, 4096), F32)] * 3,
        compiler_params=pltpu.CompilerParams(vmem_limit_bytes=40 * 1024 * 1024),
        name="chain",
    )(rows, step_in, step_out)


def per_device(
    partials, resid, low, mid, joining, step_in, step_out, targets, lengths, loss_mask, dest
):
    tensor, dp = ("y", "c"), ("zh", "zl", "x")
    me = lax.axis_index("y") * 2 + lax.axis_index("c")
    place = jnp.stack([lax.axis_index("c"), lax.axis_index("x"), lax.axis_index("y")])
    place = place.astype(jnp.int32)

    mine = lax.all_gather(jnp.swapaxes(joining, 1, 2), "zh")

    other = lax.ppermute(give_blocks(place, partials), "c", ring(2, 1))
    sums = along_y(pair_blocks(place, partials, other))

    shard = dest[:, 0]
    earlier = jnp.arange(256)[:, None] > jnp.arange(256)[None, :]
    rank = jnp.sum(((shard[:, None] == shard[None, :]) & earlier).astype(jnp.int32), axis=1)
    extra = jnp.concatenate([shard, rank]).astype(BF)[None, :]
    extra = jnp.pad(extra, ((0, 15), (0, 0)))
    pair = jnp.concatenate([low, mid, extra], axis=0)
    pairs = [pair] + [lax.ppermute(pair, "x", ring(4, shift)) for shift in range(1, 4)]

    left = remaining_steps(lengths[0], loss_mask, 256).astype(BF)
    side = lax.dynamic_slice_in_dim(targets, me * 16, 16, 1)
    side = jnp.concatenate([side, jnp.broadcast_to(left[:, None], (256, 112))], axis=1)
    slot = jnp.arange(512, dtype=jnp.int32)[:, None] == (shard * 8 + rank)[None, :]
    side = jnp.dot(slot.astype(BF), side, preferred_element_type=F32).astype(BF)
    side = side.reshape(64, 8, 128)

    high = high_copies(sums, resid)
    high, side, *pairs = lax.optimization_barrier((high, side, *pairs))
    high = lax.all_to_all(high, "x", split_axis=0, concat_axis=0, tiled=True)

    swaps = [(2 * z + c, 2 * ((z + 1 - 2 * c) % 16) + c) for z in range(16) for c in range(2)]
    theirs = lax.ppermute(mine, ("zh", "zl", "c"), swaps)
    moved = []
    for rows in (mine, theirs):
        rows = rows.reshape(4, 2, 3, 64, 512)
        other = lax.ppermute(term_half(True, place, pairs, high, rows), "c", ring(2, 1))
        own = term_half(False, place, pairs, high, rows)
        terms = (own.astype(F32) + other.astype(F32)).astype(BF)
        terms = spread(along_y([terms[step] for step in range(4)]), pairs)
        if not moved:
            terms = jnp.concatenate([terms, side], axis=1)
        moved.append(lax.all_to_all(terms, dp, split_axis=0, concat_axis=0, tiled=True))
    moved = jnp.concatenate([moved[0][:, :16], moved[1], moved[0][:, 16:]], axis=1)
    moved = lax.all_to_all(
        moved.reshape(8, 8, 40, 128), tensor, split_axis=0, concat_axis=0, tiled=True
    )
    grad, final = chain(moved, step_in, step_out)
    return (grad, final)


def along_y(parts):
    return [parts[0]] + [lax.ppermute(parts[step], "y", ring(4, step)) for step in range(1, 4)]


def ring(size, shift):
    return [(i, (i + shift) % size) for i in range(size)]


def solution(mesh):
    fine = Mesh(mesh.devices.reshape(8, 2, 4, 4, 2), ("zh", "zl", "x", "y", "c"))
    dp, tensor = ("zh", "zl", "x"), ("y", "c")
    in_specs = (
        P(dp, tensor),
        P(dp, tensor),
        P(dp, tensor),
        P(dp, tensor),
        P(None, tensor, dp),
        P(),
        P(),
        P(dp, None),
        P(dp, None),
        P(dp),
        P(dp, None),
    )
    out_specs = (P(dp + tensor, None), P(dp + tensor, None))
    return jax.shard_map(
        per_device, mesh=fine, in_specs=in_specs, out_specs=out_specs, check_vma=False
    )
```

time: 224 us -> 203 us (0.906)
  waiting for transfers between devices: 102 us -> 46.6 us
  starting transfers between devices: 43 us -> 72.1 us
  Pallas kernels: 12 us -> 24.6 us
  local copies, waits for them, and re-layouts: 9.97 us -> 6.81 us
    ppermute x1 -> x16, starting transfers between devices: 11.6 us -> 50.6 us  [the longest x9 23.6 us: along_y(): lax.ppermute(parts[step], 'y', ring(4, step))]
    reduce_scatter x1 -> x0, waiting for transfers between devices: 37.9 us -> none  [per_device(): lax.psum_scatter(split, tensor, scatter_dimension=0, tiled=False)]
    all_to_all x5 -> x2, waiting for transfers between devices: 51.1 us -> 17.7 us  [per_device(): lax.all_to_all(terms, dp, split_axis=0, concat_axis=0, tiled=True)]
    ppermute x1 -> x16, waiting for transfers between devices: 0.02 us -> 28.2 us  [the longest x9 28.2 us: along_y(): lax.ppermute(parts[step], 'y', ring(4, step))]
    pallas_call x4 -> x10, Pallas kernels: 12 us -> 24.6 us  [the longest x4 10.1 us: term_half(): pl.pallas_call(functools.partial(term_kernel, other), in_specs=[SMEM] + [...]
    all_gather x1, waiting for transfers between devices: 12.2 us -> 0.01 us  [per_device(): mine = lax.all_gather(jnp.swapaxes(joining, 1, 2), 'zh')]
    all_to_all x5 -> x2, starting transfers between devices: 31.3 us -> 21.4 us  [per_device(): lax.all_to_all(terms, dp, split_axis=0, concat_axis=0, tiled=True)]
    broadcast_in_dim x3 -> x1, local copies, waits for them, and re-layouts: 2.7 us -> 0.1 us  [per_device(): jnp.broadcast_to(left[:, None], (256, 112))]
  transfers between devices with their start and end apart: 8 -> 19, of which waited for: 6 -> 8; matrix products, arithmetic and copies ran while one was open for 2% -> 2% of each run, Pallas kernels for 1% -> 7%
where the time goes in v4:
time: 203 us; the launch traced here: 202 us
  starting transfers between devices  72.1 us (36%)
  waiting for transfers between devices  46.6 us (23%)
  blocking collectives  35.4 us (17%)
  Pallas kernels  24.6 us (12%)
  between operations  14.5 us (7%)
  local copies, waits for them, and re-layouts  6.81 us (3%)
    ppermute x9, waiting for transfers between devices, along_y(): lax.ppermute(parts[step], 'y', ring(4, step))  28.2 us
    ppermute x9, starting transfers between devices, along_y(): lax.ppermute(parts[step], 'y', ring(4, step))  23.6 us
    all_to_all x2, starting transfers between devices, per_device(): lax.all_to_all(terms, dp, split_axis=0, concat_axis=0, tiled=True)  21.4 us
    all_to_all x1, blocking collectives, per_device(): lax.all_to_all(moved.reshape(8, 8, 40, 128), tensor, split_axis=0, concat...  19.2 us
    all_to_all x2, waiting for transfers between devices, per_device(): lax.all_to_all(terms, dp, split_axis=0, concat_axis=0, tiled=True)  17.7 us
    all_to_all x1, blocking collectives, per_device(): high = lax.all_to_all(high, 'x', split_axis=0, concat_axis=0, tiled=True)  16.2 us
    pallas_call x4, Pallas kernels, term_half(): pl.pallas_call(functools.partial(term_kernel, other), in_specs=[SMEM] + [...  10.1 us
    ppermute x2, starting transfers between devices, per_device(): lax.ppermute(term_half(True, place, pairs, high, rows), 'c', ring(2, 1))  9.13 us
  transfers between devices with their start and end apart: 19, of which 8 were waited for; matrix products, arithmetic and copies ran while one was open for 2% of the time, Pallas kernels for 7%

profile of v4, /device:TPU:1, one launch (start us, length us, event | category | flops | bytes accessed | tf_op | source)
XLA Modules:
  0.0 202.0 jit_solution(17663636922848223838)
XLA Ops:
  11.2 8.8 %collective-permute-start = (bf16[4,256,512]{2,1,0:T(8,128)(2,1)}, bf16[4,256,512]{2,1,0:T(8,128)(2,1)S(1)}, u32[]{:S(2)}, u32[]{:S(2)}) collective-permute-start(bf16[4,256,512]{2,1,0:T(8,128)(2,1)} %give_blocks.1), channel_id=1, source_target_pairs={{0,1},{1,0},{2,3},{3,2},{4,5},{5,4},{6,7},{7,6},{8,9},{9,8},{10,11... | collective-permute-start | bytes 3145736 | tf_op jit(solution)/shard_map/ppermute | solution.py:243
  24.1 3.4 %collective-permute-start.4 = (bf16[528,512]{1,0:T(8,128)(2,1)S(1)}, bf16[528,512]{1,0:T(8,128)(2,1)S(1)}, u32[]{:S(2)}, u32[]{:S(2)}) collective-permute-start(bf16[528,512]{1,0:T(8,128)(2,1)S(1)} %pad_maximum_fusion.1.p0), channel_id=1, source_target_pairs={{0,8},{8,16},{16,24},{24,0},{1,9},{9,17},{17,25},{25,1},{2,10},{10... | collective-permute-start | bytes 1622024 | tf_op jit(solution)/shard_map/ppermute | solution.py:252
  33.4 2.6 %collective-permute-start.2 = (bf16[256,512]{1,0:T(8,128)(2,1)}, bf16[256,512]{1,0:T(8,128)(2,1)S(1)}, u32[]{:S(2)}, u32[]{:S(2)}) collective-permute-start(bf16[256,512]{1,0:T(8,128)(2,1)} %get-tuple-element.14), channel_id=1, source_target_pairs={{0,4},{2,6},{4,0},{6,2},{1,5},{3,7},{5,1},{7,3},{8,12},{10,14},{12... | collective-permute-start | bytes 786440 | tf_op jit(solution)/shard_map/ppermute | solution.py:286
  36.0 11.4 %collective-permute-done.1.s1 = bf16[256,512]{1,0:T(8,128)(2,1)S(1)} collective-permute-done((bf16[256,512]{1,0:T(8,128)(2,1)S(1)}, bf16[256,512]{1,0:T(8,128)(2,1)S(1)}, u32[]{:S(2)}, u32[]{:S(2)}) %collective-permute-start.1) | collective-permute-done | bytes 262176 | tf_op jit(solution)/shard_map/ppermute | solution.py:286
  49.9 5.9 %collective-permute-done.3.s3 = bf16[256,512]{1,0:T(8,128)(2,1)S(1)} collective-permute-done((bf16[256,512]{1,0:T(8,128)(2,1)S(1)}, bf16[256,512]{1,0:T(8,128)(2,1)S(1)}, u32[]{:S(2)}, u32[]{:S(2)}) %collective-permute-start.3) | collective-permute-done | bytes 262176 | tf_op jit(solution)/shard_map/ppermute | solution.py:286
  56.5 2.4 %high_copies.1 = bf16[4,256,512]{2,1,0:T(8,128)(2,1)} custom-call(bf16[256,512]{1,0:T(8,128)(2,1)} %copy-done.5, bf16[256,512]{1,0:T(8,128)(2,1)} %copy-done.6, bf16[256,512]{1,0:T(8,128)(2,1)} %copy-done.7, bf16[256,512]{1,0:T(8,128)(2,1)} %copy-done.8, bf16[256,512]{1,0:T(8,128)(2,1)} %resid_ref.1), custom_call_target="tpu_custom_call" | custom-call | tf_op jit(solution)/shard_map/high_copies/pallas_call | solution.py:81
  58.9 16.2 %all_to_all.20.high_ref = bf16[4,256,512]{2,1,0:T(8,128)(2,1)S(1)} all-to-all(bf16[4,256,512]{2,1,0:T(8,128)(2,1)} %high_copies.1), channel_id=1, replica_groups=mesh['zh'=8,'zl'=2,'x'=4,'y'=4,'c'=2] {'x'}, dimensions={0} | all-to-all | bytes 2097152 | tf_op jit(solution)/shard_map/all_to_all | solution.py:263
  75.1 2.5 %term_half.5 = bf16[4,512,128]{2,1,0:T(8,128)(2,1)S(1)} custom-call(s32[3]{0:T(128)S(1)} %pad_add_fusion.place_ref, bf16[528,512]{1,0:T(8,128)(2,1)S(1)} %pad_maximum_fusion.1.p0, bf16[528,512]{1,0:T(8,128)(2,1)S(1)} %collective-permute-done.4.p1, bf16[528,512]{1,0:T(8,128)(2,1)S(1)} %collective-permute-done.5.p2, ...), custom_call_target="tpu_custom_call" | custom-call | flops 805306368 | bytes 5242880 | tf_op jit(solution)/shard_map/term_half/pallas_call | solution.py:116
  77.6 6.0 %collective-permute-start.7 = (bf16[4,512,128]{2,1,0:T(8,128)(2,1)S(1)}, bf16[4,512,128]{2,1,0:T(8,128)(2,1)S(1)}, u32[]{:S(2)}, u32[]{:S(2)}) collective-permute-start(bf16[4,512,128]{2,1,0:T(8,128)(2,1)S(1)} %term_half.5), channel_id=1, source_target_pairs={{0,1},{1,0},{2,3},{3,2},{4,5},{5,4},{6,7},{7,6},{8,9},{9,8},{10,11... | collective-permute-start | bytes 1572872 | tf_op jit(solution)/shard_map/ppermute | solution.py:270
  85.5 2.5 %term_half.4 = bf16[4,512,128]{2,1,0:T(8,128)(2,1)S(1)} custom-call(s32[3]{0:T(128)S(1)} %pad_add_fusion.place_ref, bf16[528,512]{1,0:T(8,128)(2,1)S(1)} %pad_maximum_fusion.1.p0, bf16[528,512]{1,0:T(8,128)(2,1)S(1)} %collective-permute-done.4.p1, bf16[528,512]{1,0:T(8,128)(2,1)S(1)} %collective-permute-done.5.p2, ...), custom_call_target="tpu_custom_call" | custom-call | flops 805306368 | bytes 5242880 | tf_op jit(solution)/shard_map/term_half/pallas_call | solution.py:116
  88.3 3.4 %collective-permute-start.10 = (bf16[512,128]{1,0:T(8,128)(2,1)S(1)}, bf16[512,128]{1,0:T(8,128)(2,1)S(1)}, u32[]{:S(2)}, u32[]{:S(2)}) collective-permute-start(bf16[512,128]{1,0:T(8,128)(2,1)S(1)} %get-tuple-element.28), channel_id=1, source_target_pairs={{0,6},{2,0},{4,2},{6,4},{1,7},{3,1},{5,3},{7,5},{8,14},{10,8},{12,... | collective-permute-start | bytes 393224 | tf_op jit(solution)/shard_map/ppermute | solution.py:286
  91.7 3.7 %collective-permute-start.9 = (bf16[512,128]{1,0:T(8,128)(2,1)S(1)}, bf16[512,128]{1,0:T(8,128)(2,1)S(1)}, u32[]{:S(2)}, u32[]{:S(2)}) collective-permute-start(bf16[512,128]{1,0:T(8,128)(2,1)S(1)} %get-tuple-element.29), channel_id=1, source_target_pairs={{0,4},{2,6},{4,0},{6,2},{1,5},{3,7},{5,1},{7,3},{8,12},{10,14},{12... | collective-permute-start | bytes 393224 | tf_op jit(solution)/shard_map/ppermute | solution.py:286
  95.4 2.8 %collective-permute-start.8 = (bf16[512,128]{1,0:T(8,128)(2,1)S(1)}, bf16[512,128]{1,0:T(8,128)(2,1)S(1)}, u32[]{:S(2)}, u32[]{:S(2)}) collective-permute-start(bf16[512,128]{1,0:T(8,128)(2,1)S(1)} %get-tuple-element.30), channel_id=1, source_target_pairs={{0,2},{2,4},{4,6},{6,0},{1,3},{3,5},{5,7},{7,1},{8,10},{10,12},{12... | collective-permute-start | bytes 393224 | tf_op jit(solution)/shard_map/ppermute | solution.py:286
  99.9 3.6 %collective-permute-done.8.t1 = bf16[512,128]{1,0:T(8,128)(2,1)S(1)} collective-permute-done((bf16[512,128]{1,0:T(8,128)(2,1)S(1)}, bf16[512,128]{1,0:T(8,128)(2,1)S(1)}, u32[]{:S(2)}, u32[]{:S(2)}) %collective-permute-start.8) | collective-permute-done | bytes 131104 | tf_op jit(solution)/shard_map/ppermute | solution.py:286
  105.0 8.0 %all-to-all-start.1 = ((bf16[64,24,128]{2,1,0:T(8,128)(2,1)}), bf16[64,24,128]{2,1,0:T(8,128)(2,1)}, u32[]{:S(2)}, u32[]{:S(2)}) async-start(bf16[64,24,128]{2,1,0:T(8,128)(2,1)} %pad_maximum_fusion.2), calls=%async_computation.1 | async-start | bytes 786432 | tf_op jit(solution)/shard_map/all_to_all | solution.py:276
  113.1 2.5 %term_half.7 = bf16[4,512,128]{2,1,0:T(8,128)(2,1)S(1)} custom-call(s32[3]{0:T(128)S(1)} %pad_add_fusion.place_ref, bf16[528,512]{1,0:T(8,128)(2,1)S(1)} %pad_maximum_fusion.1.p0, bf16[528,512]{1,0:T(8,128)(2,1)S(1)} %collective-permute-done.4.p1, bf16[528,512]{1,0:T(8,128)(2,1)S(1)} %collective-permute-done.5.p2, ...), custom_call_target="tpu_custom_call" | custom-call | flops 805306368 | bytes 5242880 | tf_op jit(solution)/shard_map/term_half/pallas_call | solution.py:116
  115.6 3.2 %collective-permute-start.12 = (bf16[4,512,128]{2,1,0:T(8,128)(2,1)S(1)}, bf16[4,512,128]{2,1,0:T(8,128)(2,1)S(1)}, u32[]{:S(2)}, u32[]{:S(2)}) collective-permute-start(bf16[4,512,128]{2,1,0:T(8,128)(2,1)S(1)} %term_half.7), channel_id=1, source_target_pairs={{0,1},{1,0},{2,3},{3,2},{4,5},{5,4},{6,7},{7,6},{8,9},{9,8},{10,11... | collective-permute-start | bytes 1572872 | tf_op jit(solution)/shard_map/ppermute | solution.py:270
  118.8 2.5 %term_half.6 = bf16[4,512,128]{2,1,0:T(8,128)(2,1)S(1)} custom-call(s32[3]{0:T(128)S(1)} %pad_add_fusion.place_ref, bf16[528,512]{1,0:T(8,128)(2,1)S(1)} %pad_maximum_fusion.1.p0, bf16[528,512]{1,0:T(8,128)(2,1)S(1)} %collective-permute-done.4.p1, bf16[528,512]{1,0:T(8,128)(2,1)S(1)} %collective-permute-done.5.p2, ...), custom_call_target="tpu_custom_call" | custom-call | flops 805306368 | bytes 5242880 | tf_op jit(solution)/shard_map/term_half/pallas_call | solution.py:116
  123.4 3.3 %collective-permute-start.14 = (bf16[512,128]{1,0:T(8,128)(2,1)S(1)}, bf16[512,128]{1,0:T(8,128)(2,1)S(1)}, u32[]{:S(2)}, u32[]{:S(2)}) collective-permute-start(bf16[512,128]{1,0:T(8,128)(2,1)S(1)} %get-tuple-element.25), channel_id=1, source_target_pairs={{0,4},{2,6},{4,0},{6,2},{1,5},{3,7},{5,1},{7,3},{8,12},{10,14},{12... | collective-permute-start | bytes 393224 | tf_op jit(solution)/shard_map/ppermute | solution.py:286
  128.9 3.2 %collective-permute-done.14.t2 = bf16[512,128]{1,0:T(8,128)(2,1)S(1)} collective-permute-done((bf16[512,128]{1,0:T(8,128)(2,1)S(1)}, bf16[512,128]{1,0:T(8,128)(2,1)S(1)}, u32[]{:S(2)}, u32[]{:S(2)}) %collective-permute-start.14) | collective-permute-done | bytes 131104 | tf_op jit(solution)/shard_map/ppermute | solution.py:286
  137.1 13.4 %all-to-all-start.2 = ((bf16[64,16,128]{2,1,0:T(8,128)(2,1)}), bf16[64,16,128]{2,1,0:T(8,128)(2,1)S(1)}, u32[]{:S(2)}, u32[]{:S(2)}) async-start(bf16[64,16,128]{2,1,0:T(8,128)(2,1)} %spread.3), calls=%async_computation.2 | async-start | bytes 524288 | tf_op jit(solution)/shard_map/all_to_all | solution.py:276
  152.4 16.5 %all-to-all-done.2 = bf16[64,16,128]{2,1,0:T(8,128)(2,1)S(1)} async-done(((bf16[64,16,128]{2,1,0:T(8,128)(2,1)}), bf16[64,16,128]{2,1,0:T(8,128)(2,1)S(1)}, u32[]{:S(2)}, u32[]{:S(2)}) %all-to-all-start.2) | async-done | bytes 262176 | tf_op jit(solution)/shard_map/all_to_all | solution.py:276
  169.0 19.2 %all_to_all.21.rows_ref = bf16[8,8,40,128]{3,2,1,0:T(8,128)(2,1)S(1)} all-to-all(bf16[8,8,40,128]{3,2,1,0:T(8,128)(2,1)S(1)} %bitcast.38), channel_id=1, replica_groups=mesh['zh'=8,'zl'=2,'x'=4,'y'=4,'c'=2] {'y','c'}, dimensions={0} | all-to-all | bytes 1310720 | tf_op jit(solution)/shard_map/all_to_all | solution.py:278
  188.2 6.9 %chain.1 = (f32[64,4096]{1,0:T(8,128)}, bf16[64,4096]{1,0:T(8,128)(2,1)}) custom-call(bf16[8,8,40,128]{3,2,1,0:T(8,128)(2,1)S(1)} %all_to_all.21.rows_ref, bf16[4096,128]{1,0:T(8,128)(2,1)S(1)} %copy-done.3, bf16[128,4096]{1,0:T(8,128)(2,1)S(1)} %copy-done.4), custom_call_target="tpu_custom_call" | custom-call | tf_op jit(solution)/shard_map/chain/pallas_call | solution.py:219
  (77 shorter events, 33.7 us)
Async XLA Ops:
  7.2 42.2 %copy-start = (bf16[256,128]{1,0:T(8,128)(2,1)S(1)}, bf16[256,128]{1,0:T(8,128)(2,1)}, u32[]{:S(2)}) copy-start(bf16[256,128]{1,0:T(8,128)(2,1)} %param.18) | copy-start | bytes 196612
  7.2 67.9 %all-gather.3.cloned.1.call-start = ((), (), s32[]{:S(2)}) async-start(), calls=%async_computation.4 | async-start | bytes 1769472 | tf_op jit(solution)/shard_map/all_gather | solution.py:241
  9.6 17.9 %copy-start.13 = (s32[1,8]{1,0:T(1,128)S(1)}, s32[1,8]{1,0:T(1,128)}, u32[]{:S(2)}) copy-start(s32[1,8]{1,0:T(1,128)} %param.19) | copy-start | bytes 100
  11.2 16.5 %collective-permute-start = (bf16[4,256,512]{2,1,0:T(8,128)(2,1)}, bf16[4,256,512]{2,1,0:T(8,128)(2,1)S(1)}, u32[]{:S(2)}, u32[]{:S(2)}) collective-permute-start(bf16[4,256,512]{2,1,0:T(8,128)(2,1)} %give_blocks.1), channel_id=1, source_target_pairs={{0,1},{1,0},{2,3},{3,2},{4,5},{5,4},{6,7},{7,6},{8,9},{9,8},{10,11... | collective-permute-start | bytes 3145736 | tf_op jit(solution)/shard_map/ppermute | solution.py:243
  20.3 38.6 %collective-permute-start.6 = (bf16[528,512]{1,0:T(8,128)(2,1)S(1)}, bf16[528,512]{1,0:T(8,128)(2,1)S(1)}, u32[]{:S(2)}, u32[]{:S(2)}) collective-permute-start(bf16[528,512]{1,0:T(8,128)(2,1)S(1)} %pad_maximum_fusion.1.p0), channel_id=1, source_target_pairs={{0,24},{8,0},{16,8},{24,16},{1,25},{9,1},{17,9},{25,17},{2,26},{10... | collective-permute-start | bytes 1622024 | tf_op jit(solution)/shard_map/ppermute | solution.py:252
  22.2 36.7 %collective-permute-start.5 = (bf16[528,512]{1,0:T(8,128)(2,1)S(1)}, bf16[528,512]{1,0:T(8,128)(2,1)S(1)}, u32[]{:S(2)}, u32[]{:S(2)}) collective-permute-start(bf16[528,512]{1,0:T(8,128)(2,1)S(1)} %pad_maximum_fusion.1.p0), channel_id=1, source_target_pairs={{0,16},{8,24},{16,0},{24,8},{1,17},{9,25},{17,1},{25,9},{2,18},{10... | collective-permute-start | bytes 1622024 | tf_op jit(solution)/shard_map/ppermute | solution.py:252
  24.1 34.7 %collective-permute-start.4 = (bf16[528,512]{1,0:T(8,128)(2,1)S(1)}, bf16[528,512]{1,0:T(8,128)(2,1)S(1)}, u32[]{:S(2)}, u32[]{:S(2)}) collective-permute-start(bf16[528,512]{1,0:T(8,128)(2,1)S(1)} %pad_maximum_fusion.1.p0), channel_id=1, source_target_pairs={{0,8},{8,16},{16,24},{24,0},{1,9},{9,17},{17,25},{25,1},{2,10},{10... | collective-permute-start | bytes 1622024 | tf_op jit(solution)/shard_map/ppermute | solution.py:252
  29.3 20.0 %copy-start.12 = (s32[256]{0:T(256)S(1)}, s32[256]{0:T(256)}, u32[]{:S(2)}) copy-start(s32[256]{0:T(256)} %param.20) | copy-start | bytes 3076
  31.4 16.0 %collective-permute-start.1 = (bf16[256,512]{1,0:T(8,128)(2,1)S(1)}, bf16[256,512]{1,0:T(8,128)(2,1)S(1)}, u32[]{:S(2)}, u32[]{:S(2)}) collective-permute-start(bf16[256,512]{1,0:T(8,128)(2,1)S(1)} %get-tuple-element.13), channel_id=1, source_target_pairs={{0,2},{2,4},{4,6},{6,0},{1,3},{3,5},{5,7},{7,1},{8,10},{10,12},{12... | collective-permute-start | bytes 786440 | tf_op jit(solution)/shard_map/ppermute | solution.py:286
  33.4 16.5 %collective-permute-start.2 = (bf16[256,512]{1,0:T(8,128)(2,1)}, bf16[256,512]{1,0:T(8,128)(2,1)S(1)}, u32[]{:S(2)}, u32[]{:S(2)}) collective-permute-start(bf16[256,512]{1,0:T(8,128)(2,1)} %get-tuple-element.14), channel_id=1, source_target_pairs={{0,4},{2,6},{4,0},{6,2},{1,5},{3,7},{5,1},{7,3},{8,12},{10,14},{12... | collective-permute-start | bytes 786440 | tf_op jit(solution)/shard_map/ppermute | solution.py:286
  47.4 8.4 %collective-permute-start.3 = (bf16[256,512]{1,0:T(8,128)(2,1)S(1)}, bf16[256,512]{1,0:T(8,128)(2,1)S(1)}, u32[]{:S(2)}, u32[]{:S(2)}) collective-permute-start(bf16[256,512]{1,0:T(8,128)(2,1)S(1)} %get-tuple-element.15), channel_id=1, source_target_pairs={{0,6},{2,0},{4,2},{6,4},{1,7},{3,1},{5,3},{7,5},{8,14},{10,8},{12,... | collective-permute-start | bytes 786440 | tf_op jit(solution)/shard_map/ppermute | solution.py:286
  77.6 10.4 %collective-permute-start.7 = (bf16[4,512,128]{2,1,0:T(8,128)(2,1)S(1)}, bf16[4,512,128]{2,1,0:T(8,128)(2,1)S(1)}, u32[]{:S(2)}, u32[]{:S(2)}) collective-permute-start(bf16[4,512,128]{2,1,0:T(8,128)(2,1)S(1)} %term_half.5), channel_id=1, source_target_pairs={{0,1},{1,0},{2,3},{3,2},{4,5},{5,4},{6,7},{7,6},{8,9},{9,8},{10,11... | collective-permute-start | bytes 1572872 | tf_op jit(solution)/shard_map/ppermute | solution.py:270
  83.6 29.5 %collective-permute-start.11 = (bf16[8,3,64,512]{3,2,1,0:T(8,128)(2,1)}, bf16[8,3,64,512]{3,2,1,0:T(8,128)(2,1)}, u32[]{:S(2)}, u32[]{:S(2)}) collective-permute-start(bf16[8,3,64,512]{3,2,1,0:T(8,128)(2,1)} %bitcast.17), channel_id=1, source_target_pairs={{0,32},{1,481},{32,64},{33,1},{64,96},{65,33},{96,128},{97,65},{12... | collective-permute-start | bytes 4718600 | tf_op jit(solution)/shard_map/ppermute | solution.py:266
  88.3 9.9 %collective-permute-start.10 = (bf16[512,128]{1,0:T(8,128)(2,1)S(1)}, bf16[512,128]{1,0:T(8,128)(2,1)S(1)}, u32[]{:S(2)}, u32[]{:S(2)}) collective-permute-start(bf16[512,128]{1,0:T(8,128)(2,1)S(1)} %get-tuple-element.28), channel_id=1, source_target_pairs={{0,6},{2,0},{4,2},{6,4},{1,7},{3,1},{5,3},{7,5},{8,14},{10,8},{12,... | collective-permute-start | bytes 393224 | tf_op jit(solution)/shard_map/ppermute | solution.py:286
  91.7 8.2 %collective-permute-start.9 = (bf16[512,128]{1,0:T(8,128)(2,1)S(1)}, bf16[512,128]{1,0:T(8,128)(2,1)S(1)}, u32[]{:S(2)}, u32[]{:S(2)}) collective-permute-start(bf16[512,128]{1,0:T(8,128)(2,1)S(1)} %get-tuple-element.29), channel_id=1, source_target_pairs={{0,4},{2,6},{4,0},{6,2},{1,5},{3,7},{5,1},{7,3},{8,12},{10,14},{12... | collective-permute-start | bytes 393224 | tf_op jit(solution)/shard_map/ppermute | solution.py:286
  95.4 8.1 %collective-permute-start.8 = (bf16[512,128]{1,0:T(8,128)(2,1)S(1)}, bf16[512,128]{1,0:T(8,128)(2,1)S(1)}, u32[]{:S(2)}, u32[]{:S(2)}) collective-permute-start(bf16[512,128]{1,0:T(8,128)(2,1)S(1)} %get-tuple-element.30), channel_id=1, source_target_pairs={{0,2},{2,4},{4,6},{6,0},{1,3},{3,5},{5,7},{7,1},{8,10},{10,12},{12... | collective-permute-start | bytes 393224 | tf_op jit(solution)/shard_map/ppermute | solution.py:286
  105.0 32.1 %all-to-all-start.1 = ((bf16[64,24,128]{2,1,0:T(8,128)(2,1)}), bf16[64,24,128]{2,1,0:T(8,128)(2,1)}, u32[]{:S(2)}, u32[]{:S(2)}) async-start(bf16[64,24,128]{2,1,0:T(8,128)(2,1)} %pad_maximum_fusion.2), calls=%async_computation.1 | async-start | bytes 786432 | tf_op jit(solution)/shard_map/all_to_all | solution.py:276
  115.6 5.7 %collective-permute-start.12 = (bf16[4,512,128]{2,1,0:T(8,128)(2,1)S(1)}, bf16[4,512,128]{2,1,0:T(8,128)(2,1)S(1)}, u32[]{:S(2)}, u32[]{:S(2)}) collective-permute-start(bf16[4,512,128]{2,1,0:T(8,128)(2,1)S(1)} %term_half.7), channel_id=1, source_target_pairs={{0,1},{1,0},{2,3},{3,2},{4,5},{5,4},{6,7},{7,6},{8,9},{9,8},{10,11... | collective-permute-start | bytes 1572872 | tf_op jit(solution)/shard_map/ppermute | solution.py:270
  121.5 7.4 %collective-permute-start.15 = (bf16[512,128]{1,0:T(8,128)(2,1)S(1)}, bf16[512,128]{1,0:T(8,128)(2,1)S(1)}, u32[]{:S(2)}, u32[]{:S(2)}) collective-permute-start(bf16[512,128]{1,0:T(8,128)(2,1)S(1)} %get-tuple-element.24), channel_id=1, source_target_pairs={{0,6},{2,0},{4,2},{6,4},{1,7},{3,1},{5,3},{7,5},{8,14},{10,8},{12,... | collective-permute-start | bytes 393224 | tf_op jit(solution)/shard_map/ppermute | solution.py:286
  123.4 8.6 %collective-permute-start.14 = (bf16[512,128]{1,0:T(8,128)(2,1)S(1)}, bf16[512,128]{1,0:T(8,128)(2,1)S(1)}, u32[]{:S(2)}, u32[]{:S(2)}) collective-permute-start(bf16[512,128]{1,0:T(8,128)(2,1)S(1)} %get-tuple-element.25), channel_id=1, source_target_pairs={{0,4},{2,6},{4,0},{6,2},{1,5},{3,7},{5,1},{7,3},{8,12},{10,14},{12... | collective-permute-start | bytes 393224 | tf_op jit(solution)/shard_map/ppermute | solution.py:286
  126.7 7.7 %collective-permute-start.13 = (bf16[512,128]{1,0:T(8,128)(2,1)S(1)}, bf16[512,128]{1,0:T(8,128)(2,1)S(1)}, u32[]{:S(2)}, u32[]{:S(2)}) collective-permute-start(bf16[512,128]{1,0:T(8,128)(2,1)S(1)} %get-tuple-element.26), channel_id=1, source_target_pairs={{0,2},{2,4},{4,6},{6,0},{1,3},{3,5},{5,7},{7,1},{8,10},{10,12},{12... | collective-permute-start | bytes 393224 | tf_op jit(solution)/shard_map/ppermute | solution.py:286
  137.1 31.9 %all-to-all-start.2 = ((bf16[64,16,128]{2,1,0:T(8,128)(2,1)}), bf16[64,16,128]{2,1,0:T(8,128)(2,1)S(1)}, u32[]{:S(2)}, u32[]{:S(2)}) async-start(bf16[64,16,128]{2,1,0:T(8,128)(2,1)} %spread.3), calls=%async_computation.2 | async-start | bytes 524288 | tf_op jit(solution)/shard_map/all_to_all | solution.py:276
  152.4 35.8 %copy-start.3 = (bf16[4096,128]{1,0:T(8,128)(2,1)S(1)}, bf16[4096,128]{1,0:T(8,128)(2,1)}, u32[]{:S(2)}) copy-start(bf16[4096,128]{1,0:T(8,128)(2,1)} %in_ref.1) | copy-start | bytes 3145732
  152.4 35.8 %copy-start.4 = (bf16[128,4096]{1,0:T(8,128)(2,1)S(1)}, bf16[128,4096]{1,0:T(8,128)(2,1)}, u32[]{:S(2)}) copy-start(bf16[128,4096]{1,0:T(8,128)(2,1)} %out_ref.1) | copy-start | bytes 3145732
  (9 other events, 50.5 us)
Sparse Core Ops, SparseCore 0:
  10.1 61.0 all-gather.2

commit v5 on v4

--- a/solution.py
+++ b/solution.py
@@ -87,94 +87,115 @@
     )(*sums, resid)
 
 
-def term_kernel(other, place_ref, p0, p1, p2, p3, high_ref, rows_ref, out_ref):
-    half = 1 - place_ref[0] if other else place_ref[0]
-    weights = [
-        jnp.concatenate(
-            [rows_ref[lax.rem(place_ref[2] + step, 4), half, piece] for step in range(4)], axis=0
-        )
-        for piece in range(3)
-    ]
-    pairs = (p0, p1, p2, p3)
-
-    def terms(group):
-        pair_ref = pairs[group]
-        total = dot(pair_ref[0:256], weights[0], NT)
-        total += dot(pair_ref[256:512], weights[1], NT)
-        return total + dot(high_ref[lax.rem(place_ref[1] + (4 - group), 4)], weights[2], NT)
-
-    for low in range(2):
-        left, right = terms(low), terms(low + 2)
-        for step in range(4):
-            cut = slice(step * 64, step * 64 + 64)
-            out_ref[step, low * 256 : (low + 1) * 256, :] = jnp.concatenate(
-                [left[:, cut], right[:, cut]], axis=1
-            ).astype(BF)
+def term_kernel(other, place_ref, p0, p1, p2, p3, high_ref, r0, r1, r2, r3, out_ref, held, sems):
+    core, along, z = place_ref[0], place_ref[1], place_ref[3]
+    half = 1 - core if other else core
+
+    def away(block, odd):
+        behind = z - (4 * block + 2 * half + odd)
+        return lax.rem(jnp.where(core == 0, behind, -behind) + 32, 16)
+
+    for odd in range(2):
+        part = lax.rem(away(0, odd), 4)
+        for k, rows_ref in enumerate((r0, r1, r2, r3)):
+
+            @pl.when(part == k)
+            def _(rows_ref=rows_ref):
+                pltpu.make_async_copy(rows_ref, held.at[odd], sems.at[odd]).start()
+
+    for odd in range(2):
+        pltpu.make_async_copy(r0, held.at[odd], sems.at[odd]).wait()
+    for two in range(2):
+        weights = []
+        for piece in range(3):
+            weights.append(
+                jnp.concatenate(
+                    [
+                        held[odd, lax.div(away(2 * two + block, odd), 4), piece]
+                        for block in range(2)
+                        for odd in range(2)
+                    ],
+                    axis=0,
+                )
+            )
+        for group, pair_ref in enumerate((p0, p1, p2, p3)):
+            total = dot(pair_ref[0:256], weights[0], NT)
+            total += dot(pair_ref[256:512], weights[1], NT)
+            total += dot(high_ref[lax.rem(along + (4 - group), 4)], weights[2], NT)
+            total = total.astype(BF)
+            for block in range(2):
+                out_ref[2 * two + block, group * 256 : (group + 1) * 256, :] = total[
+                    :, block * 128 : (block + 1) * 128
+                ]
 
 
 def term_half(other, place, pairs, high, rows):
     return pl.pallas_call(
         functools.partial(term_kernel, other),
-        in_specs=[SMEM] + [VMEM] * 6,
+        in_specs=[SMEM] + [VMEM] * 5 + [pl.BlockSpec(memory_space=pl.ANY)] * 4,
         out_specs=VMEM,
-        out_shape=jax.ShapeDtypeStruct((4, 512, 128), BF),
+        out_shape=jax.ShapeDtypeStruct((4, 1024, 128), BF),
+        scratch_shapes=[
+            pltpu.VMEM((2, 4, 3, 64, 512), BF),
+            pltpu.SemaphoreType.DMA((2,)),
+        ],
         compiler_params=PLENTY,
         cost_estimate=pl.CostEstimate(
-            flops=2 * 1024 * 1536 * 256, bytes_accessed=5 * 1024 * 1024, transcendentals=0
+            flops=2 * 1024 * 1536 * 512, bytes_accessed=6 * 1024 * 1024, transcendentals=0
         ),
         name="term_half",
-    )(place, *pairs, high, rows)
-
-
-def spread_kernel(t0, t1, t2, t3, p0, p1, p2, p3, out_ref):
-    total = t0[...].astype(F32) + t1[...].astype(F32) + t2[...].astype(F32) + t3[...].astype(F32)
+    )(place, *pairs, high, *rows)
+
+
+def spread_kernel(terms_ref, p0, p1, p2, p3, out_ref):
+    total = terms_ref[0].astype(F32)
+    for part in range(1, 4):
+        total += terms_ref[part].astype(F32)
     joined = total.astype(BF)
     row = lax.broadcasted_iota(jnp.int32, (1024, 256), 0)
-    parts = []
-    for group, pair_ref in enumerate((p0, p1, p2, p3)):
-        low = group % 2
-        shard = pair_ref[512:513, 0:256].astype(jnp.int32)
-        rank = pair_ref[512:513, 256:512].astype(jnp.int32)
-        hot = jnp.where(row == shard * 16 + (low * 8 + rank), 1.0, 0.0).astype(BF)
-        parts.append(dot(hot, joined[low * 256 : (low + 1) * 256]))
-    lane = lax.broadcasted_iota(jnp.int32, (1024, 128), 1)
-    moved = jnp.where(lane < 64, parts[0] + parts[1], parts[2] + parts[3])
-    out_ref[...] = moved.astype(BF).reshape(64, 16, 128)
+    for two in range(2):
+        moved = None
+        for odd, pair_ref in enumerate(((p0, p1), (p2, p3))[two]):
+            group = 2 * two + odd
+            shard = pair_ref[512:513, 0:256].astype(jnp.int32)
+            rank = pair_ref[512:513, 256:512].astype(jnp.int32)
+            slot = shard * 16 + (odd * 8 + rank)
+            hot = jnp.where(row == slot, 1.0, 0.0).astype(BF)
+            part = dot(hot, joined[group * 256 : (group + 1) * 256])
+            moved = part if moved is None else moved + part
+        out_ref[:, two * 16 : (two + 1) * 16, :] = moved.astype(BF).reshape(64, 16, 128)
 
 
 def spread(terms, pairs):
     return pl.pallas_call(
         spread_kernel,
-        in_specs=[VMEM] * 8,
+        in_specs=[VMEM] * 5,
         out_specs=VMEM,
-        out_shape=jax.ShapeDtypeStruct((64, 16, 128), BF),
+        out_shape=jax.ShapeDtypeStruct((64, 32, 128), BF),
         compiler_params=PLENTY,
         name="spread",
-    )(*terms, *pairs)
-
-
-def source_rows(rows_ref, block, parity, x):
-    pieces = []
-    for odd in range(2):
-        tile = rows_ref[block, 4 * odd + x].astype(F32)
-        for group in range(4):
-            came = (x - group) % 4
-            low, right = came % 2, came // 2
-            at = (parity ^ odd) * 16 + low * 8
-            pieces.append(tile[at : at + 8, right * 64 : right * 64 + 64])
-    return jnp.concatenate(pieces, axis=0)
+    )(terms, *pairs)
+
+
+def source_rows(tile, x):
+    tile = tile.astype(F32)
+    order = [8 * ((x - group) % 4) for group in range(4)]
+    return [tile[at : at + 8] for at in order]
 
 
 def chain_kernel(rows_ref, in_ref, out_ref, grad_ref, final_ref, h0, h1, h2):
     for block in range(8):
+        tiles = [
+            jnp.concatenate(
+                source_rows(rows_ref[block, x], x) + source_rows(rows_ref[block, 4 + x], x), axis=0
+            )
+            for x in range(4)
+        ]
         for k in range(4):
+            lane = (k // 2) * 64
             x = 2 * (k % 2)
             h0[:, block * 512 + k * 128 : block * 512 + (k + 1) * 128] = jnp.concatenate(
-                [
-                    source_rows(rows_ref, block, k // 2, x),
-                    source_rows(rows_ref, block, k // 2, x + 1),
-                ],
-                axis=1,
+                [tiles[x][:, lane : lane + 64], tiles[x + 1][:, lane : lane + 64]], axis=1
             )
     goals, lefts = [], []
     for source in range(8):
@@ -225,7 +246,7 @@
             jax.ShapeDtypeStruct((64, 4096), BF),
         ],
         scratch_shapes=[pltpu.VMEM((64, 4096), F32)] * 3,
-        compiler_params=pltpu.CompilerParams(vmem_limit_bytes=40 * 1024 * 1024),
+        compiler_params=PLENTY,
         name="chain",
     )(rows, step_in, step_out)
 
@@ -233,12 +254,16 @@
 def per_device(
     partials, resid, low, mid, joining, step_in, step_out, targets, lengths, loss_mask, dest
 ):
-    tensor, dp = ("y", "c"), ("zh", "zl", "x")
+    tensor, dp = ("y", "c"), ("z", "x")
     me = lax.axis_index("y") * 2 + lax.axis_index("c")
-    place = jnp.stack([lax.axis_index("c"), lax.axis_index("x"), lax.axis_index("y")])
-    place = place.astype(jnp.int32)
-
-    mine = lax.all_gather(jnp.swapaxes(joining, 1, 2), "zh")
+    place = jnp.stack([lax.axis_index(axis) for axis in ("c", "x", "y", "z")]).astype(jnp.int32)
+
+    quarter = [jnp.swapaxes(joining, 1, 2)]
+    for _ in range(3):
+        quarter.append(along_z(quarter[-1], 4))
+    rows = [jnp.stack(quarter)]
+    for _ in range(3):
+        rows.append(along_z(rows[-1], 1))
 
     other = lax.ppermute(give_blocks(place, partials), "c", ring(2, 1))
     sums = along_y(pair_blocks(place, partials, other))
@@ -262,19 +287,12 @@
     high, side, *pairs = lax.optimization_barrier((high, side, *pairs))
     high = lax.all_to_all(high, "x", split_axis=0, concat_axis=0, tiled=True)
 
-    swaps = [(2 * z + c, 2 * ((z + 1 - 2 * c) % 16) + c) for z in range(16) for c in range(2)]
-    theirs = lax.ppermute(mine, ("zh", "zl", "c"), swaps)
-    moved = []
-    for rows in (mine, theirs):
-        rows = rows.reshape(4, 2, 3, 64, 512)
-        other = lax.ppermute(term_half(True, place, pairs, high, rows), "c", ring(2, 1))
-        own = term_half(False, place, pairs, high, rows)
-        terms = (own.astype(F32) + other.astype(F32)).astype(BF)
-        terms = spread(along_y([terms[step] for step in range(4)]), pairs)
-        if not moved:
-            terms = jnp.concatenate([terms, side], axis=1)
-        moved.append(lax.all_to_all(terms, dp, split_axis=0, concat_axis=0, tiled=True))
-    moved = jnp.concatenate([moved[0][:, :16], moved[1], moved[0][:, 16:]], axis=1)
+    other = lax.ppermute(term_half(True, place, pairs, high, rows), "c", ring(2, 1))
+    own = term_half(False, place, pairs, high, rows)
+    terms = (own.astype(F32) + other.astype(F32)).astype(BF)
+    terms = lax.all_to_all(terms, "y", split_axis=0, concat_axis=0, tiled=True)
+    moved = jnp.concatenate([spread(terms, pairs), side], axis=1)
+    moved = lax.all_to_all(moved, dp, split_axis=0, concat_axis=0, tiled=True)
     moved = lax.all_to_all(
         moved.reshape(8, 8, 40, 128), tensor, split_axis=0, concat_axis=0, tiled=True
     )
@@ -286,13 +304,18 @@
     return [parts[0]] + [lax.ppermute(parts[step], "y", ring(4, step)) for step in range(1, 4)]
 
 
+def along_z(part, step):
+    pairs = [(2 * z + c, 2 * ((z + step * (1 - 2 * c)) % 16) + c) for z in range(16) for c in range(2)]
+    return lax.ppermute(part, ("z", "c"), pairs)
+
+
 def ring(size, shift):
     return [(i, (i + shift) % size) for i in range(size)]
 
 
 def solution(mesh):
-    fine = Mesh(mesh.devices.reshape(8, 2, 4, 4, 2), ("zh", "zl", "x", "y", "c"))
-    dp, tensor = ("zh", "zl", "x"), ("y", "c")
+    fine = Mesh(mesh.devices.reshape(16, 4, 4, 2), ("z", "x", "y", "c"))
+    dp, tensor = ("z", "x"), ("y", "c")
     in_specs = (
         P(dp, tensor),
         P(dp, tensor),

time: 203 us -> 218 us (1.074)
  blocking collectives: 35.4 us -> 81.3 us
  between operations: 14.5 us -> 1.07 us
  waiting for transfers between devices: 46.6 us -> 36.2 us
  Pallas kernels: 24.6 us -> 19.5 us
    all_to_all x1 -> x2, blocking collectives: 16.2 us -> 62.8 us  [the longest x1 44.3 us: per_device(): moved = lax.all_to_all(moved, dp, split_axis=0, concat_axis=0, tiled=True)]
    ppermute x1 -> x6, starting transfers between devices: 1.92 us -> 38.5 us  [along_z(): return lax.ppermute(part, ('z', 'c'), pairs)]
    ppermute x9 -> x3, waiting for transfers between devices: 28.2 us -> 3.55 us  [along_y(): lax.ppermute(parts[step], 'y', ring(4, step))]
    ppermute x1 -> x6, waiting for transfers between devices: 0.01 us -> 18.5 us  [along_z(): return lax.ppermute(part, ('z', 'c'), pairs)]
    all_to_all x2 -> x1, starting transfers between devices: 21.4 us -> 3.52 us  [per_device(): high = lax.all_to_all(high, 'x', split_axis=0, concat_axis=0, tiled=True)]
    ppermute x9 -> x3, starting transfers between devices: 23.6 us -> 10.7 us  [along_y(): lax.ppermute(parts[step], 'y', ring(4, step))]
    all_to_all x2 -> x1, waiting for transfers between devices: 17.7 us -> 10.3 us  [per_device(): high = lax.all_to_all(high, 'x', split_axis=0, concat_axis=0, tiled=True)]
    ppermute x1, starting transfers between devices: 8.77 us -> 1.92 us  [per_device(): other = lax.ppermute(give_blocks(place, partials), 'c', ring(2, 1))]
  transfers between devices with their start and end apart: 19 -> 15, of which waited for: 8 -> 7; matrix products, arithmetic and copies ran while one was open for 2% -> 1% of each run, Pallas kernels for 7% -> 4%
where the time goes in v5:
time: 218 us; the launch traced here: 217 us
  blocking collectives  81.3 us (37%)
  starting transfers between devices  70.6 us (32%)
  waiting for transfers between devices  36.2 us (17%)
  Pallas kernels  19.5 us (9%)
  local copies, waits for them, and re-layouts  5.98 us (3%)
    all_to_all x1, blocking collectives, per_device(): moved = lax.all_to_all(moved, dp, split_axis=0, concat_axis=0, tiled=True)  44.3 us
    ppermute x6, starting transfers between devices, along_z(): return lax.ppermute(part, ('z', 'c'), pairs)  38.5 us
    all_to_all x1, blocking collectives, per_device(): lax.all_to_all(moved.reshape(8, 8, 40, 128), tensor, split_axis=0, concat...  18.5 us
    ppermute x6, waiting for transfers between devices, along_z(): return lax.ppermute(part, ('z', 'c'), pairs)  18.5 us
    all_to_all x1, blocking collectives, per_device(): terms = lax.all_to_all(terms, 'y', split_axis=0, concat_axis=0, tiled=True)  18.5 us
    ppermute x3, starting transfers between devices, along_y(): lax.ppermute(parts[step], 'y', ring(4, step))  10.7 us
    all_to_all x1, waiting for transfers between devices, per_device(): high = lax.all_to_all(high, 'x', split_axis=0, concat_axis=0, tiled=True)  10.3 us
    ppermute x3, starting transfers between devices, per_device(): lax.ppermute(pair, 'x', ring(4, shift))  9.33 us
  transfers between devices with their start and end apart: 15, of which 7 were waited for; matrix products, arithmetic and copies ran while one was open for 1% of the time, Pallas kernels for 4%

profile of v5, /device:TPU:1, one launch (start us, length us, event | category | flops | bytes accessed | tf_op | source)
XLA Modules:
  0.0 217.2 jit_solution(12574092974332272123)
XLA Ops:
  0.6 13.4 %collective-permute-start.7 = (bf16[3,64,512]{2,1,0:T(8,128)(2,1)}, bf16[3,64,512]{2,1,0:T(8,128)(2,1)S(1)}, u32[]{:S(2)}, u32[]{:S(2)}) collective-permute-start(bf16[3,64,512]{2,1,0:T(8,128)(2,1)} %bitcast.26), channel_id=1, source_target_pairs={{0,128},{1,385},{32,160},{33,417},{64,192},{65,449},{96,224},{97,4... | collective-permute-start | bytes 589832 | tf_op jit(solution)/shard_map/ppermute | solution.py:309
  14.1 9.3 %collective-permute-done.7 = bf16[3,64,512]{2,1,0:T(8,128)(2,1)S(1)} collective-permute-done((bf16[3,64,512]{2,1,0:T(8,128)(2,1)}, bf16[3,64,512]{2,1,0:T(8,128)(2,1)S(1)}, u32[]{:S(2)}, u32[]{:S(2)}) %collective-permute-start.7) | collective-permute-done | bytes 196640 | tf_op jit(solution)/shard_map/ppermute | solution.py:309
  23.3 7.9 %collective-permute-start.8 = (bf16[3,64,512]{2,1,0:T(8,128)(2,1)S(1)}, bf16[3,64,512]{2,1,0:T(8,128)(2,1)S(1)}, u32[]{:S(2)}, u32[]{:S(2)}) collective-permute-start(bf16[3,64,512]{2,1,0:T(8,128)(2,1)S(1)} %collective-permute-done.7), channel_id=1, source_target_pairs={{0,128},{1,385},{32,160},{33,417},{64,192},{65,449},{96,224},{97,4... | collective-permute-start | bytes 589832 | tf_op jit(solution)/shard_map/ppermute | solution.py:309
  37.3 7.3 %collective-permute-start.9 = (bf16[3,64,512]{2,1,0:T(8,128)(2,1)S(1)}, bf16[3,64,512]{2,1,0:T(8,128)(2,1)S(1)}, u32[]{:S(2)}, u32[]{:S(2)}) collective-permute-start(bf16[3,64,512]{2,1,0:T(8,128)(2,1)S(1)} %collective-permute-done.8), channel_id=1, source_target_pairs={{0,128},{1,385},{32,160},{33,417},{64,192},{65,449},{96,224},{97,4... | collective-permute-start | bytes 589832 | tf_op jit(solution)/shard_map/ppermute | solution.py:309
  44.7 6.3 %collective-permute-done.9 = bf16[3,64,512]{2,1,0:T(8,128)(2,1)S(1)} collective-permute-done((bf16[3,64,512]{2,1,0:T(8,128)(2,1)S(1)}, bf16[3,64,512]{2,1,0:T(8,128)(2,1)S(1)}, u32[]{:S(2)}, u32[]{:S(2)}) %collective-permute-start.9) | collective-permute-done | bytes 196640 | tf_op jit(solution)/shard_map/ppermute | solution.py:309
  51.1 5.1 %collective-permute-start.10 = (bf16[4,3,64,512]{3,2,1,0:T(8,128)(2,1)S(1)}, bf16[4,3,64,512]{3,2,1,0:T(8,128)(2,1)}, u32[]{:S(2)}, u32[]{:S(2)}) collective-permute-start(bf16[4,3,64,512]{3,2,1,0:T(8,128)(2,1)S(1)} %pad_maximum_fusion.r0), channel_id=1, source_target_pairs={{0,32},{1,481},{32,64},{33,1},{64,96},{65,33},{96,128},{97,65},{12... | collective-permute-start | bytes 2359304 | tf_op jit(solution)/shard_map/ppermute | solution.py:309
  60.0 3.2 %collective-permute-start.1 = (bf16[256,512]{1,0:T(8,128)(2,1)}, bf16[256,512]{1,0:T(8,128)(2,1)S(1)}, u32[]{:S(2)}, u32[]{:S(2)}) collective-permute-start(bf16[256,512]{1,0:T(8,128)(2,1)} %get-tuple-element.13), channel_id=1, source_target_pairs={{0,2},{2,4},{4,6},{6,0},{1,3},{3,5},{5,7},{7,1},{8,10},{10,12},{12... | collective-permute-start | bytes 786440 | tf_op jit(solution)/shard_map/ppermute | solution.py:304
  63.2 4.4 %collective-permute-start.6 = (bf16[528,512]{1,0:T(8,128)(2,1)S(1)}, bf16[528,512]{1,0:T(8,128)(2,1)S(1)}, u32[]{:S(2)}, u32[]{:S(2)}) collective-permute-start(bf16[528,512]{1,0:T(8,128)(2,1)S(1)} %pad_maximum_fusion.2.p0), channel_id=1, source_target_pairs={{0,24},{8,0},{16,8},{24,16},{1,25},{9,1},{17,9},{25,17},{2,26},{10... | collective-permute-start | bytes 1622024 | tf_op jit(solution)/shard_map/ppermute | solution.py:277
  67.6 2.4 %collective-permute-start.5 = (bf16[528,512]{1,0:T(8,128)(2,1)S(1)}, bf16[528,512]{1,0:T(8,128)(2,1)S(1)}, u32[]{:S(2)}, u32[]{:S(2)}) collective-permute-start(bf16[528,512]{1,0:T(8,128)(2,1)S(1)} %pad_maximum_fusion.2.p0), channel_id=1, source_target_pairs={{0,16},{8,24},{16,0},{24,8},{1,17},{9,25},{17,1},{25,9},{2,18},{10... | collective-permute-start | bytes 1622024 | tf_op jit(solution)/shard_map/ppermute | solution.py:277
  70.3 4.5 %collective-permute-start.2 = (bf16[256,512]{1,0:T(8,128)(2,1)}, bf16[256,512]{1,0:T(8,128)(2,1)S(1)}, u32[]{:S(2)}, u32[]{:S(2)}) collective-permute-start(bf16[256,512]{1,0:T(8,128)(2,1)} %copy-done.8), channel_id=1, source_target_pairs={{0,4},{2,6},{4,0},{6,2},{1,5},{3,7},{5,1},{7,3},{8,12},{10,14},{12... | collective-permute-start | bytes 786440 | tf_op jit(solution)/shard_map/ppermute | solution.py:304
  74.8 2.8 %collective-permute-start.11 = (bf16[4,3,64,512]{3,2,1,0:T(8,128)(2,1)}, bf16[4,3,64,512]{3,2,1,0:T(8,128)(2,1)}, u32[]{:S(2)}, u32[]{:S(2)}) collective-permute-start(bf16[4,3,64,512]{3,2,1,0:T(8,128)(2,1)} %collective-permute-done.10.r1), channel_id=1, source_target_pairs={{0,32},{1,481},{32,64},{33,1},{64,96},{65,33},{96,128},{97,65},{12... | collective-permute-start | bytes 2359304 | tf_op jit(solution)/shard_map/ppermute | solution.py:309
  77.7 2.5 %collective-permute-start.4 = (bf16[528,512]{1,0:T(8,128)(2,1)S(1)}, bf16[528,512]{1,0:T(8,128)(2,1)S(1)}, u32[]{:S(2)}, u32[]{:S(2)}) collective-permute-start(bf16[528,512]{1,0:T(8,128)(2,1)S(1)} %pad_maximum_fusion.2.p0), channel_id=1, source_target_pairs={{0,8},{8,16},{16,24},{24,0},{1,9},{9,17},{17,25},{25,1},{2,10},{10... | collective-permute-start | bytes 1622024 | tf_op jit(solution)/shard_map/ppermute | solution.py:277
  80.9 3.0 %collective-permute-start.3 = (bf16[256,512]{1,0:T(8,128)(2,1)}, bf16[256,512]{1,0:T(8,128)(2,1)}, u32[]{:S(2)}, u32[]{:S(2)}) collective-permute-start(bf16[256,512]{1,0:T(8,128)(2,1)} %copy-done.7), channel_id=1, source_target_pairs={{0,6},{2,0},{4,2},{6,4},{1,7},{3,1},{5,3},{7,5},{8,14},{10,8},{12,... | collective-permute-start | bytes 786440 | tf_op jit(solution)/shard_map/ppermute | solution.py:304
  85.1 3.5 %collective-permute-done.3.s3 = bf16[256,512]{1,0:T(8,128)(2,1)} collective-permute-done((bf16[256,512]{1,0:T(8,128)(2,1)}, bf16[256,512]{1,0:T(8,128)(2,1)}, u32[]{:S(2)}, u32[]{:S(2)}) %collective-permute-start.3) | collective-permute-done | bytes 262176 | tf_op jit(solution)/shard_map/ppermute | solution.py:304
  91.1 3.8 %collective-permute-done.4.p1 = bf16[528,512]{1,0:T(8,128)(2,1)S(1)} collective-permute-done((bf16[528,512]{1,0:T(8,128)(2,1)S(1)}, bf16[528,512]{1,0:T(8,128)(2,1)S(1)}, u32[]{:S(2)}, u32[]{:S(2)}) %collective-permute-start.4) | collective-permute-done | bytes 540704 | tf_op jit(solution)/shard_map/ppermute | solution.py:277
  95.7 3.5 %all-to-all-start = ((bf16[4,256,512]{2,1,0:T(8,128)(2,1)}), bf16[4,256,512]{2,1,0:T(8,128)(2,1)S(1)}, u32[]{:S(2)}, u32[]{:S(2)}) async-start(bf16[4,256,512]{2,1,0:T(8,128)(2,1)} %high_copies.1), calls=%async_computation | async-start | bytes 2097152 | tf_op jit(solution)/shard_map/all_to_all | solution.py:288
  101.1 10.3 %all-to-all-done.high_ref = bf16[4,256,512]{2,1,0:T(8,128)(2,1)S(1)} async-done(((bf16[4,256,512]{2,1,0:T(8,128)(2,1)}), bf16[4,256,512]{2,1,0:T(8,128)(2,1)S(1)}, u32[]{:S(2)}, u32[]{:S(2)}) %all-to-all-start) | async-done | bytes 1048608 | tf_op jit(solution)/shard_map/all_to_all | solution.py:288
  113.6 3.6 %term_half.3 = bf16[4,1024,128]{2,1,0:T(8,128)(2,1)S(1)} custom-call(s32[4]{0:T(128)S(1)} %pad_add_fusion.place_ref, bf16[528,512]{1,0:T(8,128)(2,1)S(1)} %pad_maximum_fusion.2.p0, bf16[528,512]{1,0:T(8,128)(2,1)S(1)} %copy-done.3, bf16[528,512]{1,0:T(8,128)(2,1)S(1)} %collective-permute-done.5.p2, bf16[528,512]{1,0:T(8,128)(2,1)S(1)} %collective-permute-done.6.p3, ...), custom_call_target="tpu_custom_call" | custom-call | flops 1610612736 | bytes 6291456 | tf_op jit(solution)/shard_map/term_half/pallas_call | solution.py:133
  117.2 6.7 %collective-permute-start.13 = (bf16[4,1024,128]{2,1,0:T(8,128)(2,1)S(1)}, bf16[4,1024,128]{2,1,0:T(8,128)(2,1)S(1)}, u32[]{:S(2)}, u32[]{:S(2)}) collective-permute-start(bf16[4,1024,128]{2,1,0:T(8,128)(2,1)S(1)} %term_half.3), channel_id=1, source_target_pairs={{0,1},{1,0},{2,3},{3,2},{4,5},{5,4},{6,7},{7,6},{8,9},{9,8},{10,11... | collective-permute-start | bytes 3145736 | tf_op jit(solution)/shard_map/ppermute | solution.py:290
  123.9 3.8 %term_half.2 = bf16[4,1024,128]{2,1,0:T(8,128)(2,1)S(1)} custom-call(s32[4]{0:T(128)S(1)} %pad_add_fusion.place_ref, bf16[528,512]{1,0:T(8,128)(2,1)S(1)} %pad_maximum_fusion.2.p0, bf16[528,512]{1,0:T(8,128)(2,1)S(1)} %copy-done.3, bf16[528,512]{1,0:T(8,128)(2,1)S(1)} %collective-permute-done.5.p2, bf16[528,512]{1,0:T(8,128)(2,1)S(1)} %collective-permute-done.6.p3, ...), custom_call_target="tpu_custom_call" | custom-call | flops 1610612736 | bytes 6291456 | tf_op jit(solution)/shard_map/term_half/pallas_call | solution.py:133
  128.0 18.5 %all_to_all.20.terms_ref = bf16[4,1024,128]{2,1,0:T(8,128)(2,1)S(1)} all-to-all(bf16[4,1024,128]{2,1,0:T(8,128)(2,1)S(1)} %add_convert_fusion), channel_id=1, replica_groups=mesh['z'=16,'x'=4,'y'=4,'c'=2] {'y'}, dimensions={0} | all-to-all | bytes 2097152 | tf_op jit(solution)/shard_map/all_to_all | solution.py:293
  147.4 44.3 %all_to_all.21 = bf16[64,40,128]{2,1,0:T(8,128)(2,1)S(1)} all-to-all(bf16[64,40,128]{2,1,0:T(8,128)(2,1)S(1)} %pad_maximum_fusion.1), channel_id=1, replica_groups=mesh['z'=16,'x'=4,'y'=4,'c'=2] {'z','x'}, dimensions={0} | all-to-all | bytes 1310720 | tf_op jit(solution)/shard_map/all_to_all | solution.py:295
  191.7 18.5 %all_to_all.22.rows_ref = bf16[8,8,40,128]{3,2,1,0:T(8,128)(2,1)S(1)} all-to-all(bf16[8,8,40,128]{3,2,1,0:T(8,128)(2,1)S(1)} %bitcast.25), channel_id=1, replica_groups=mesh['z'=16,'x'=4,'y'=4,'c'=2] {'y','c'}, dimensions={0} | all-to-all | bytes 1310720 | tf_op jit(solution)/shard_map/all_to_all | solution.py:296
  210.3 7.0 %chain.1 = (f32[64,4096]{1,0:T(8,128)}, bf16[64,4096]{1,0:T(8,128)(2,1)}) custom-call(bf16[8,8,40,128]{3,2,1,0:T(8,128)(2,1)S(1)} %all_to_all.22.rows_ref, bf16[4096,128]{1,0:T(8,128)(2,1)S(1)} %copy-done.4, bf16[128,4096]{1,0:T(8,128)(2,1)S(1)} %copy-done.5), custom_call_target="tpu_custom_call" | custom-call | tf_op jit(solution)/shard_map/chain/pallas_call | solution.py:240
  (71 shorter events, 20.6 us)
Async XLA Ops:
  0.6 83.3 %copy-start = (bf16[256,128]{1,0:T(8,128)(2,1)S(1)}, bf16[256,128]{1,0:T(8,128)(2,1)}, u32[]{:S(2)}) copy-start(bf16[256,128]{1,0:T(8,128)(2,1)} %param.18) | copy-start | bytes 196612
  0.6 22.7 %collective-permute-start.7 = (bf16[3,64,512]{2,1,0:T(8,128)(2,1)}, bf16[3,64,512]{2,1,0:T(8,128)(2,1)S(1)}, u32[]{:S(2)}, u32[]{:S(2)}) collective-permute-start(bf16[3,64,512]{2,1,0:T(8,128)(2,1)} %bitcast.26), channel_id=1, source_target_pairs={{0,128},{1,385},{32,160},{33,417},{64,192},{65,449},{96,224},{97,4... | collective-permute-start | bytes 589832 | tf_op jit(solution)/shard_map/ppermute | solution.py:309
  23.3 14.0 %collective-permute-start.8 = (bf16[3,64,512]{2,1,0:T(8,128)(2,1)S(1)}, bf16[3,64,512]{2,1,0:T(8,128)(2,1)S(1)}, u32[]{:S(2)}, u32[]{:S(2)}) collective-permute-start(bf16[3,64,512]{2,1,0:T(8,128)(2,1)S(1)} %collective-permute-done.7), channel_id=1, source_target_pairs={{0,128},{1,385},{32,160},{33,417},{64,192},{65,449},{96,224},{97,4... | collective-permute-start | bytes 589832 | tf_op jit(solution)/shard_map/ppermute | solution.py:309
  32.9 18.1 %copy-start.13 = (bf16[3,512,64]{1,2,0:T(8,128)(2,1)S(1)}, bf16[3,512,64]{1,2,0:T(8,128)(2,1)}, u32[]{:S(2)}) copy-start(bf16[3,512,64]{1,2,0:T(8,128)(2,1)} %param.15) | copy-start | bytes 589828
  33.5 22.7 %copy-start.15 = (s32[256,1]{0,1:T(1,128)S(1)}, s32[256,1]{0,1:T(1,128)}, u32[]{:S(2)}) copy-start(s32[256,1]{0,1:T(1,128)} %param.21) | copy-start | bytes 3076
  33.5 22.9 %collective-permute-start = (bf16[4,256,512]{2,1,0:T(8,128)(2,1)S(1)}, bf16[4,256,512]{2,1,0:T(8,128)(2,1)S(1)}, u32[]{:S(2)}, u32[]{:S(2)}) collective-permute-start(bf16[4,256,512]{2,1,0:T(8,128)(2,1)S(1)} %give_blocks.1), channel_id=1, source_target_pairs={{0,1},{1,0},{2,3},{3,2},{4,5},{5,4},{6,7},{7,6},{8,9},{9,8},{10,11... | collective-permute-start | bytes 3145736 | tf_op jit(solution)/shard_map/ppermute | solution.py:268
  37.3 13.6 %collective-permute-start.9 = (bf16[3,64,512]{2,1,0:T(8,128)(2,1)S(1)}, bf16[3,64,512]{2,1,0:T(8,128)(2,1)S(1)}, u32[]{:S(2)}, u32[]{:S(2)}) collective-permute-start(bf16[3,64,512]{2,1,0:T(8,128)(2,1)S(1)} %collective-permute-done.8), channel_id=1, source_target_pairs={{0,128},{1,385},{32,160},{33,417},{64,192},{65,449},{96,224},{97,4... | collective-permute-start | bytes 589832 | tf_op jit(solution)/shard_map/ppermute | solution.py:309
  51.1 23.7 %collective-permute-start.10 = (bf16[4,3,64,512]{3,2,1,0:T(8,128)(2,1)S(1)}, bf16[4,3,64,512]{3,2,1,0:T(8,128)(2,1)}, u32[]{:S(2)}, u32[]{:S(2)}) collective-permute-start(bf16[4,3,64,512]{3,2,1,0:T(8,128)(2,1)S(1)} %pad_maximum_fusion.r0), channel_id=1, source_target_pairs={{0,32},{1,481},{32,64},{33,1},{64,96},{65,33},{96,128},{97,65},{12... | collective-permute-start | bytes 2359304 | tf_op jit(solution)/shard_map/ppermute | solution.py:309
  56.4 13.6 %copy-start.17 = (s32[1,8]{1,0:T(1,128)S(1)}, s32[1,8]{1,0:T(1,128)}, u32[]{:S(2)}) copy-start(s32[1,8]{1,0:T(1,128)} %param.19) | copy-start | bytes 100
  56.4 27.5 %copy-start.16 = (s32[256]{0:T(256)S(1)}, s32[256]{0:T(256)}, u32[]{:S(2)}) copy-start(s32[256]{0:T(256)} %param.20) | copy-start | bytes 3076
  60.0 17.7 %collective-permute-start.1 = (bf16[256,512]{1,0:T(8,128)(2,1)}, bf16[256,512]{1,0:T(8,128)(2,1)S(1)}, u32[]{:S(2)}, u32[]{:S(2)}) collective-permute-start(bf16[256,512]{1,0:T(8,128)(2,1)} %get-tuple-element.13), channel_id=1, source_target_pairs={{0,2},{2,4},{4,6},{6,0},{1,3},{3,5},{5,7},{7,1},{8,10},{10,12},{12... | collective-permute-start | bytes 786440 | tf_op jit(solution)/shard_map/ppermute | solution.py:304
  63.2 27.8 %collective-permute-start.6 = (bf16[528,512]{1,0:T(8,128)(2,1)S(1)}, bf16[528,512]{1,0:T(8,128)(2,1)S(1)}, u32[]{:S(2)}, u32[]{:S(2)}) collective-permute-start(bf16[528,512]{1,0:T(8,128)(2,1)S(1)} %pad_maximum_fusion.2.p0), channel_id=1, source_target_pairs={{0,24},{8,0},{16,8},{24,16},{1,25},{9,1},{17,9},{25,17},{2,26},{10... | collective-permute-start | bytes 1622024 | tf_op jit(solution)/shard_map/ppermute | solution.py:277
  67.6 23.4 %collective-permute-start.5 = (bf16[528,512]{1,0:T(8,128)(2,1)S(1)}, bf16[528,512]{1,0:T(8,128)(2,1)S(1)}, u32[]{:S(2)}, u32[]{:S(2)}) collective-permute-start(bf16[528,512]{1,0:T(8,128)(2,1)S(1)} %pad_maximum_fusion.2.p0), channel_id=1, source_target_pairs={{0,16},{8,24},{16,0},{24,8},{1,17},{9,25},{17,1},{25,9},{2,18},{10... | collective-permute-start | bytes 1622024 | tf_op jit(solution)/shard_map/ppermute | solution.py:277
  70.3 10.7 %collective-permute-start.2 = (bf16[256,512]{1,0:T(8,128)(2,1)}, bf16[256,512]{1,0:T(8,128)(2,1)S(1)}, u32[]{:S(2)}, u32[]{:S(2)}) collective-permute-start(bf16[256,512]{1,0:T(8,128)(2,1)} %copy-done.8), channel_id=1, source_target_pairs={{0,4},{2,6},{4,0},{6,2},{1,5},{3,7},{5,1},{7,3},{8,12},{10,14},{12... | collective-permute-start | bytes 786440 | tf_op jit(solution)/shard_map/ppermute | solution.py:304
  74.8 24.4 %collective-permute-start.11 = (bf16[4,3,64,512]{3,2,1,0:T(8,128)(2,1)}, bf16[4,3,64,512]{3,2,1,0:T(8,128)(2,1)}, u32[]{:S(2)}, u32[]{:S(2)}) collective-permute-start(bf16[4,3,64,512]{3,2,1,0:T(8,128)(2,1)} %collective-permute-done.10.r1), channel_id=1, source_target_pairs={{0,32},{1,481},{32,64},{33,1},{64,96},{65,33},{96,128},{97,65},{12... | collective-permute-start | bytes 2359304 | tf_op jit(solution)/shard_map/ppermute | solution.py:309
  77.7 11.0 %copy-start.9 = (bf16[256,512]{1,0:T(8,128)(2,1)}, bf16[256,512]{1,0:T(8,128)(2,1)S(1)}, u32[]{:S(2)}) copy-start(bf16[256,512]{1,0:T(8,128)(2,1)S(1)} %collective-permute-done.1.s1) | copy-start | bytes 786436
  77.7 17.2 %collective-permute-start.4 = (bf16[528,512]{1,0:T(8,128)(2,1)S(1)}, bf16[528,512]{1,0:T(8,128)(2,1)S(1)}, u32[]{:S(2)}, u32[]{:S(2)}) collective-permute-start(bf16[528,512]{1,0:T(8,128)(2,1)S(1)} %pad_maximum_fusion.2.p0), channel_id=1, source_target_pairs={{0,8},{8,16},{16,24},{24,0},{1,9},{9,17},{17,25},{25,1},{2,10},{10... | collective-permute-start | bytes 1622024 | tf_op jit(solution)/shard_map/ppermute | solution.py:277
  80.9 7.7 %copy-start.10 = (bf16[256,512]{1,0:T(8,128)(2,1)}, bf16[256,512]{1,0:T(8,128)(2,1)S(1)}, u32[]{:S(2)}) copy-start(bf16[256,512]{1,0:T(8,128)(2,1)S(1)} %collective-permute-done.2.s2) | copy-start | bytes 786436
  80.9 7.7 %collective-permute-start.3 = (bf16[256,512]{1,0:T(8,128)(2,1)}, bf16[256,512]{1,0:T(8,128)(2,1)}, u32[]{:S(2)}, u32[]{:S(2)}) collective-permute-start(bf16[256,512]{1,0:T(8,128)(2,1)} %copy-done.7), channel_id=1, source_target_pairs={{0,6},{2,0},{4,2},{6,4},{1,7},{3,1},{5,3},{7,5},{8,14},{10,8},{12,... | collective-permute-start | bytes 786440 | tf_op jit(solution)/shard_map/ppermute | solution.py:304
  95.7 15.8 %all-to-all-start = ((bf16[4,256,512]{2,1,0:T(8,128)(2,1)}), bf16[4,256,512]{2,1,0:T(8,128)(2,1)S(1)}, u32[]{:S(2)}, u32[]{:S(2)}) async-start(bf16[4,256,512]{2,1,0:T(8,128)(2,1)} %high_copies.1), calls=%async_computation | async-start | bytes 2097152 | tf_op jit(solution)/shard_map/all_to_all | solution.py:288
  99.2 13.3 %collective-permute-start.12 = (bf16[4,3,64,512]{3,2,1,0:T(8,128)(2,1)}, bf16[4,3,64,512]{3,2,1,0:T(8,128)(2,1)}, u32[]{:S(2)}, u32[]{:S(2)}) collective-permute-start(bf16[4,3,64,512]{3,2,1,0:T(8,128)(2,1)} %collective-permute-done.11.r2), channel_id=1, source_target_pairs={{0,32},{1,481},{32,64},{33,1},{64,96},{65,33},{96,128},{97,65},{12... | collective-permute-start | bytes 2359304 | tf_op jit(solution)/shard_map/ppermute | solution.py:309
  117.2 10.5 %collective-permute-start.13 = (bf16[4,1024,128]{2,1,0:T(8,128)(2,1)S(1)}, bf16[4,1024,128]{2,1,0:T(8,128)(2,1)S(1)}, u32[]{:S(2)}, u32[]{:S(2)}) collective-permute-start(bf16[4,1024,128]{2,1,0:T(8,128)(2,1)S(1)} %term_half.3), channel_id=1, source_target_pairs={{0,1},{1,0},{2,3},{3,2},{4,5},{5,4},{6,7},{7,6},{8,9},{9,8},{10,11... | collective-permute-start | bytes 3145736 | tf_op jit(solution)/shard_map/ppermute | solution.py:290
  147.4 62.8 %copy-start.4 = (bf16[4096,128]{1,0:T(8,128)(2,1)S(1)}, bf16[4096,128]{1,0:T(8,128)(2,1)}, u32[]{:S(2)}) copy-start(bf16[4096,128]{1,0:T(8,128)(2,1)} %in_ref.1) | copy-start | bytes 3145732
  147.4 62.8 %copy-start.5 = (bf16[128,4096]{1,0:T(8,128)(2,1)S(1)}, bf16[128,4096]{1,0:T(8,128)(2,1)}, u32[]{:S(2)}) copy-start(bf16[128,4096]{1,0:T(8,128)(2,1)} %out_ref.1) | copy-start | bytes 3145732
  (10 other events, 27.4 us)

commit v6 on v3

--- a/solution.py
+++ b/solution.py
@@ -27,67 +27,34 @@
     return (jnp.minimum(length - 1 - offset, 3) * mask).astype(F32)
 
 
-def split_kernel(in_ref, out_ref, sems):
+def high_kernel(summed_ref, resid_ref, out_ref):
+    for block in range(8):
+        total = summed_ref[:, block * 512 : (block + 1) * 512].astype(F32)
+        high = (total + resid_ref[block].astype(F32)).astype(BF)
+        for x in range(4):
+            out_ref[8 * x + block] = high
+
+
+def high_copies(summed, resid):
+    return pl.pallas_call(
+        high_kernel,
+        in_specs=[VMEM, VMEM],
+        out_specs=VMEM,
+        out_shape=jax.ShapeDtypeStruct((32, 32, 512), BF),
+        name="high_copies",
+    )(summed, resid)
+
+
+def term_kernel(half_ref, p0, p1, p2, p3, high_ref, rows_ref, out_ref, held, sems):
+    half = half_ref[0]
     copies = [
-        pltpu.make_async_copy(in_ref.at[:, pl.ds(i * 512, 512)], out_ref.at[i], sems.at[i])
-        for i in range(8)
+        pltpu.make_async_copy(rows_ref.at[i, :, half], held.at[i], sems.at[i]) for i in range(2)
     ]
     for copy in copies:
         copy.start()
-    for copy in copies:
-        copy.wait()
-
-
-def split_blocks(partials):
-    return pl.pallas_call(
-        split_kernel,
-        in_specs=[HBM],
-        out_specs=HBM,
-        out_shape=jax.ShapeDtypeStruct((8, 256, 512), BF),
-        scratch_shapes=[pltpu.SemaphoreType.DMA((8,))],
-        name="split_blocks",
-    )(partials)
-
-
-def high_kernel(summed_ref, resid_ref, out_ref):
-    high = (summed_ref[...].astype(F32) + resid_ref[...].astype(F32)).astype(BF)
-    for x in range(4):
-        out_ref[x] = high
-
-
-def high_copies(summed, resid):
-    return pl.pallas_call(
-        high_kernel,
-        in_specs=[VMEM, VMEM],
-        out_specs=VMEM,
-        out_shape=jax.ShapeDtypeStruct((4, 256, 512), BF),
-        name="high_copies",
-    )(summed, resid)
-
-
-def term_kernel(half_ref, p0, p1, p2, p3, high_ref, mine_ref, below_ref, above_ref, out_ref, held, sems):
-    half = half_ref[0]
-    copies = []
-    for i, other in ((0, below_ref), (1, above_ref)):
-        copies.append(
-            (
-                pltpu.make_async_copy(mine_ref.at[i, :, half], held.at[i, 0], sems.at[i, 0]),
-                pltpu.make_async_copy(other.at[:, half], held.at[i, 1], sems.at[i, 1]),
-            )
-        )
-    for two in copies:
-        for copy in two:
-            copy.start()
     for i in range(2):
-        for copy in copies[i]:
-            copy.wait()
-        weights = [
-            jnp.concatenate(
-                [held[i, 0, 0, piece], held[i, 1, 0, piece], held[i, 0, 1, piece], held[i, 1, 1, piece]],
-                axis=0,
-            )
-            for piece in range(3)
-        ]
+        copies[i].wait()
+        weights = [held[i, :, :, piece].reshape(256, 512) for piece in range(3)]
         for group, pair_ref in enumerate((p0, p1, p2, p3)):
             total = dot(pair_ref[0:256], weights[0], NT)
             total += dot(pair_ref[256:512], weights[1], NT)
@@ -99,22 +66,22 @@
                 ]
 
 
-def term_half(half, pairs, high, mine, below, above):
+def term_half(half, pairs, high, rows):
     return pl.pallas_call(
         term_kernel,
-        in_specs=[pl.BlockSpec(memory_space=pltpu.SMEM)] + [VMEM] * 5 + [HBM] * 3,
+        in_specs=[pl.BlockSpec(memory_space=pltpu.SMEM)] + [VMEM] * 5 + [HBM],
         out_specs=VMEM,
         out_shape=jax.ShapeDtypeStruct((4, 1024, 128), BF),
         scratch_shapes=[
             pltpu.VMEM((2, 2, 2, 3, 64, 512), BF),
-            pltpu.SemaphoreType.DMA((2, 2)),
+            pltpu.SemaphoreType.DMA((2,)),
         ],
         compiler_params=pltpu.CompilerParams(vmem_limit_bytes=40 * 1024 * 1024),
         cost_estimate=pl.CostEstimate(
             flops=2 * 1024 * 1536 * 512, bytes_accessed=6 * 1024 * 1024, transcendentals=0
         ),
         name="term_half",
-    )(half, *pairs, high, mine, below, above)
+    )(half, *pairs, high, rows)
 
 
 def spread_kernel(terms_ref, p0, p1, p2, p3, out_ref):
@@ -147,21 +114,17 @@
     )(terms, *pairs)
 
 
-def source_rows(tile, odd, x):
+def source_rows(tile, x):
     tile = tile.astype(F32)
-    tile = jnp.concatenate(
-        [tile[8 * ((x - group) % 4) : 8 * ((x - group) % 4) + 8] for group in range(4)], axis=0
-    )
-    if odd:
-        tile = jnp.concatenate([tile[:, 64:], tile[:, :64]], axis=1)
-    return tile
+    order = [8 * ((x - group) % 4) for group in range(4)]
+    return [tile[at : at + 8] for at in order]
 
 
 def chain_kernel(rows_ref, goal_ref, left_ref, in_ref, out_ref, grad_ref, final_ref, h0, h1, h2):
     for block in range(8):
         tiles = [
             jnp.concatenate(
-                [source_rows(rows_ref[block, 4 * odd + x], odd, x) for odd in range(2)], axis=0
+                source_rows(rows_ref[block, x], x) + source_rows(rows_ref[block, 4 + x], x), axis=0
             )
             for x in range(4)
         ]
@@ -223,12 +186,15 @@
 def per_device(
     partials, resid, low, mid, joining, step_in, step_out, targets, lengths, loss_mask, dest
 ):
-    tensor, dp, z = ("y", "c"), ("zh", "zl", "x"), ("zh", "zl")
+    tensor, dp, z = ("y", "c"), ("z", "x"), "z"
     me = lax.axis_index("y") * 2 + lax.axis_index("c")
     core, along = lax.axis_index("c"), lax.axis_index("x")
 
-    mine = lax.all_gather(jnp.swapaxes(joining, 1, 2), "zh")
-    summed = lax.psum_scatter(split_blocks(partials), tensor, scatter_dimension=0, tiled=False)
+    rows = lax.all_gather(jnp.swapaxes(joining, 1, 2), z).reshape(2, 2, 2, 2, 3, 64, 512)
+    summed = lax.psum_scatter(partials, tensor, scatter_dimension=0, tiled=True)
+    resid = lax.all_to_all(
+        resid.reshape(8, 32, 512), tensor, split_axis=0, concat_axis=0, tiled=True
+    )
 
     shard = dest[:, 0]
     earlier = jnp.arange(256)[:, None] > jnp.arange(256)[None, :]
@@ -237,11 +203,6 @@
     extra = jnp.pad(extra, ((0, 15), (0, 0)))
     pair = jnp.concatenate([low, mid, extra], axis=0)
     pairs = [pair] + [lax.ppermute(pair, "x", ring(4, shift)) for shift in range(1, 4)]
-
-    mine, *pairs = lax.optimization_barrier((mine, *pairs))
-    below = lax.ppermute(mine[:4], z, ring(16, 1)).reshape(2, 2, 3, 64, 512)
-    above = lax.ppermute(mine[4:], z, ring(16, -1)).reshape(2, 2, 3, 64, 512)
-    mine = mine.reshape(2, 2, 2, 3, 64, 512)
 
     left = remaining_steps(lengths[0], loss_mask, 256).astype(BF)
     side = lax.dynamic_slice_in_dim(targets, me * 16, 16, 1)
@@ -256,12 +217,13 @@
     left = jnp.broadcast_to(side[0, :, 16:17], (64, 128))
 
     high = high_copies(summed, resid)
-    high, goal, left = lax.optimization_barrier((high, goal, left))
-    high = lax.all_to_all(high, "x", split_axis=0, concat_axis=0, tiled=True)
-
-    other = term_half(jnp.stack([1 - core, along]).astype(jnp.int32), pairs, high, mine, below, above)
+    high, goal, left, *pairs = lax.optimization_barrier((high, goal, left, *pairs))
+    high = lax.all_to_all(high, ("x",) + tensor, split_axis=0, concat_axis=0, tiled=True)
+    high = high.reshape(4, 256, 512)
+
+    other = term_half(jnp.stack([1 - core, along]).astype(jnp.int32), pairs, high, rows)
     other = lax.ppermute(other, "c", ring(2, 1))
-    own = term_half(jnp.stack([core, along]).astype(jnp.int32), pairs, high, mine, below, above)
+    own = term_half(jnp.stack([core, along]).astype(jnp.int32), pairs, high, rows)
     terms = (own.astype(F32) + other.astype(F32)).astype(BF)
     terms = lax.all_to_all(terms, "y", split_axis=0, concat_axis=0, tiled=True)
     moved = spread(terms, pairs)
@@ -278,8 +240,8 @@
 
 
 def solution(mesh):
-    fine = Mesh(mesh.devices.reshape(8, 2, 4, 4, 2), ("zh", "zl", "x", "y", "c"))
-    dp, tensor = ("zh", "zl", "x"), ("y", "c")
+    fine = Mesh(mesh.devices.reshape(16, 4, 4, 2), ("z", "x", "y", "c"))
+    dp, tensor = ("z", "x"), ("y", "c")
     in_specs = (
         P(dp, tensor),
         P(dp, tensor),

time: 259 us -> 195 us (0.75)
  Pallas kernels: 81.9 us -> 15 us
  waiting for transfers between devices: 23.9 us -> 33.6 us
  local copies, waits for them, and re-layouts: 8.12 us -> 3.6 us
    pallas_call x1 -> x0, Pallas kernels: 64.7 us -> none  [split_blocks(): pl.pallas_call(split_kernel, in_specs=[HBM], out_specs=HBM, out_shape=jax...]
    all_to_all x1 -> x2, waiting for transfers between devices: 1.31 us -> 23 us  [the longest x1 16.9 us: per_device(): lax.all_to_all(high, ('x',) + tensor, split_axis=0, concat_axis=0, tiled=...]
    ppermute x2 -> x0, waiting for transfers between devices: 12.4 us -> none  [the longest x1 9.33 us: per_device(): above = lax.ppermute(mine[4:], z, ring(16, -1)).reshape(2, 2, 3, 64, 512)]
    ppermute x2 -> x0, starting transfers between devices: 5.28 us -> none  [the longest x1 3.11 us: per_device(): below = lax.ppermute(mine[:4], z, ring(16, 1)).reshape(2, 2, 3, 64, 512)]
    all_to_all x1 -> x2, starting transfers between devices: 3.52 us -> 8.68 us  [the longest x1 4.63 us: per_device(): lax.all_to_all(high, ('x',) + tensor, split_axis=0, concat_axis=0, tiled=...]
    slice x1 -> x0, local copies, waits for them, and re-layouts: 3.21 us -> none  [per_device(): above = lax.ppermute(mine[4:], z, ring(16, -1)).reshape(2, 2, 3, 64, 512)]
  transfers between devices with their start and end apart: 10 -> 9, of which waited for: 4 -> 3; matrix products, arithmetic and copies ran while one was open for 2% -> 1% of each run, Pallas kernels for 27% -> 2%
where the time goes in v6:
time: 195 us
  blocking collectives  96.7 us (50%)
  waiting for transfers between devices  33.6 us (17%)
  starting transfers between devices  28.8 us (15%)
  between operations  15.8 us (8%)
  Pallas kernels  15 us (8%)
  local copies, waits for them, and re-layouts  3.6 us (2%)
    all_to_all x1, blocking collectives, per_device(): moved = lax.all_to_all(moved, dp, split_axis=0, concat_axis=0, tiled=True)  36.5 us
    all_to_all x1, blocking collectives, per_device(): lax.all_to_all(side.reshape(64, 2, 128), dp, split_axis=0, concat_axis=0,...  30.8 us
    all_to_all x1, blocking collectives, per_device(): terms = lax.all_to_all(terms, 'y', split_axis=0, concat_axis=0, tiled=True)  17.5 us
    all_to_all x1, waiting for transfers between devices, per_device(): lax.all_to_all(high, ('x',) + tensor, split_axis=0, concat_axis=0, tiled=...  16.9 us
    all_to_all x1, blocking collectives, per_device(): lax.all_to_all(side.reshape(8, 16, 128), tensor, split_axis=0, concat_axi...  11.8 us
    ppermute x3, starting transfers between devices, per_device(): lax.ppermute(pair, 'x', ring(4, shift))  10.2 us
    all_to_all x1, waiting for transfers between devices, per_device(): lax.all_to_all(moved.reshape(8, 256, 128), tensor, split_axis=0, concat_a...  9.41 us
    all_to_all x1, starting transfers between devices, per_device(): lax.all_to_all(moved.reshape(8, 256, 128), tensor, split_axis=0, concat_a...  7.84 us
  transfers between devices with their start and end apart: 9, of which 3 were waited for; matrix products, arithmetic and copies ran while one was open for 1% of the time, Pallas kernels for 2%

profile of v6, /device:TPU:1, one launch (start us, length us, event | category | flops | bytes accessed | tf_op | source)
XLA Modules:
  0.0 194.7 jit_solution(7334498848571380234)
XLA Ops:
  8.1 0.7 reduce-scatter.2.cloned.1.call-update
  8.8 0.5 all-gather.3.cloned.1.call-update
  9.7 5.2 %collective-permute-start.2 = (bf16[528,512]{1,0:T(8,128)(2,1)S(1)}, bf16[528,512]{1,0:T(8,128)(2,1)S(1)}, u32[]{:S(2)}, u32[]{:S(2)}) collective-permute-start(bf16[528,512]{1,0:T(8,128)(2,1)S(1)} %pad_maximum_fusion.p0), channel_id=1, source_target_pairs={{0,24},{8,0},{16,8},{24,16},{1,25},{9,1},{17,9},{25,17},{2,26},{10... | collective-permute-start | bytes 1622024 | tf_op jit(solution)/shard_map/ppermute | solution.py:205
  14.9 2.4 %collective-permute-start.1 = (bf16[528,512]{1,0:T(8,128)(2,1)S(1)}, bf16[528,512]{1,0:T(8,128)(2,1)S(1)}, u32[]{:S(2)}, u32[]{:S(2)}) collective-permute-start(bf16[528,512]{1,0:T(8,128)(2,1)S(1)} %pad_maximum_fusion.p0), channel_id=1, source_target_pairs={{0,16},{8,24},{16,0},{24,8},{1,17},{9,25},{17,1},{25,9},{2,18},{10... | collective-permute-start | bytes 1622024 | tf_op jit(solution)/shard_map/ppermute | solution.py:205
  17.3 2.5 %collective-permute-start = (bf16[528,512]{1,0:T(8,128)(2,1)S(1)}, bf16[528,512]{1,0:T(8,128)(2,1)S(1)}, u32[]{:S(2)}, u32[]{:S(2)}) collective-permute-start(bf16[528,512]{1,0:T(8,128)(2,1)S(1)} %pad_maximum_fusion.p0), channel_id=1, source_target_pairs={{0,8},{8,16},{16,24},{24,0},{1,9},{9,17},{17,25},{25,1},{2,10},{10... | collective-permute-start | bytes 1622024 | tf_op jit(solution)/shard_map/ppermute | solution.py:205
  20.9 30.8 %all_to_all.35 = bf16[64,2,128]{2,1,0:T(2,128)(2,1)S(1)} all-to-all(bf16[64,2,128]{2,1,0:T(2,128)(2,1)S(1)} %reshape.87), channel_id=1, replica_groups=mesh['z'=16,'x'=4,'y'=4,'c'=2] {'z','x'}, dimensions={0} | all-to-all | bytes 65536 | tf_op jit(solution)/shard_map/all_to_all | solution.py:212
  51.7 11.8 %all_to_all.36 = bf16[8,16,128]{2,1,0:T(8,128)(2,1)S(1)} all-to-all(bf16[8,16,128]{2,1,0:T(8,128)(2,1)S(1)} %bitcast.32), channel_id=1, replica_groups=mesh['z'=16,'x'=4,'y'=4,'c'=2] {'y','c'}, dimensions={0} | all-to-all | bytes 65536 | tf_op jit(solution)/shard_map/all_to_all | solution.py:213
  63.5 4.0 %all-to-all-start = ((bf16[8,32,512]{2,1,0:T(8,128)(2,1)}), bf16[8,32,512]{2,1,0:T(8,128)(2,1)S(1)}, u32[]{:S(2)}, u32[]{:S(2)}) async-start(bf16[8,32,512]{2,1,0:T(8,128)(2,1)} %bitcast.2), calls=%async_computation.1 | async-start | bytes 524288 | tf_op jit(solution)/shard_map/all_to_all | solution.py:195
  68.0 6.1 %all-to-all-done.resid_ref = bf16[8,32,512]{2,1,0:T(8,128)(2,1)S(1)} async-done(((bf16[8,32,512]{2,1,0:T(8,128)(2,1)}), bf16[8,32,512]{2,1,0:T(8,128)(2,1)S(1)}, u32[]{:S(2)}, u32[]{:S(2)}) %all-to-all-start) | async-done | bytes 262176 | tf_op jit(solution)/shard_map/all_to_all | solution.py:195
  74.1 0.7 copy-done.5
  74.8 2.1 %high_copies.1 = bf16[32,32,512]{2,1,0:T(8,128)(2,1)} custom-call(bf16[32,4096]{1,0:T(8,128)(2,1)} %reduce-scatter.2.cloned.1.call-done.summed_ref, bf16[8,32,512]{2,1,0:T(8,128)(2,1)} %copy-done.5), custom_call_target="tpu_custom_call" | custom-call | tf_op jit(solution)/shard_map/high_copies/pallas_call | solution.py:39
  77.0 4.6 %all-to-all-start.3 = ((bf16[32,32,512]{2,1,0:T(8,128)(2,1)}), bf16[32,32,512]{2,1,0:T(8,128)(2,1)S(1)}, u32[]{:S(2)}, u32[]{:S(2)}) async-start(bf16[32,32,512]{2,1,0:T(8,128)(2,1)} %high_copies.1), calls=%async_computation.4 | async-start | bytes 2097152 | tf_op jit(solution)/shard_map/all_to_all | solution.py:221
  81.7 16.9 %all-to-all-done.3 = bf16[32,32,512]{2,1,0:T(8,128)(2,1)S(1)} async-done(((bf16[32,32,512]{2,1,0:T(8,128)(2,1)}), bf16[32,32,512]{2,1,0:T(8,128)(2,1)S(1)}, u32[]{:S(2)}, u32[]{:S(2)}) %all-to-all-start.3) | async-done | bytes 1048608 | tf_op jit(solution)/shard_map/all_to_all | solution.py:221
  98.6 1.9 copy-done.1
  100.5 2.7 %term_half.3 = bf16[4,1024,128]{2,1,0:T(8,128)(2,1)S(1)} custom-call(s32[2]{0:T(128)S(1)} %pad_add_fusion.1.half_ref, bf16[528,512]{1,0:T(8,128)(2,1)S(1)} %pad_maximum_fusion.p0, bf16[528,512]{1,0:T(8,128)(2,1)S(1)} %collective-permute-done.p1, bf16[528,512]{1,0:T(8,128)(2,1)S(1)} %collective-permute-done.1.p2, ...), custom_call_target="tpu_custom_call" | custom-call | flops 1610612736 | bytes 6291456 | tf_op jit(solution)/shard_map/term_half/pallas_call | solution.py:70
  103.2 2.0 %collective-permute-start.3 = (bf16[4,1024,128]{2,1,0:T(8,128)(2,1)S(1)}, bf16[4,1024,128]{2,1,0:T(8,128)(2,1)S(1)}, u32[]{:S(2)}, u32[]{:S(2)}) collective-permute-start(bf16[4,1024,128]{2,1,0:T(8,128)(2,1)S(1)} %term_half.3), channel_id=1, source_target_pairs={{0,1},{1,0},{2,3},{3,2},{4,5},{5,4},{6,7},{7,6},{8,9},{9,8},{10,11... | collective-permute-start | bytes 3145736 | tf_op jit(solution)/shard_map/ppermute | solution.py:225
  105.3 2.7 %term_half.2 = bf16[4,1024,128]{2,1,0:T(8,128)(2,1)S(1)} custom-call(s32[2]{0:T(128)S(1)} %pad_add_fusion.half_ref, bf16[528,512]{1,0:T(8,128)(2,1)S(1)} %pad_maximum_fusion.p0, bf16[528,512]{1,0:T(8,128)(2,1)S(1)} %collective-permute-done.p1, bf16[528,512]{1,0:T(8,128)(2,1)S(1)} %collective-permute-done.1.p2, ...), custom_call_target="tpu_custom_call" | custom-call | flops 1610612736 | bytes 6291456 | tf_op jit(solution)/shard_map/term_half/pallas_call | solution.py:70
  108.0 0.3 add_convert_fusion
  108.3 17.5 %all_to_all.37.terms_ref = bf16[4,1024,128]{2,1,0:T(8,128)(2,1)S(1)} all-to-all(bf16[4,1024,128]{2,1,0:T(8,128)(2,1)S(1)} %add_convert_fusion), channel_id=1, replica_groups=mesh['z'=16,'x'=4,'y'=4,'c'=2] {'y'}, dimensions={0} | all-to-all | bytes 2097152 | tf_op jit(solution)/shard_map/all_to_all | solution.py:228
  125.8 0.7 spread.1
  126.6 36.5 %all_to_all.38 = bf16[64,32,128]{2,1,0:T(8,128)(2,1)} all-to-all(bf16[64,32,128]{2,1,0:T(8,128)(2,1)S(1)} %spread.1), channel_id=1, replica_groups=mesh['z'=16,'x'=4,'y'=4,'c'=2] {'z','x'}, dimensions={0} | all-to-all | bytes 1048576 | tf_op jit(solution)/shard_map/all_to_all | solution.py:230
  163.1 7.8 %all-to-all-start.6 = ((bf16[8,256,128]{2,1,0:T(8,128)(2,1)}), bf16[8,256,128]{2,1,0:T(8,128)(2,1)S(1)}, u32[]{:S(2)}, u32[]{:S(2)}) async-start(bf16[8,256,128]{2,1,0:T(8,128)(2,1)} %bitcast.17), calls=%async_computation.7 | async-start | bytes 1048576 | tf_op jit(solution)/shard_map/all_to_all | solution.py:231
  171.0 9.4 %all-to-all-done.6 = bf16[8,256,128]{2,1,0:T(8,128)(2,1)S(1)} async-done(((bf16[8,256,128]{2,1,0:T(8,128)(2,1)}), bf16[8,256,128]{2,1,0:T(8,128)(2,1)S(1)}, u32[]{:S(2)}, u32[]{:S(2)}) %all-to-all-start.6) | async-done | bytes 524320 | tf_op jit(solution)/shard_map/all_to_all | solution.py:231
  180.5 6.8 %chain.1 = (f32[64,4096]{1,0:T(8,128)}, bf16[64,4096]{1,0:T(8,128)(2,1)}) custom-call(bf16[8,8,32,128]{3,2,1,0:T(8,128)(2,1)S(1)} %bitcast.29, bf16[64,128]{1,0:T(8,128)(2,1)S(1)} %copy.27.goal_ref, bf16[64,128]{1,0:T(8,128)(2,1)S(1)} %broadcast_in_dim.43.left_ref, bf16[4096,128]{1,0:T(8,128)(2,1)S(1)} %copy-done.3, bf16[128,4096]{1,0:T(8,128)(2,1)S(1)} %copy-done.4), custom_call_target="tpu_custom_call" | custom-call | tf_op jit(solution)/shard_map/chain/pallas_call | solution.py:172
  (52 shorter events, 2.0 us)
Async XLA Ops:
  8.0 12.1 %copy-start = (bf16[256,128]{1,0:T(8,128)(2,1)S(1)}, bf16[256,128]{1,0:T(8,128)(2,1)}, u32[]{:S(2)}) copy-start(bf16[256,128]{1,0:T(8,128)(2,1)} %param.18) | copy-start | bytes 196612
  8.0 1.4 copy-start.8
  8.0 1.6 copy-start.6
  8.0 1.6 copy-start.7
  8.0 11.8 %copy-start.10 = (s32[1,8]{1,0:T(1,128)S(1)}, s32[1,8]{1,0:T(1,128)}, u32[]{:S(2)}) copy-start(s32[1,8]{1,0:T(1,128)} %param.19) | copy-start | bytes 100
  8.1 12.3 %copy-start.9 = (s32[256]{0:T(256)S(1)}, s32[256]{0:T(256)}, u32[]{:S(2)}) copy-start(s32[256]{0:T(256)} %param.20) | copy-start | bytes 3076
  8.1 66.0 %reduce-scatter.2.cloned.1.call-start = ((), (), s32[]{:S(2)}) async-start(), calls=%async_computation.8 | async-start | bytes 2359296 | tf_op jit(solution)/shard_map/reduce_scatter | solution.py:194
  8.8 89.8 %all-gather.3.cloned.1.call-start = ((), (), s32[]{:S(2)}) async-start(), calls=%async_computation.9 | async-start | bytes 3342336 | tf_op jit(solution)/shard_map/all_gather | solution.py:193
  9.7 67.2 %collective-permute-start.2 = (bf16[528,512]{1,0:T(8,128)(2,1)S(1)}, bf16[528,512]{1,0:T(8,128)(2,1)S(1)}, u32[]{:S(2)}, u32[]{:S(2)}) collective-permute-start(bf16[528,512]{1,0:T(8,128)(2,1)S(1)} %pad_maximum_fusion.p0), channel_id=1, source_target_pairs={{0,24},{8,0},{16,8},{24,16},{1,25},{9,1},{17,9},{25,17},{2,26},{10... | collective-permute-start | bytes 1622024 | tf_op jit(solution)/shard_map/ppermute | solution.py:205
  14.9 62.0 %collective-permute-start.1 = (bf16[528,512]{1,0:T(8,128)(2,1)S(1)}, bf16[528,512]{1,0:T(8,128)(2,1)S(1)}, u32[]{:S(2)}, u32[]{:S(2)}) collective-permute-start(bf16[528,512]{1,0:T(8,128)(2,1)S(1)} %pad_maximum_fusion.p0), channel_id=1, source_target_pairs={{0,16},{8,24},{16,0},{24,8},{1,17},{9,25},{17,1},{25,9},{2,18},{10... | collective-permute-start | bytes 1622024 | tf_op jit(solution)/shard_map/ppermute | solution.py:205
  17.3 59.5 %collective-permute-start = (bf16[528,512]{1,0:T(8,128)(2,1)S(1)}, bf16[528,512]{1,0:T(8,128)(2,1)S(1)}, u32[]{:S(2)}, u32[]{:S(2)}) collective-permute-start(bf16[528,512]{1,0:T(8,128)(2,1)S(1)} %pad_maximum_fusion.p0), channel_id=1, source_target_pairs={{0,8},{8,16},{16,24},{24,0},{1,9},{9,17},{17,25},{25,1},{2,10},{10... | collective-permute-start | bytes 1622024 | tf_op jit(solution)/shard_map/ppermute | solution.py:205
  63.5 10.6 %all-to-all-start = ((bf16[8,32,512]{2,1,0:T(8,128)(2,1)}), bf16[8,32,512]{2,1,0:T(8,128)(2,1)S(1)}, u32[]{:S(2)}, u32[]{:S(2)}) async-start(bf16[8,32,512]{2,1,0:T(8,128)(2,1)} %bitcast.2), calls=%async_computation.1 | async-start | bytes 524288 | tf_op jit(solution)/shard_map/all_to_all | solution.py:195
  74.1 0.7 copy-start.5
  77.0 21.6 %all-to-all-start.3 = ((bf16[32,32,512]{2,1,0:T(8,128)(2,1)}), bf16[32,32,512]{2,1,0:T(8,128)(2,1)S(1)}, u32[]{:S(2)}, u32[]{:S(2)}) async-start(bf16[32,32,512]{2,1,0:T(8,128)(2,1)} %high_copies.1), calls=%async_computation.4 | async-start | bytes 2097152 | tf_op jit(solution)/shard_map/all_to_all | solution.py:221
  98.6 1.9 copy-start.1
  100.5 4.8 %copy-start.2 = (bf16[48,64,512]{2,1,0:T(8,128)(2,1)S(1)}, bf16[48,64,512]{2,1,0:T(8,128)(2,1)}, u32[]{:S(2)}) copy-start(bf16[48,64,512]{2,1,0:T(8,128)(2,1)} %all-gather.3.cloned.1.call-done) | copy-start | bytes 9437188
  103.2 4.8 %collective-permute-start.3 = (bf16[4,1024,128]{2,1,0:T(8,128)(2,1)S(1)}, bf16[4,1024,128]{2,1,0:T(8,128)(2,1)S(1)}, u32[]{:S(2)}, u32[]{:S(2)}) collective-permute-start(bf16[4,1024,128]{2,1,0:T(8,128)(2,1)S(1)} %term_half.3), channel_id=1, source_target_pairs={{0,1},{1,0},{2,3},{3,2},{4,5},{5,4},{6,7},{7,6},{8,9},{9,8},{10,11... | collective-permute-start | bytes 3145736 | tf_op jit(solution)/shard_map/ppermute | solution.py:225
  126.6 53.9 %copy-start.3 = (bf16[4096,128]{1,0:T(8,128)(2,1)S(1)}, bf16[4096,128]{1,0:T(8,128)(2,1)}, u32[]{:S(2)}) copy-start(bf16[4096,128]{1,0:T(8,128)(2,1)} %in_ref.1) | copy-start | bytes 3145732
  126.6 53.9 %copy-start.4 = (bf16[128,4096]{1,0:T(8,128)(2,1)S(1)}, bf16[128,4096]{1,0:T(8,128)(2,1)}, u32[]{:S(2)}) copy-start(bf16[128,4096]{1,0:T(8,128)(2,1)} %out_ref.1) | copy-start | bytes 3145732
  163.1 17.3 %all-to-all-start.6 = ((bf16[8,256,128]{2,1,0:T(8,128)(2,1)}), bf16[8,256,128]{2,1,0:T(8,128)(2,1)S(1)}, u32[]{:S(2)}, u32[]{:S(2)}) async-start(bf16[8,256,128]{2,1,0:T(8,128)(2,1)} %bitcast.17), calls=%async_computation.7 | async-start | bytes 1048576 | tf_op jit(solution)/shard_map/all_to_all | solution.py:231
Sparse Core Ops, SparseCore 0:
  11.7 45.4 reduce-scatter.1
Sparse Core Ops, SparseCore 1:
  11.3 73.4 all-gather.2

commit v7 on v6

--- a/solution.py
+++ b/solution.py
@@ -209,16 +209,19 @@
     side = jnp.concatenate([side, jnp.broadcast_to(left[:, None], (256, 16))], axis=1)
     slot = jnp.arange(512, dtype=jnp.int32)[:, None] == (shard * 8 + rank)[None, :]
     side = jnp.dot(slot.astype(BF), side, preferred_element_type=F32).astype(BF)
+    resid, side = lax.optimization_barrier((resid, side))
     side = lax.all_to_all(side.reshape(64, 2, 128), dp, split_axis=0, concat_axis=0, tiled=True)
+
+    high = high_copies(summed, resid)
+    high, side, *pairs = lax.optimization_barrier((high, side, *pairs))
+    high = lax.all_to_all(high, ("x",) + tensor, split_axis=0, concat_axis=0, tiled=True)
+    high, side = lax.optimization_barrier((high, side))
     side = lax.all_to_all(
         side.reshape(8, 16, 128), tensor, split_axis=0, concat_axis=0, tiled=True
     ).reshape(8, 64, 32)
     goal = jnp.swapaxes(side[:, :, :16], 0, 1).reshape(64, 128)
     left = jnp.broadcast_to(side[0, :, 16:17], (64, 128))
-
-    high = high_copies(summed, resid)
-    high, goal, left, *pairs = lax.optimization_barrier((high, goal, left, *pairs))
-    high = lax.all_to_all(high, ("x",) + tensor, split_axis=0, concat_axis=0, tiled=True)
+    high, goal, left = lax.optimization_barrier((high, goal, left))
     high = high.reshape(4, 256, 512)
 
     other = term_half(jnp.stack([1 - core, along]).astype(jnp.int32), pairs, high, rows)

time: 195 us -> 198 us (1.015)
  blocking collectives: 96.7 us -> 56.1 us
  starting transfers between devices: 28.8 us -> 54.1 us
  waiting for transfers between devices: 33.6 us -> 49.6 us
    all_to_all x2 -> x0, blocking collectives: 42.7 us -> none  [the longest x1 30.8 us: per_device(): lax.all_to_all(side.reshape(64, 2, 128), dp, split_axis=0, concat_axis=0,...]
    all_to_all x0 -> x2, starting transfers between devices: none -> 19.4 us  [the longest x1 16 us: per_device(): lax.all_to_all(side.reshape(64, 2, 128), dp, split_axis=0, concat_axis=0,...]
    all_to_all x0 -> x2, waiting for transfers between devices: none -> 10.1 us  [the longest x1 5.41 us: per_device(): lax.all_to_all(side.reshape(64, 2, 128), dp, split_axis=0, concat_axis=0,...]
    reduce_scatter x1, waiting for transfers between devices: 0.01 us -> 5.83 us  [per_device(): summed = lax.psum_scatter(partials, tensor, scatter_dimension=0, tiled=True)]
    all_to_all x1, starting transfers between devices: 4.05 us -> 7.81 us  [per_device(): lax.all_to_all(resid.reshape(8, 32, 512), tensor, split_axis=0, concat_ax...]
    all_to_all x1, blocking collectives: 36.5 us -> 38.7 us  [per_device(): moved = lax.all_to_all(moved, dp, split_axis=0, concat_axis=0, tiled=True)]
  transfers between devices with their start and end apart: 9 -> 11, of which waited for: 3 -> 6; matrix products, arithmetic and copies ran while one was open for 1% -> 2% of each run, Pallas kernels for 2% -> 2%
where the time goes in v7:
time: 198 us; the launch traced here: 197 us
  blocking collectives  56.1 us (28%)
  starting transfers between devices  54.1 us (27%)
  waiting for transfers between devices  49.6 us (25%)
  between operations  15.8 us (8%)
  Pallas kernels  15 us (8%)
  local copies, waits for them, and re-layouts  5.07 us (3%)
    all_to_all x1, blocking collectives, per_device(): moved = lax.all_to_all(moved, dp, split_axis=0, concat_axis=0, tiled=True)  38.7 us
    all_to_all x1, blocking collectives, per_device(): terms = lax.all_to_all(terms, 'y', split_axis=0, concat_axis=0, tiled=True)  17.4 us
    all_to_all x1, waiting for transfers between devices, per_device(): lax.all_to_all(high, ('x',) + tensor, split_axis=0, concat_axis=0, tiled=...  17 us
    all_to_all x1, starting transfers between devices, per_device(): lax.all_to_all(side.reshape(64, 2, 128), dp, split_axis=0, concat_axis=0,...  16 us
    ppermute x3, starting transfers between devices, per_device(): lax.ppermute(pair, 'x', ring(4, shift))  10.2 us
    all_to_all x1, waiting for transfers between devices, per_device(): lax.all_to_all(moved.reshape(8, 256, 128), tensor, split_axis=0, concat_a...  9.41 us
    all_to_all x1, starting transfers between devices, per_device(): lax.all_to_all(moved.reshape(8, 256, 128), tensor, split_axis=0, concat_a...  7.85 us
    all_to_all x1, starting transfers between devices, per_device(): lax.all_to_all(resid.reshape(8, 32, 512), tensor, split_axis=0, concat_ax...  7.81 us
  transfers between devices with their start and end apart: 11, of which 6 were waited for; matrix products, arithmetic and copies ran while one was open for 2% of the time, Pallas kernels for 2%

profile of v7, /device:TPU:1, one launch (start us, length us, event | category | flops | bytes accessed | tf_op | source)
XLA Modules:
  0.0 196.9 jit_solution(4854010558126627967)
XLA Ops:
  9.7 5.2 %collective-permute-start.2 = (bf16[528,512]{1,0:T(8,128)(2,1)S(1)}, bf16[528,512]{1,0:T(8,128)(2,1)S(1)}, u32[]{:S(2)}, u32[]{:S(2)}) collective-permute-start(bf16[528,512]{1,0:T(8,128)(2,1)S(1)} %pad_maximum_fusion.p0), channel_id=1, source_target_pairs={{0,24},{8,0},{16,8},{24,16},{1,25},{9,1},{17,9},{25,17},{2,26},{10... | collective-permute-start | bytes 1622024 | tf_op jit(solution)/shard_map/ppermute | solution.py:205
  14.9 2.4 %collective-permute-start.1 = (bf16[528,512]{1,0:T(8,128)(2,1)S(1)}, bf16[528,512]{1,0:T(8,128)(2,1)S(1)}, u32[]{:S(2)}, u32[]{:S(2)}) collective-permute-start(bf16[528,512]{1,0:T(8,128)(2,1)S(1)} %pad_maximum_fusion.p0), channel_id=1, source_target_pairs={{0,16},{8,24},{16,0},{24,8},{1,17},{9,25},{17,1},{25,9},{2,18},{10... | collective-permute-start | bytes 1622024 | tf_op jit(solution)/shard_map/ppermute | solution.py:205
  17.3 2.5 %collective-permute-start = (bf16[528,512]{1,0:T(8,128)(2,1)S(1)}, bf16[528,512]{1,0:T(8,128)(2,1)S(1)}, u32[]{:S(2)}, u32[]{:S(2)}) collective-permute-start(bf16[528,512]{1,0:T(8,128)(2,1)S(1)} %pad_maximum_fusion.p0), channel_id=1, source_target_pairs={{0,8},{8,16},{16,24},{24,0},{1,9},{9,17},{17,25},{25,1},{2,10},{10... | collective-permute-start | bytes 1622024 | tf_op jit(solution)/shard_map/ppermute | solution.py:205
  19.9 7.8 %all-to-all-start = ((bf16[8,32,512]{2,1,0:T(8,128)(2,1)}), bf16[8,32,512]{2,1,0:T(8,128)(2,1)S(1)}, u32[]{:S(2)}, u32[]{:S(2)}) async-start(bf16[8,32,512]{2,1,0:T(8,128)(2,1)} %bitcast.2), calls=%async_computation.1 | async-start | bytes 524288 | tf_op jit(solution)/shard_map/all_to_all | solution.py:195
  28.4 6.1 %all-to-all-done.resid_ref = bf16[8,32,512]{2,1,0:T(8,128)(2,1)S(1)} async-done(((bf16[8,32,512]{2,1,0:T(8,128)(2,1)}), bf16[8,32,512]{2,1,0:T(8,128)(2,1)S(1)}, u32[]{:S(2)}, u32[]{:S(2)}) %all-to-all-start) | async-done | bytes 262176 | tf_op jit(solution)/shard_map/all_to_all | solution.py:195
  35.4 16.0 %all-to-all-start.1 = ((bf16[64,2,128]{2,1,0:T(2,128)(2,1)}), bf16[64,2,128]{2,1,0:T(2,128)(2,1)}, u32[]{:S(2)}, u32[]{:S(2)}) async-start(bf16[64,2,128]{2,1,0:T(2,128)(2,1)} %reshape.87), calls=%async_computation.2 | async-start | bytes 65536 | tf_op jit(solution)/shard_map/all_to_all | solution.py:213
  51.4 5.8 %reduce-scatter.2.cloned.1.call-done.summed_ref = bf16[32,4096]{1,0:T(8,128)(2,1)} async-done(((bf16[256,4096]{1,0:T(8,128)(2,1)}), bf16[32,4096]{1,0:T(8,128)(2,1)}) %reduce-scatter.2.cloned.1.call-update) | async-done | bytes 262160 | tf_op jit(solution)/shard_map/reduce_scatter | solution.py:194
  57.2 2.1 %high_copies.1 = bf16[32,32,512]{2,1,0:T(8,128)(2,1)} custom-call(bf16[32,4096]{1,0:T(8,128)(2,1)} %reduce-scatter.2.cloned.1.call-done.summed_ref, bf16[8,32,512]{2,1,0:T(8,128)(2,1)} %copy-done.5), custom_call_target="tpu_custom_call" | custom-call | tf_op jit(solution)/shard_map/high_copies/pallas_call | solution.py:39
  59.3 5.4 %all-to-all-done.1 = bf16[64,2,128]{2,1,0:T(2,128)(2,1)} async-done(((bf16[64,2,128]{2,1,0:T(2,128)(2,1)}), bf16[64,2,128]{2,1,0:T(2,128)(2,1)}, u32[]{:S(2)}, u32[]{:S(2)}) %all-to-all-start.1) | async-done | bytes 32800 | tf_op jit(solution)/shard_map/all_to_all | solution.py:213
  64.7 6.2 %all-to-all-start.2 = ((bf16[32,32,512]{2,1,0:T(8,128)(2,1)}), bf16[32,32,512]{2,1,0:T(8,128)(2,1)S(1)}, u32[]{:S(2)}, u32[]{:S(2)}) async-start(bf16[32,32,512]{2,1,0:T(8,128)(2,1)} %high_copies.1), calls=%async_computation.3 | async-start | bytes 2097152 | tf_op jit(solution)/shard_map/all_to_all | solution.py:217
  70.9 17.0 %all-to-all-done.2 = bf16[32,32,512]{2,1,0:T(8,128)(2,1)S(1)} async-done(((bf16[32,32,512]{2,1,0:T(8,128)(2,1)}), bf16[32,32,512]{2,1,0:T(8,128)(2,1)S(1)}, u32[]{:S(2)}, u32[]{:S(2)}) %all-to-all-start.2) | async-done | bytes 1048608 | tf_op jit(solution)/shard_map/all_to_all | solution.py:217
  87.9 3.4 %all-to-all-start.3 = ((bf16[8,16,128]{2,1,0:T(8,128)(2,1)}), bf16[8,16,128]{2,1,0:T(8,128)(2,1)S(1)}, u32[]{:S(2)}, u32[]{:S(2)}) async-start(bf16[8,16,128]{2,1,0:T(8,128)(2,1)} %bitcast.10), calls=%async_computation.4 | async-start | bytes 65536 | tf_op jit(solution)/shard_map/all_to_all | solution.py:219
  91.3 4.7 %all-to-all-done.3 = bf16[8,16,128]{2,1,0:T(8,128)(2,1)S(1)} async-done(((bf16[8,16,128]{2,1,0:T(8,128)(2,1)}), bf16[8,16,128]{2,1,0:T(8,128)(2,1)S(1)}, u32[]{:S(2)}, u32[]{:S(2)}) %all-to-all-start.3) | async-done | bytes 32800 | tf_op jit(solution)/shard_map/all_to_all | solution.py:219
  96.8 1.0 copy.26
  98.1 1.9 copy-done.1
  100.0 2.7 %term_half.3 = bf16[4,1024,128]{2,1,0:T(8,128)(2,1)S(1)} custom-call(s32[2]{0:T(128)S(1)} %pad_add_fusion.1.half_ref, bf16[528,512]{1,0:T(8,128)(2,1)S(1)} %pad_maximum_fusion.p0, bf16[528,512]{1,0:T(8,128)(2,1)S(1)} %collective-permute-done.p1, bf16[528,512]{1,0:T(8,128)(2,1)S(1)} %collective-permute-done.1.p2, ...), custom_call_target="tpu_custom_call" | custom-call | flops 1610612736 | bytes 6291456 | tf_op jit(solution)/shard_map/term_half/pallas_call | solution.py:70
  102.7 2.6 %collective-permute-start.3 = (bf16[4,1024,128]{2,1,0:T(8,128)(2,1)S(1)}, bf16[4,1024,128]{2,1,0:T(8,128)(2,1)S(1)}, u32[]{:S(2)}, u32[]{:S(2)}) collective-permute-start(bf16[4,1024,128]{2,1,0:T(8,128)(2,1)S(1)} %term_half.3), channel_id=1, source_target_pairs={{0,1},{1,0},{2,3},{3,2},{4,5},{5,4},{6,7},{7,6},{8,9},{9,8},{10,11... | collective-permute-start | bytes 3145736 | tf_op jit(solution)/shard_map/ppermute | solution.py:228
  105.4 2.7 %term_half.2 = bf16[4,1024,128]{2,1,0:T(8,128)(2,1)S(1)} custom-call(s32[2]{0:T(128)S(1)} %pad_add_fusion.half_ref, bf16[528,512]{1,0:T(8,128)(2,1)S(1)} %pad_maximum_fusion.p0, bf16[528,512]{1,0:T(8,128)(2,1)S(1)} %collective-permute-done.p1, bf16[528,512]{1,0:T(8,128)(2,1)S(1)} %collective-permute-done.1.p2, ...), custom_call_target="tpu_custom_call" | custom-call | flops 1610612736 | bytes 6291456 | tf_op jit(solution)/shard_map/term_half/pallas_call | solution.py:70
  108.4 17.4 %all_to_all.35.terms_ref = bf16[4,1024,128]{2,1,0:T(8,128)(2,1)S(1)} all-to-all(bf16[4,1024,128]{2,1,0:T(8,128)(2,1)S(1)} %add_convert_fusion), channel_id=1, replica_groups=mesh['z'=16,'x'=4,'y'=4,'c'=2] {'y'}, dimensions={0} | all-to-all | bytes 2097152 | tf_op jit(solution)/shard_map/all_to_all | solution.py:231
  125.8 0.7 spread.1
  126.5 38.7 %all_to_all.36 = bf16[64,32,128]{2,1,0:T(8,128)(2,1)} all-to-all(bf16[64,32,128]{2,1,0:T(8,128)(2,1)S(1)} %spread.1), channel_id=1, replica_groups=mesh['z'=16,'x'=4,'y'=4,'c'=2] {'z','x'}, dimensions={0} | all-to-all | bytes 1048576 | tf_op jit(solution)/shard_map/all_to_all | solution.py:233
  165.3 7.9 %all-to-all-start.6 = ((bf16[8,256,128]{2,1,0:T(8,128)(2,1)}), bf16[8,256,128]{2,1,0:T(8,128)(2,1)S(1)}, u32[]{:S(2)}, u32[]{:S(2)}) async-start(bf16[8,256,128]{2,1,0:T(8,128)(2,1)} %bitcast.17), calls=%async_computation.7 | async-start | bytes 1048576 | tf_op jit(solution)/shard_map/all_to_all | solution.py:234
  173.2 9.4 %all-to-all-done.6 = bf16[8,256,128]{2,1,0:T(8,128)(2,1)S(1)} async-done(((bf16[8,256,128]{2,1,0:T(8,128)(2,1)}), bf16[8,256,128]{2,1,0:T(8,128)(2,1)S(1)}, u32[]{:S(2)}, u32[]{:S(2)}) %all-to-all-start.6) | async-done | bytes 524320 | tf_op jit(solution)/shard_map/all_to_all | solution.py:234
  182.6 6.8 %chain.1 = (f32[64,4096]{1,0:T(8,128)}, bf16[64,4096]{1,0:T(8,128)(2,1)}) custom-call(bf16[8,8,32,128]{3,2,1,0:T(8,128)(2,1)S(1)} %bitcast.29, bf16[64,128]{1,0:T(8,128)(2,1)S(1)} %copy.27.goal_ref, bf16[64,128]{1,0:T(8,128)(2,1)S(1)} %broadcast_in_dim.43.left_ref, bf16[4096,128]{1,0:T(8,128)(2,1)S(1)} %copy-done.3, bf16[128,4096]{1,0:T(8,128)(2,1)S(1)} %copy-done.4), custom_call_target="tpu_custom_call" | custom-call | tf_op jit(solution)/shard_map/chain/pallas_call | solution.py:172
  (54 shorter events, 4.7 us)
Async XLA Ops:
  8.0 20.0 %copy-start = (bf16[256,128]{1,0:T(8,128)(2,1)S(1)}, bf16[256,128]{1,0:T(8,128)(2,1)}, u32[]{:S(2)}) copy-start(bf16[256,128]{1,0:T(8,128)(2,1)} %param.18) | copy-start | bytes 196612
  8.0 1.4 copy-start.8
  8.0 1.6 copy-start.6
  8.0 1.6 copy-start.7
  8.0 19.6 %copy-start.10 = (s32[1,8]{1,0:T(1,128)S(1)}, s32[1,8]{1,0:T(1,128)}, u32[]{:S(2)}) copy-start(s32[1,8]{1,0:T(1,128)} %param.19) | copy-start | bytes 100
  8.1 19.9 %copy-start.9 = (s32[256]{0:T(256)S(1)}, s32[256]{0:T(256)}, u32[]{:S(2)}) copy-start(s32[256]{0:T(256)} %param.20) | copy-start | bytes 3076
  8.1 49.2 %reduce-scatter.2.cloned.1.call-start = ((), (), s32[]{:S(2)}) async-start(), calls=%async_computation.8 | async-start | bytes 2359296 | tf_op jit(solution)/shard_map/reduce_scatter | solution.py:194
  8.8 89.2 %all-gather.3.cloned.1.call-start = ((), (), s32[]{:S(2)}) async-start(), calls=%async_computation.9 | async-start | bytes 3342336 | tf_op jit(solution)/shard_map/all_gather | solution.py:193
  9.7 55.0 %collective-permute-start.2 = (bf16[528,512]{1,0:T(8,128)(2,1)S(1)}, bf16[528,512]{1,0:T(8,128)(2,1)S(1)}, u32[]{:S(2)}, u32[]{:S(2)}) collective-permute-start(bf16[528,512]{1,0:T(8,128)(2,1)S(1)} %pad_maximum_fusion.p0), channel_id=1, source_target_pairs={{0,24},{8,0},{16,8},{24,16},{1,25},{9,1},{17,9},{25,17},{2,26},{10... | collective-permute-start | bytes 1622024 | tf_op jit(solution)/shard_map/ppermute | solution.py:205
  14.9 49.8 %collective-permute-start.1 = (bf16[528,512]{1,0:T(8,128)(2,1)S(1)}, bf16[528,512]{1,0:T(8,128)(2,1)S(1)}, u32[]{:S(2)}, u32[]{:S(2)}) collective-permute-start(bf16[528,512]{1,0:T(8,128)(2,1)S(1)} %pad_maximum_fusion.p0), channel_id=1, source_target_pairs={{0,16},{8,24},{16,0},{24,8},{1,17},{9,25},{17,1},{25,9},{2,18},{10... | collective-permute-start | bytes 1622024 | tf_op jit(solution)/shard_map/ppermute | solution.py:205
  17.3 47.4 %collective-permute-start = (bf16[528,512]{1,0:T(8,128)(2,1)S(1)}, bf16[528,512]{1,0:T(8,128)(2,1)S(1)}, u32[]{:S(2)}, u32[]{:S(2)}) collective-permute-start(bf16[528,512]{1,0:T(8,128)(2,1)S(1)} %pad_maximum_fusion.p0), channel_id=1, source_target_pairs={{0,8},{8,16},{16,24},{24,0},{1,9},{9,17},{17,25},{25,1},{2,10},{10... | collective-permute-start | bytes 1622024 | tf_op jit(solution)/shard_map/ppermute | solution.py:205
  19.9 14.6 %all-to-all-start = ((bf16[8,32,512]{2,1,0:T(8,128)(2,1)}), bf16[8,32,512]{2,1,0:T(8,128)(2,1)S(1)}, u32[]{:S(2)}, u32[]{:S(2)}) async-start(bf16[8,32,512]{2,1,0:T(8,128)(2,1)} %bitcast.2), calls=%async_computation.1 | async-start | bytes 524288 | tf_op jit(solution)/shard_map/all_to_all | solution.py:195
  34.5 22.7 %copy-start.5 = (bf16[8,32,512]{2,1,0:T(8,128)(2,1)}, bf16[8,32,512]{2,1,0:T(8,128)(2,1)S(1)}, u32[]{:S(2)}) copy-start(bf16[8,32,512]{2,1,0:T(8,128)(2,1)S(1)} %all-to-all-done.resid_ref) | copy-start | bytes 786436
  35.4 29.4 %all-to-all-start.1 = ((bf16[64,2,128]{2,1,0:T(2,128)(2,1)}), bf16[64,2,128]{2,1,0:T(2,128)(2,1)}, u32[]{:S(2)}, u32[]{:S(2)}) async-start(bf16[64,2,128]{2,1,0:T(2,128)(2,1)} %reshape.87), calls=%async_computation.2 | async-start | bytes 65536 | tf_op jit(solution)/shard_map/all_to_all | solution.py:213
  64.7 23.2 %all-to-all-start.2 = ((bf16[32,32,512]{2,1,0:T(8,128)(2,1)}), bf16[32,32,512]{2,1,0:T(8,128)(2,1)S(1)}, u32[]{:S(2)}, u32[]{:S(2)}) async-start(bf16[32,32,512]{2,1,0:T(8,128)(2,1)} %high_copies.1), calls=%async_computation.3 | async-start | bytes 2097152 | tf_op jit(solution)/shard_map/all_to_all | solution.py:217
  87.9 8.1 %all-to-all-start.3 = ((bf16[8,16,128]{2,1,0:T(8,128)(2,1)}), bf16[8,16,128]{2,1,0:T(8,128)(2,1)S(1)}, u32[]{:S(2)}, u32[]{:S(2)}) async-start(bf16[8,16,128]{2,1,0:T(8,128)(2,1)} %bitcast.10), calls=%async_computation.4 | async-start | bytes 65536 | tf_op jit(solution)/shard_map/all_to_all | solution.py:219
  98.0 1.9 copy-start.1
  99.9 5.4 %copy-start.2 = (bf16[48,64,512]{2,1,0:T(8,128)(2,1)S(1)}, bf16[48,64,512]{2,1,0:T(8,128)(2,1)}, u32[]{:S(2)}) copy-start(bf16[48,64,512]{2,1,0:T(8,128)(2,1)} %all-gather.3.cloned.1.call-done) | copy-start | bytes 9437188
  102.7 5.4 %collective-permute-start.3 = (bf16[4,1024,128]{2,1,0:T(8,128)(2,1)S(1)}, bf16[4,1024,128]{2,1,0:T(8,128)(2,1)S(1)}, u32[]{:S(2)}, u32[]{:S(2)}) collective-permute-start(bf16[4,1024,128]{2,1,0:T(8,128)(2,1)S(1)} %term_half.3), channel_id=1, source_target_pairs={{0,1},{1,0},{2,3},{3,2},{4,5},{5,4},{6,7},{7,6},{8,9},{9,8},{10,11... | collective-permute-start | bytes 3145736 | tf_op jit(solution)/shard_map/ppermute | solution.py:228
  126.5 56.1 %copy-start.3 = (bf16[4096,128]{1,0:T(8,128)(2,1)S(1)}, bf16[4096,128]{1,0:T(8,128)(2,1)}, u32[]{:S(2)}) copy-start(bf16[4096,128]{1,0:T(8,128)(2,1)} %in_ref.1) | copy-start | bytes 3145732
  126.5 56.1 %copy-start.4 = (bf16[128,4096]{1,0:T(8,128)(2,1)S(1)}, bf16[128,4096]{1,0:T(8,128)(2,1)}, u32[]{:S(2)}) copy-start(bf16[128,4096]{1,0:T(8,128)(2,1)} %out_ref.1) | copy-start | bytes 3145732
  165.3 17.4 %all-to-all-start.6 = ((bf16[8,256,128]{2,1,0:T(8,128)(2,1)}), bf16[8,256,128]{2,1,0:T(8,128)(2,1)S(1)}, u32[]{:S(2)}, u32[]{:S(2)}) async-start(bf16[8,256,128]{2,1,0:T(8,128)(2,1)} %bitcast.17), calls=%async_computation.7 | async-start | bytes 1048576 | tf_op jit(solution)/shard_map/all_to_all | solution.py:234
Sparse Core Ops, SparseCore 0:
  11.7 45.4 reduce-scatter.1
Sparse Core Ops, SparseCore 1:
  11.3 73.5 all-gather.2

commit v8 on v7

--- a/solution.py
+++ b/solution.py
@@ -1,3 +1,5 @@
+import functools
+
 import jax
 import jax.numpy as jnp
 from jax import lax
@@ -45,49 +47,52 @@
     )(summed, resid)
 
 
-def term_kernel(half_ref, p0, p1, p2, p3, high_ref, rows_ref, out_ref, held, sems):
-    half = half_ref[0]
+FIRST, SECOND = (1, 3), (3, 1)
+
+
+def term_kernel(other, give, place_ref, p0, p1, p2, p3, high_ref, rows_ref, out_ref, held, sems):
+    half = 1 - place_ref[0] if other else place_ref[0]
+    first = 1 + 2 * half
+    y = place_ref[2]
+    blocks = (y ^ first, y ^ 2) if give else (y, y ^ first ^ 2)
     copies = [
-        pltpu.make_async_copy(rows_ref.at[i, :, half], held.at[i], sems.at[i]) for i in range(2)
+        pltpu.make_async_copy(rows_ref.at[block, half], held.at[i], sems.at[i])
+        for i, block in enumerate(blocks)
     ]
     for copy in copies:
         copy.start()
-    for i in range(2):
-        copies[i].wait()
-        weights = [held[i, :, :, piece].reshape(256, 512) for piece in range(3)]
-        for group, pair_ref in enumerate((p0, p1, p2, p3)):
-            total = dot(pair_ref[0:256], weights[0], NT)
-            total += dot(pair_ref[256:512], weights[1], NT)
-            total += dot(high_ref[lax.rem(half_ref[1] + (4 - group), 4)], weights[2], NT)
-            total = total.astype(BF)
-            for part in range(2):
-                out_ref[2 * i + part, group * 256 : (group + 1) * 256, :] = total[
-                    :, part * 128 : (part + 1) * 128
-                ]
-
-
-def term_half(half, pairs, high, rows):
-    return pl.pallas_call(
-        term_kernel,
+    for copy in copies:
+        copy.wait()
+    weights = [held[:, :, piece].reshape(256, 512) for piece in range(3)]
+    for group, pair_ref in enumerate((p0, p1, p2, p3)):
+        total = dot(pair_ref[0:256], weights[0], NT)
+        total += dot(pair_ref[256:512], weights[1], NT)
+        total += dot(high_ref[lax.rem(place_ref[1] + (4 - group), 4)], weights[2], NT)
+        total = total.astype(BF)
+        for i in range(2):
+            out_ref[i, group * 256 : (group + 1) * 256, :] = total[:, i * 128 : (i + 1) * 128]
+
+
+def term_half(other, give, place, pairs, high, rows):
+    return pl.pallas_call(
+        functools.partial(term_kernel, other, give),
         in_specs=[pl.BlockSpec(memory_space=pltpu.SMEM)] + [VMEM] * 5 + [HBM],
         out_specs=VMEM,
-        out_shape=jax.ShapeDtypeStruct((4, 1024, 128), BF),
+        out_shape=jax.ShapeDtypeStruct((2, 1024, 128), BF),
         scratch_shapes=[
-            pltpu.VMEM((2, 2, 2, 3, 64, 512), BF),
+            pltpu.VMEM((2, 2, 3, 64, 512), BF),
             pltpu.SemaphoreType.DMA((2,)),
         ],
         compiler_params=pltpu.CompilerParams(vmem_limit_bytes=40 * 1024 * 1024),
         cost_estimate=pl.CostEstimate(
-            flops=2 * 1024 * 1536 * 512, bytes_accessed=6 * 1024 * 1024, transcendentals=0
+            flops=2 * 1024 * 1536 * 256, bytes_accessed=5 * 1024 * 1024, transcendentals=0
         ),
         name="term_half",
-    )(half, *pairs, high, rows)
-
-
-def spread_kernel(terms_ref, p0, p1, p2, p3, out_ref):
-    total = terms_ref[0].astype(F32)
-    for part in range(1, 4):
-        total += terms_ref[part].astype(F32)
+    )(place, *pairs, high, rows)
+
+
+def spread_kernel(t0, t1, t2, t3, p0, p1, p2, p3, out_ref):
+    total = t0[0].astype(F32) + t1[0].astype(F32) + t2[0].astype(F32) + t3[...].astype(F32)
     joined = total.astype(BF)
     row = lax.broadcasted_iota(jnp.int32, (1024, 256), 0)
     for two in range(2):
@@ -106,12 +111,12 @@
 def spread(terms, pairs):
     return pl.pallas_call(
         spread_kernel,
-        in_specs=[VMEM] * 5,
+        in_specs=[VMEM] * 8,
         out_specs=VMEM,
         out_shape=jax.ShapeDtypeStruct((64, 32, 128), BF),
         compiler_params=pltpu.CompilerParams(vmem_limit_bytes=40 * 1024 * 1024),
         name="spread",
-    )(terms, *pairs)
+    )(*terms, *pairs)
 
 
 def source_rows(tile, x):
@@ -188,9 +193,9 @@
 ):
     tensor, dp, z = ("y", "c"), ("z", "x"), "z"
     me = lax.axis_index("y") * 2 + lax.axis_index("c")
-    core, along = lax.axis_index("c"), lax.axis_index("x")
-
-    rows = lax.all_gather(jnp.swapaxes(joining, 1, 2), z).reshape(2, 2, 2, 2, 3, 64, 512)
+    place = jnp.stack([lax.axis_index(axis) for axis in ("c", "x", "y")]).astype(jnp.int32)
+
+    rows = lax.all_gather(jnp.swapaxes(joining, 1, 2), z).reshape(4, 2, 2, 3, 64, 512)
     summed = lax.psum_scatter(partials, tensor, scatter_dimension=0, tiled=True)
     resid = lax.all_to_all(
         resid.reshape(8, 32, 512), tensor, split_axis=0, concat_axis=0, tiled=True
@@ -218,24 +223,36 @@
     high, side = lax.optimization_barrier((high, side))
     side = lax.all_to_all(
         side.reshape(8, 16, 128), tensor, split_axis=0, concat_axis=0, tiled=True
-    ).reshape(8, 64, 32)
+    )
+    high, side = lax.optimization_barrier((high, side))
+    side = side.reshape(8, 64, 32)
     goal = jnp.swapaxes(side[:, :, :16], 0, 1).reshape(64, 128)
     left = jnp.broadcast_to(side[0, :, 16:17], (64, 128))
-    high, goal, left = lax.optimization_barrier((high, goal, left))
     high = high.reshape(4, 256, 512)
 
-    other = term_half(jnp.stack([1 - core, along]).astype(jnp.int32), pairs, high, rows)
-    other = lax.ppermute(other, "c", ring(2, 1))
-    own = term_half(jnp.stack([core, along]).astype(jnp.int32), pairs, high, rows)
-    terms = (own.astype(F32) + other.astype(F32)).astype(BF)
-    terms = lax.all_to_all(terms, "y", split_axis=0, concat_axis=0, tiled=True)
-    moved = spread(terms, pairs)
+    def both(give, place):
+        other = term_half(True, give, place, pairs, high, rows)
+        return term_half(False, give, place, pairs, high, rows), lax.ppermute(other, "c", ring(2, 1))
+
+    own, other = both(True, place)
+    given = (own.astype(F32) + other.astype(F32)).astype(BF)
+    given, place = lax.optimization_barrier((given, place))
+    given = meet(given, FIRST)
+    own, other = both(False, place)
+    second = own[1].astype(F32) + other[1].astype(F32) + given[1].astype(F32)
+    second = meet(second.astype(BF), SECOND)
+    moved = spread((own, other, given, second), pairs)
     moved = lax.all_to_all(moved, dp, split_axis=0, concat_axis=0, tiled=True)
     moved = lax.all_to_all(
         moved.reshape(8, 256, 128), tensor, split_axis=0, concat_axis=0, tiled=True
     )
     grad, final = chain(moved.reshape(8, 8, 32, 128), goal, left, step_in, step_out)
     return (grad, final)
+
+
+def meet(part, steps):
+    pairs = [(2 * y + c, 2 * (y ^ steps[c]) + c) for y in range(4) for c in range(2)]
+    return lax.ppermute(part, ("y", "c"), pairs)
 
 
 def ring(size, shift):

time: 198 us -> 199 us (level)
  blocking collectives: 56.1 us -> 38 us
  waiting for transfers between devices: 49.6 us -> 61.1 us
  starting transfers between devices: 54.1 us -> 61.6 us
  Pallas kernels: 15 us -> 17.5 us
    all_to_all x1 -> x0, blocking collectives: 17.4 us -> none  [per_device(): terms = lax.all_to_all(terms, 'y', split_axis=0, concat_axis=0, tiled=True)]
    ppermute x1 -> x4, waiting for transfers between devices: 0.01 us -> 11.9 us  [the longest x2 11.9 us: meet(): return lax.ppermute(part, ('y', 'c'), pairs)]
    ppermute x1 -> x4, starting transfers between devices: 2.64 us -> 9.27 us  [the longest x2 4.7 us: meet(): return lax.ppermute(part, ('y', 'c'), pairs)]
    pallas_call x3 -> x5, Pallas kernels: 6.14 us -> 8.56 us  [the longest x4 7.82 us: term_half(): pl.pallas_call(functools.partial(term_kernel, other, give), in_specs=[pl....]
  transfers between devices with their start and end apart: 11 -> 14, of which waited for: 6 -> 8; matrix products, arithmetic and copies ran while one was open for 2% -> 1% of each run, Pallas kernels for 2% -> 3%
where the time goes in v8:
time: 199 us
  starting transfers between devices  61.6 us (31%)
  waiting for transfers between devices  61.1 us (31%)
  blocking collectives  38 us (19%)
  Pallas kernels  17.5 us (9%)
  between operations  15.8 us (8%)
  local copies, waits for them, and re-layouts  3.51 us (2%)
    all_to_all x1, blocking collectives, per_device(): moved = lax.all_to_all(moved, dp, split_axis=0, concat_axis=0, tiled=True)  38 us
    all_to_all x1, waiting for transfers between devices, per_device(): lax.all_to_all(high, ('x',) + tensor, split_axis=0, concat_axis=0, tiled=...  17 us
    all_to_all x1, starting transfers between devices, per_device(): lax.all_to_all(side.reshape(64, 2, 128), dp, split_axis=0, concat_axis=0,...  14.2 us
    ppermute x2, waiting for transfers between devices, meet(): return lax.ppermute(part, ('y', 'c'), pairs)  11.9 us
    ppermute x3, starting transfers between devices, per_device(): lax.ppermute(pair, 'x', ring(4, shift))  11.4 us
    all_to_all x1, starting transfers between devices, per_device(): lax.all_to_all(moved.reshape(8, 256, 128), tensor, split_axis=0, concat_a...  9.31 us
    all_to_all x1, waiting for transfers between devices, per_device(): lax.all_to_all(moved.reshape(8, 256, 128), tensor, split_axis=0, concat_a...  8.97 us
    pallas_call x4, Pallas kernels, term_half(): pl.pallas_call(functools.partial(term_kernel, other, give), in_specs=[pl....  7.82 us
  transfers between devices with their start and end apart: 14, of which 8 were waited for; matrix products, arithmetic and copies ran while one was open for 1% of the time, Pallas kernels for 3%

profile of v8, /device:TPU:1, one launch (start us, length us, event | category | flops | bytes accessed | tf_op | source)
XLA Modules:
  0.0 198.6 jit_solution(15035997612674032363)
XLA Ops:
  9.7 3.9 %collective-permute-start = (bf16[528,512]{1,0:T(8,128)(2,1)S(1)}, bf16[528,512]{1,0:T(8,128)(2,1)S(1)}, u32[]{:S(2)}, u32[]{:S(2)}) collective-permute-start(bf16[528,512]{1,0:T(8,128)(2,1)S(1)} %pad_maximum_fusion.p0), channel_id=1, source_target_pairs={{0,8},{8,16},{16,24},{24,0},{1,9},{9,17},{17,25},{25,1},{2,10},{10... | collective-permute-start | bytes 1622024 | tf_op jit(solution)/shard_map/ppermute | solution.py:210
  13.6 4.4 %collective-permute-start.1 = (bf16[528,512]{1,0:T(8,128)(2,1)S(1)}, bf16[528,512]{1,0:T(8,128)(2,1)S(1)}, u32[]{:S(2)}, u32[]{:S(2)}) collective-permute-start(bf16[528,512]{1,0:T(8,128)(2,1)S(1)} %pad_maximum_fusion.p0), channel_id=1, source_target_pairs={{0,16},{8,24},{16,0},{24,8},{1,17},{9,25},{17,1},{25,9},{2,18},{10... | collective-permute-start | bytes 1622024 | tf_op jit(solution)/shard_map/ppermute | solution.py:210
  18.0 3.1 %collective-permute-start.2 = (bf16[528,512]{1,0:T(8,128)(2,1)S(1)}, bf16[528,512]{1,0:T(8,128)(2,1)S(1)}, u32[]{:S(2)}, u32[]{:S(2)}) collective-permute-start(bf16[528,512]{1,0:T(8,128)(2,1)S(1)} %pad_maximum_fusion.p0), channel_id=1, source_target_pairs={{0,24},{8,0},{16,8},{24,16},{1,25},{9,1},{17,9},{25,17},{2,26},{10... | collective-permute-start | bytes 1622024 | tf_op jit(solution)/shard_map/ppermute | solution.py:210
  21.1 7.8 %all-to-all-start = ((bf16[8,32,512]{2,1,0:T(8,128)(2,1)}), bf16[8,32,512]{2,1,0:T(8,128)(2,1)S(1)}, u32[]{:S(2)}, u32[]{:S(2)}) async-start(bf16[8,32,512]{2,1,0:T(8,128)(2,1)} %bitcast.3), calls=%async_computation.1 | async-start | bytes 524288 | tf_op jit(solution)/shard_map/all_to_all | solution.py:200
  29.6 6.1 %all-to-all-done.resid_ref = bf16[8,32,512]{2,1,0:T(8,128)(2,1)S(1)} async-done(((bf16[8,32,512]{2,1,0:T(8,128)(2,1)}), bf16[8,32,512]{2,1,0:T(8,128)(2,1)S(1)}, u32[]{:S(2)}, u32[]{:S(2)}) %all-to-all-start) | async-done | bytes 262176 | tf_op jit(solution)/shard_map/all_to_all | solution.py:200
  36.6 14.2 %all-to-all-start.1 = ((bf16[64,2,128]{2,1,0:T(2,128)(2,1)}), bf16[64,2,128]{2,1,0:T(2,128)(2,1)}, u32[]{:S(2)}, u32[]{:S(2)}) async-start(bf16[64,2,128]{2,1,0:T(2,128)(2,1)} %reshape.93), calls=%async_computation.2 | async-start | bytes 65536 | tf_op jit(solution)/shard_map/all_to_all | solution.py:218
  50.8 6.5 %reduce-scatter.2.cloned.1.call-done.summed_ref = bf16[32,4096]{1,0:T(8,128)(2,1)} async-done(((bf16[256,4096]{1,0:T(8,128)(2,1)}), bf16[32,4096]{1,0:T(8,128)(2,1)}) %reduce-scatter.2.cloned.1.call-update) | async-done | bytes 262160 | tf_op jit(solution)/shard_map/reduce_scatter | solution.py:199
  57.3 2.1 %high_copies.1 = bf16[32,32,512]{2,1,0:T(8,128)(2,1)} custom-call(bf16[32,4096]{1,0:T(8,128)(2,1)} %reduce-scatter.2.cloned.1.call-done.summed_ref, bf16[8,32,512]{2,1,0:T(8,128)(2,1)} %copy-done.4), custom_call_target="tpu_custom_call" | custom-call | tf_op jit(solution)/shard_map/high_copies/pallas_call | solution.py:41
  59.4 4.9 %all-to-all-done.1 = bf16[64,2,128]{2,1,0:T(2,128)(2,1)} async-done(((bf16[64,2,128]{2,1,0:T(2,128)(2,1)}), bf16[64,2,128]{2,1,0:T(2,128)(2,1)}, u32[]{:S(2)}, u32[]{:S(2)}) %all-to-all-start.1) | async-done | bytes 32800 | tf_op jit(solution)/shard_map/all_to_all | solution.py:218
  64.2 6.1 %all-to-all-start.2 = ((bf16[32,32,512]{2,1,0:T(8,128)(2,1)}), bf16[32,32,512]{2,1,0:T(8,128)(2,1)S(1)}, u32[]{:S(2)}, u32[]{:S(2)}) async-start(bf16[32,32,512]{2,1,0:T(8,128)(2,1)} %high_copies.1), calls=%async_computation.3 | async-start | bytes 2097152 | tf_op jit(solution)/shard_map/all_to_all | solution.py:222
  70.4 17.0 %all-to-all-done.2 = bf16[32,32,512]{2,1,0:T(8,128)(2,1)S(1)} async-done(((bf16[32,32,512]{2,1,0:T(8,128)(2,1)}), bf16[32,32,512]{2,1,0:T(8,128)(2,1)S(1)}, u32[]{:S(2)}, u32[]{:S(2)}) %all-to-all-start.2) | async-done | bytes 1048608 | tf_op jit(solution)/shard_map/all_to_all | solution.py:222
  87.3 3.4 %all-to-all-start.3 = ((bf16[8,16,128]{2,1,0:T(8,128)(2,1)}), bf16[8,16,128]{2,1,0:T(8,128)(2,1)S(1)}, u32[]{:S(2)}, u32[]{:S(2)}) async-start(bf16[8,16,128]{2,1,0:T(8,128)(2,1)} %bitcast.11), calls=%async_computation.4 | async-start | bytes 65536 | tf_op jit(solution)/shard_map/all_to_all | solution.py:224
  90.8 4.7 %all-to-all-done.3 = bf16[8,16,128]{2,1,0:T(8,128)(2,1)S(1)} async-done(((bf16[8,16,128]{2,1,0:T(8,128)(2,1)}), bf16[8,16,128]{2,1,0:T(8,128)(2,1)S(1)}, u32[]{:S(2)}, u32[]{:S(2)}) %all-to-all-start.3) | async-done | bytes 32800 | tf_op jit(solution)/shard_map/all_to_all | solution.py:224
  97.4 2.0 term_half.5
  99.3 2.6 %collective-permute-start.3 = (bf16[2,1024,128]{2,1,0:T(8,128)(2,1)S(1)}, bf16[2,1024,128]{2,1,0:T(8,128)(2,1)S(1)}, u32[]{:S(2)}, u32[]{:S(2)}) collective-permute-start(bf16[2,1024,128]{2,1,0:T(8,128)(2,1)S(1)} %term_half.5), channel_id=1, source_target_pairs={{0,1},{1,0},{2,3},{3,2},{4,5},{5,4},{6,7},{7,6},{8,9},{9,8},{10,11... | collective-permute-start | bytes 1572872 | tf_op jit(solution)/shard_map/ppermute | solution.py:235
  102.0 2.0 term_half.4
  104.1 2.0 term_half.7
  108.0 2.8 %collective-permute-start.5 = (bf16[2,1024,128]{2,1,0:T(8,128)(2,1)S(1)}, bf16[2,1024,128]{2,1,0:T(8,128)(2,1)S(1)}, u32[]{:S(2)}, u32[]{:S(2)}) collective-permute-start(bf16[2,1024,128]{2,1,0:T(8,128)(2,1)S(1)} %add_convert_fusion), channel_id=1, source_target_pairs={{0,2},{1,7},{2,0},{3,5},{4,6},{5,3},{6,4},{7,1},{8,10},{9,15},{10,... | collective-permute-start | bytes 1572872 | tf_op jit(solution)/shard_map/ppermute | solution.py:255
  112.7 6.4 %collective-permute-done.5.t2 = bf16[2,1024,128]{2,1,0:T(8,128)(2,1)S(1)} collective-permute-done((bf16[2,1024,128]{2,1,0:T(8,128)(2,1)S(1)}, bf16[2,1024,128]{2,1,0:T(8,128)(2,1)S(1)}, u32[]{:S(2)}, u32[]{:S(2)}) %collective-permute-start.5) | collective-permute-done | bytes 524320 | tf_op jit(solution)/shard_map/ppermute | solution.py:255
  121.2 5.5 %collective-permute-done.6.t3 = bf16[1024,128]{1,0:T(8,128)(2,1)S(1)} collective-permute-done((bf16[1024,128]{1,0:T(8,128)(2,1)S(1)}, bf16[1024,128]{1,0:T(8,128)(2,1)S(1)}, u32[]{:S(2)}, u32[]{:S(2)}) %collective-permute-start.6) | collective-permute-done | bytes 262176 | tf_op jit(solution)/shard_map/ppermute | solution.py:255
  127.4 38.0 %all_to_all.30 = bf16[64,32,128]{2,1,0:T(8,128)(2,1)} all-to-all(bf16[64,32,128]{2,1,0:T(8,128)(2,1)S(1)} %spread.1), channel_id=1, replica_groups=mesh['z'=16,'x'=4,'y'=4,'c'=2] {'z','x'}, dimensions={0} | all-to-all | bytes 1048576 | tf_op jit(solution)/shard_map/all_to_all | solution.py:245
  165.4 9.3 %all-to-all-start.5 = ((bf16[8,256,128]{2,1,0:T(8,128)(2,1)}), bf16[8,256,128]{2,1,0:T(8,128)(2,1)S(1)}, u32[]{:S(2)}, u32[]{:S(2)}) async-start(bf16[8,256,128]{2,1,0:T(8,128)(2,1)} %bitcast.16), calls=%async_computation.6 | async-start | bytes 1048576 | tf_op jit(solution)/shard_map/all_to_all | solution.py:246
  175.3 9.0 %all-to-all-done.5 = bf16[8,256,128]{2,1,0:T(8,128)(2,1)S(1)} async-done(((bf16[8,256,128]{2,1,0:T(8,128)(2,1)}), bf16[8,256,128]{2,1,0:T(8,128)(2,1)S(1)}, u32[]{:S(2)}, u32[]{:S(2)}) %all-to-all-start.5) | async-done | bytes 524320 | tf_op jit(solution)/shard_map/all_to_all | solution.py:246
  184.3 6.8 %chain.1 = (f32[64,4096]{1,0:T(8,128)}, bf16[64,4096]{1,0:T(8,128)(2,1)}) custom-call(bf16[8,8,32,128]{3,2,1,0:T(8,128)(2,1)S(1)} %bitcast.35, bf16[64,128]{1,0:T(8,128)(2,1)S(1)} %copy.27.goal_ref, bf16[64,128]{1,0:T(8,128)(2,1)S(1)} %broadcast_in_dim.43.left_ref, bf16[4096,128]{1,0:T(8,128)(2,1)S(1)} %copy-done.2, bf16[128,4096]{1,0:T(8,128)(2,1)S(1)} %copy-done.3), custom_call_target="tpu_custom_call" | custom-call | tf_op jit(solution)/shard_map/chain/pallas_call | solution.py:177
  (59 shorter events, 12.4 us)
Async XLA Ops:
  8.0 21.2 %copy-start = (bf16[256,128]{1,0:T(8,128)(2,1)S(1)}, bf16[256,128]{1,0:T(8,128)(2,1)}, u32[]{:S(2)}) copy-start(bf16[256,128]{1,0:T(8,128)(2,1)} %param.18) | copy-start | bytes 196612
  8.0 1.4 copy-start.7
  8.0 1.6 copy-start.5
  8.0 1.6 copy-start.6
  8.0 49.3 %reduce-scatter.2.cloned.1.call-start = ((), (), s32[]{:S(2)}) async-start(), calls=%async_computation.7 | async-start | bytes 2359296 | tf_op jit(solution)/shard_map/reduce_scatter | solution.py:199
  8.8 20.1 %copy-start.9 = (s32[1,8]{1,0:T(1,128)S(1)}, s32[1,8]{1,0:T(1,128)}, u32[]{:S(2)}) copy-start(s32[1,8]{1,0:T(1,128)} %param.19) | copy-start | bytes 100
  8.8 20.4 %copy-start.8 = (s32[256]{0:T(256)S(1)}, s32[256]{0:T(256)}, u32[]{:S(2)}) copy-start(s32[256]{0:T(256)} %param.20) | copy-start | bytes 3076
  8.8 86.7 %all-gather.3.cloned.1.call-start = ((), (), s32[]{:S(2)}) async-start(), calls=%async_computation.8 | async-start | bytes 3342336 | tf_op jit(solution)/shard_map/all_gather | solution.py:198
  9.7 54.5 %collective-permute-start = (bf16[528,512]{1,0:T(8,128)(2,1)S(1)}, bf16[528,512]{1,0:T(8,128)(2,1)S(1)}, u32[]{:S(2)}, u32[]{:S(2)}) collective-permute-start(bf16[528,512]{1,0:T(8,128)(2,1)S(1)} %pad_maximum_fusion.p0), channel_id=1, source_target_pairs={{0,8},{8,16},{16,24},{24,0},{1,9},{9,17},{17,25},{25,1},{2,10},{10... | collective-permute-start | bytes 1622024 | tf_op jit(solution)/shard_map/ppermute | solution.py:210
  13.6 50.6 %collective-permute-start.1 = (bf16[528,512]{1,0:T(8,128)(2,1)S(1)}, bf16[528,512]{1,0:T(8,128)(2,1)S(1)}, u32[]{:S(2)}, u32[]{:S(2)}) collective-permute-start(bf16[528,512]{1,0:T(8,128)(2,1)S(1)} %pad_maximum_fusion.p0), channel_id=1, source_target_pairs={{0,16},{8,24},{16,0},{24,8},{1,17},{9,25},{17,1},{25,9},{2,18},{10... | collective-permute-start | bytes 1622024 | tf_op jit(solution)/shard_map/ppermute | solution.py:210
  18.0 46.2 %collective-permute-start.2 = (bf16[528,512]{1,0:T(8,128)(2,1)S(1)}, bf16[528,512]{1,0:T(8,128)(2,1)S(1)}, u32[]{:S(2)}, u32[]{:S(2)}) collective-permute-start(bf16[528,512]{1,0:T(8,128)(2,1)S(1)} %pad_maximum_fusion.p0), channel_id=1, source_target_pairs={{0,24},{8,0},{16,8},{24,16},{1,25},{9,1},{17,9},{25,17},{2,26},{10... | collective-permute-start | bytes 1622024 | tf_op jit(solution)/shard_map/ppermute | solution.py:210
  21.1 14.6 %all-to-all-start = ((bf16[8,32,512]{2,1,0:T(8,128)(2,1)}), bf16[8,32,512]{2,1,0:T(8,128)(2,1)S(1)}, u32[]{:S(2)}, u32[]{:S(2)}) async-start(bf16[8,32,512]{2,1,0:T(8,128)(2,1)} %bitcast.3), calls=%async_computation.1 | async-start | bytes 524288 | tf_op jit(solution)/shard_map/all_to_all | solution.py:200
  35.7 21.6 %copy-start.4 = (bf16[8,32,512]{2,1,0:T(8,128)(2,1)}, bf16[8,32,512]{2,1,0:T(8,128)(2,1)S(1)}, u32[]{:S(2)}) copy-start(bf16[8,32,512]{2,1,0:T(8,128)(2,1)S(1)} %all-to-all-done.resid_ref) | copy-start | bytes 786436
  36.6 27.7 %all-to-all-start.1 = ((bf16[64,2,128]{2,1,0:T(2,128)(2,1)}), bf16[64,2,128]{2,1,0:T(2,128)(2,1)}, u32[]{:S(2)}, u32[]{:S(2)}) async-start(bf16[64,2,128]{2,1,0:T(2,128)(2,1)} %reshape.93), calls=%async_computation.2 | async-start | bytes 65536 | tf_op jit(solution)/shard_map/all_to_all | solution.py:218
  64.2 23.1 %all-to-all-start.2 = ((bf16[32,32,512]{2,1,0:T(8,128)(2,1)}), bf16[32,32,512]{2,1,0:T(8,128)(2,1)S(1)}, u32[]{:S(2)}, u32[]{:S(2)}) async-start(bf16[32,32,512]{2,1,0:T(8,128)(2,1)} %high_copies.1), calls=%async_computation.3 | async-start | bytes 2097152 | tf_op jit(solution)/shard_map/all_to_all | solution.py:222
  87.3 8.1 %all-to-all-start.3 = ((bf16[8,16,128]{2,1,0:T(8,128)(2,1)}), bf16[8,16,128]{2,1,0:T(8,128)(2,1)S(1)}, u32[]{:S(2)}, u32[]{:S(2)}) async-start(bf16[8,16,128]{2,1,0:T(8,128)(2,1)} %bitcast.11), calls=%async_computation.4 | async-start | bytes 65536 | tf_op jit(solution)/shard_map/all_to_all | solution.py:224
  95.5 1.9 copy-start.1
  99.3 4.6 %collective-permute-start.3 = (bf16[2,1024,128]{2,1,0:T(8,128)(2,1)S(1)}, bf16[2,1024,128]{2,1,0:T(8,128)(2,1)S(1)}, u32[]{:S(2)}, u32[]{:S(2)}) collective-permute-start(bf16[2,1024,128]{2,1,0:T(8,128)(2,1)S(1)} %term_half.5), channel_id=1, source_target_pairs={{0,1},{1,0},{2,3},{3,2},{4,5},{5,4},{6,7},{7,6},{8,9},{9,8},{10,11... | collective-permute-start | bytes 1572872 | tf_op jit(solution)/shard_map/ppermute | solution.py:235
  106.1 6.7 %collective-permute-start.4 = (bf16[2,1024,128]{2,1,0:T(8,128)(2,1)S(1)}, bf16[2,1024,128]{2,1,0:T(8,128)(2,1)S(1)}, u32[]{:S(2)}, u32[]{:S(2)}) collective-permute-start(bf16[2,1024,128]{2,1,0:T(8,128)(2,1)S(1)} %term_half.7), channel_id=1, source_target_pairs={{0,1},{1,0},{2,3},{3,2},{4,5},{5,4},{6,7},{7,6},{8,9},{9,8},{10,11... | collective-permute-start | bytes 1572872 | tf_op jit(solution)/shard_map/ppermute | solution.py:235
  108.0 11.1 %collective-permute-start.5 = (bf16[2,1024,128]{2,1,0:T(8,128)(2,1)S(1)}, bf16[2,1024,128]{2,1,0:T(8,128)(2,1)S(1)}, u32[]{:S(2)}, u32[]{:S(2)}) collective-permute-start(bf16[2,1024,128]{2,1,0:T(8,128)(2,1)S(1)} %add_convert_fusion), channel_id=1, source_target_pairs={{0,2},{1,7},{2,0},{3,5},{4,6},{5,3},{6,4},{7,1},{8,10},{9,15},{10,... | collective-permute-start | bytes 1572872 | tf_op jit(solution)/shard_map/ppermute | solution.py:255
  119.2 7.4 %collective-permute-start.6 = (bf16[1024,128]{1,0:T(8,128)(2,1)S(1)}, bf16[1024,128]{1,0:T(8,128)(2,1)S(1)}, u32[]{:S(2)}, u32[]{:S(2)}) collective-permute-start(bf16[1024,128]{1,0:T(8,128)(2,1)S(1)} %fusion), channel_id=1, source_target_pairs={{0,6},{1,3},{2,4},{3,1},{4,2},{5,7},{6,0},{7,5},{8,14},{9,11},{10,... | collective-permute-start | bytes 786440 | tf_op jit(solution)/shard_map/ppermute | solution.py:255
  127.4 56.9 %copy-start.3 = (bf16[128,4096]{1,0:T(8,128)(2,1)S(1)}, bf16[128,4096]{1,0:T(8,128)(2,1)}, u32[]{:S(2)}) copy-start(bf16[128,4096]{1,0:T(8,128)(2,1)} %out_ref.1) | copy-start | bytes 3145732
  165.4 18.9 %copy-start.2 = (bf16[4096,128]{1,0:T(8,128)(2,1)S(1)}, bf16[4096,128]{1,0:T(8,128)(2,1)}, u32[]{:S(2)}) copy-start(bf16[4096,128]{1,0:T(8,128)(2,1)} %in_ref.1) | copy-start | bytes 3145732
  165.4 18.8 %all-to-all-start.5 = ((bf16[8,256,128]{2,1,0:T(8,128)(2,1)}), bf16[8,256,128]{2,1,0:T(8,128)(2,1)S(1)}, u32[]{:S(2)}, u32[]{:S(2)}) async-start(bf16[8,256,128]{2,1,0:T(8,128)(2,1)} %bitcast.16), calls=%async_computation.6 | async-start | bytes 1048576 | tf_op jit(solution)/shard_map/all_to_all | solution.py:246
Sparse Core Ops, SparseCore 0:
  11.7 45.5 reduce-scatter.1
Sparse Core Ops, SparseCore 1:
  11.3 73.5 all-gather.2

commit v9 on v7

--- a/solution.py
+++ b/solution.py
@@ -10,7 +10,6 @@
 NT = (((1,), (1,)), ((), ()))
 NN = (((1,), (0,)), ((), ()))
 VMEM = pl.BlockSpec(memory_space=pltpu.VMEM)
-HBM = pl.BlockSpec(memory_space=pltpu.HBM)
 
 
 def dot(a, b, dims=NN):
@@ -45,16 +44,10 @@
     )(summed, resid)
 
 
-def term_kernel(half_ref, p0, p1, p2, p3, high_ref, rows_ref, out_ref, held, sems):
+def term_kernel(half_ref, p0, p1, p2, p3, high_ref, rows_ref, out_ref):
     half = half_ref[0]
-    copies = [
-        pltpu.make_async_copy(rows_ref.at[i, :, half], held.at[i], sems.at[i]) for i in range(2)
-    ]
-    for copy in copies:
-        copy.start()
     for i in range(2):
-        copies[i].wait()
-        weights = [held[i, :, :, piece].reshape(256, 512) for piece in range(3)]
+        weights = [rows_ref[i, :, half, :, piece].reshape(256, 512) for piece in range(3)]
         for group, pair_ref in enumerate((p0, p1, p2, p3)):
             total = dot(pair_ref[0:256], weights[0], NT)
             total += dot(pair_ref[256:512], weights[1], NT)
@@ -69,13 +62,9 @@
 def term_half(half, pairs, high, rows):
     return pl.pallas_call(
         term_kernel,
-        in_specs=[pl.BlockSpec(memory_space=pltpu.SMEM)] + [VMEM] * 5 + [HBM],
+        in_specs=[pl.BlockSpec(memory_space=pltpu.SMEM)] + [VMEM] * 6,
         out_specs=VMEM,
         out_shape=jax.ShapeDtypeStruct((4, 1024, 128), BF),
-        scratch_shapes=[
-            pltpu.VMEM((2, 2, 2, 3, 64, 512), BF),
-            pltpu.SemaphoreType.DMA((2,)),
-        ],
         compiler_params=pltpu.CompilerParams(vmem_limit_bytes=40 * 1024 * 1024),
         cost_estimate=pl.CostEstimate(
             flops=2 * 1024 * 1536 * 512, bytes_accessed=6 * 1024 * 1024, transcendentals=0
@@ -192,9 +181,6 @@
 
     rows = lax.all_gather(jnp.swapaxes(joining, 1, 2), z).reshape(2, 2, 2, 2, 3, 64, 512)
     summed = lax.psum_scatter(partials, tensor, scatter_dimension=0, tiled=True)
-    resid = lax.all_to_all(
-        resid.reshape(8, 32, 512), tensor, split_axis=0, concat_axis=0, tiled=True
-    )
 
     shard = dest[:, 0]
     earlier = jnp.arange(256)[:, None] > jnp.arange(256)[None, :]
@@ -209,19 +195,23 @@
     side = jnp.concatenate([side, jnp.broadcast_to(left[:, None], (256, 16))], axis=1)
     slot = jnp.arange(512, dtype=jnp.int32)[:, None] == (shard * 8 + rank)[None, :]
     side = jnp.dot(slot.astype(BF), side, preferred_element_type=F32).astype(BF)
+    side = lax.all_to_all(side.reshape(64, 2, 128), dp, split_axis=0, concat_axis=0, tiled=True)
+
     resid, side = lax.optimization_barrier((resid, side))
-    side = lax.all_to_all(side.reshape(64, 2, 128), dp, split_axis=0, concat_axis=0, tiled=True)
-
+    resid = lax.all_to_all(
+        resid.reshape(8, 32, 512), tensor, split_axis=0, concat_axis=0, tiled=True
+    )
     high = high_copies(summed, resid)
     high, side, *pairs = lax.optimization_barrier((high, side, *pairs))
     high = lax.all_to_all(high, ("x",) + tensor, split_axis=0, concat_axis=0, tiled=True)
     high, side = lax.optimization_barrier((high, side))
     side = lax.all_to_all(
         side.reshape(8, 16, 128), tensor, split_axis=0, concat_axis=0, tiled=True
-    ).reshape(8, 64, 32)
+    )
+    high, side = lax.optimization_barrier((high, side))
+    side = side.reshape(8, 64, 32)
     goal = jnp.swapaxes(side[:, :, :16], 0, 1).reshape(64, 128)
     left = jnp.broadcast_to(side[0, :, 16:17], (64, 128))
-    high, goal, left = lax.optimization_barrier((high, goal, left))
     high = high.reshape(4, 256, 512)
 
     other = term_half(jnp.stack([1 - core, along]).astype(jnp.int32), pairs, high, rows)

time: 198 us -> 196 us (0.990)
  blocking collectives: 56.1 us -> 100 us
  starting transfers between devices: 54.1 us -> 28.7 us
  waiting for transfers between devices: 49.6 us -> 31.8 us
  local copies, waits for them, and re-layouts: 5.07 us -> 2.92 us
    all_to_all x0 -> x2, blocking collectives: none -> 44.6 us  [the longest x1 31 us: per_device(): lax.all_to_all(side.reshape(64, 2, 128), dp, split_axis=0, concat_axis=0,...]
    all_to_all x2 -> x0, starting transfers between devices: 23.8 us -> none  [the longest x1 16 us: per_device(): lax.all_to_all(side.reshape(64, 2, 128), dp, split_axis=0, concat_axis=0,...]
    all_to_all x2 -> x0, waiting for transfers between devices: 11.5 us -> none  [the longest x1 6.11 us: per_device(): lax.all_to_all(resid.reshape(8, 32, 512), tensor, split_axis=0, concat_ax...]
    reduce_scatter x1, waiting for transfers between devices: 5.83 us -> 0.01 us  [per_device(): summed = lax.psum_scatter(partials, tensor, scatter_dimension=0, tiled=True)]
  transfers between devices with their start and end apart: 11 -> 9, of which waited for: 6 -> 3; matrix products, arithmetic and copies ran while one was open for 2% -> 1% of each run, Pallas kernels for 2% -> 2%
where the time goes in v9:
time: 196 us; the launch traced here: 195 us
  blocking collectives  100 us (51%)
  waiting for transfers between devices  31.8 us (16%)
  starting transfers between devices  28.7 us (15%)
  between operations  15.8 us (8%)
  Pallas kernels  14.4 us (7%)
  local copies, waits for them, and re-layouts  2.92 us (1%)
    all_to_all x1, blocking collectives, per_device(): moved = lax.all_to_all(moved, dp, split_axis=0, concat_axis=0, tiled=True)  38.7 us
    all_to_all x1, blocking collectives, per_device(): lax.all_to_all(side.reshape(64, 2, 128), dp, split_axis=0, concat_axis=0,...  31 us
    all_to_all x1, blocking collectives, per_device(): terms = lax.all_to_all(terms, 'y', split_axis=0, concat_axis=0, tiled=True)  17.3 us
    all_to_all x1, waiting for transfers between devices, per_device(): lax.all_to_all(high, ('x',) + tensor, split_axis=0, concat_axis=0, tiled=...  17 us
    all_to_all x1, blocking collectives, per_device(): lax.all_to_all(resid.reshape(8, 32, 512), tensor, split_axis=0, concat_ax...  13.6 us
    ppermute x3, starting transfers between devices, per_device(): lax.ppermute(pair, 'x', ring(4, shift))  10.2 us
    all_to_all x1, waiting for transfers between devices, per_device(): lax.all_to_all(moved.reshape(8, 256, 128), tensor, split_axis=0, concat_a...  8.97 us
    all_to_all x1, starting transfers between devices, per_device(): lax.all_to_all(moved.reshape(8, 256, 128), tensor, split_axis=0, concat_a...  7.85 us
  transfers between devices with their start and end apart: 9, of which 3 were waited for; matrix products, arithmetic and copies ran while one was open for 1% of the time, Pallas kernels for 2%

profile of v9, /device:TPU:1, one launch (start us, length us, event | category | flops | bytes accessed | tf_op | source)
XLA Modules:
  0.0 195.3 jit_solution(12232366915354921273)
XLA Ops:
  8.1 0.7 reduce-scatter.2.cloned.1.call-update
  8.9 0.5 all-gather.3.cloned.1.call-update
  9.7 5.2 %collective-permute-start.2 = (bf16[528,512]{1,0:T(8,128)(2,1)S(1)}, bf16[528,512]{1,0:T(8,128)(2,1)S(1)}, u32[]{:S(2)}, u32[]{:S(2)}) collective-permute-start(bf16[528,512]{1,0:T(8,128)(2,1)S(1)} %pad_maximum_fusion.p0), channel_id=1, source_target_pairs={{0,24},{8,0},{16,8},{24,16},{1,25},{9,1},{17,9},{25,17},{2,26},{10... | collective-permute-start | bytes 1622024 | tf_op jit(solution)/shard_map/ppermute | solution.py:191
  14.9 2.4 %collective-permute-start.1 = (bf16[528,512]{1,0:T(8,128)(2,1)S(1)}, bf16[528,512]{1,0:T(8,128)(2,1)S(1)}, u32[]{:S(2)}, u32[]{:S(2)}) collective-permute-start(bf16[528,512]{1,0:T(8,128)(2,1)S(1)} %pad_maximum_fusion.p0), channel_id=1, source_target_pairs={{0,16},{8,24},{16,0},{24,8},{1,17},{9,25},{17,1},{25,9},{2,18},{10... | collective-permute-start | bytes 1622024 | tf_op jit(solution)/shard_map/ppermute | solution.py:191
  17.4 2.5 %collective-permute-start = (bf16[528,512]{1,0:T(8,128)(2,1)S(1)}, bf16[528,512]{1,0:T(8,128)(2,1)S(1)}, u32[]{:S(2)}, u32[]{:S(2)}) collective-permute-start(bf16[528,512]{1,0:T(8,128)(2,1)S(1)} %pad_maximum_fusion.p0), channel_id=1, source_target_pairs={{0,8},{8,16},{16,24},{24,0},{1,9},{9,17},{17,25},{25,1},{2,10},{10... | collective-permute-start | bytes 1622024 | tf_op jit(solution)/shard_map/ppermute | solution.py:191
  20.4 0.2 convolution_convert_fusion
  20.9 31.0 %all_to_all.35 = bf16[64,2,128]{2,1,0:T(2,128)(2,1)} all-to-all(bf16[64,2,128]{2,1,0:T(2,128)(2,1)S(1)} %reshape.86), channel_id=1, replica_groups=mesh['z'=16,'x'=4,'y'=4,'c'=2] {'z','x'}, dimensions={0} | all-to-all | bytes 65536 | tf_op jit(solution)/shard_map/all_to_all | solution.py:198
  51.9 13.6 %all_to_all.36.resid_ref = bf16[8,32,512]{2,1,0:T(8,128)(2,1)} all-to-all(bf16[8,32,512]{2,1,0:T(8,128)(2,1)S(1)} %bitcast.30), channel_id=1, replica_groups=mesh['z'=16,'x'=4,'y'=4,'c'=2] {'y','c'}, dimensions={0} | all-to-all | bytes 524288 | tf_op jit(solution)/shard_map/all_to_all | solution.py:201
  65.5 2.1 %high_copies.1 = bf16[32,32,512]{2,1,0:T(8,128)(2,1)} custom-call(bf16[32,4096]{1,0:T(8,128)(2,1)} %reduce-scatter.2.cloned.1.call-done.summed_ref, bf16[8,32,512]{2,1,0:T(8,128)(2,1)} %all_to_all.36.resid_ref), custom_call_target="tpu_custom_call" | custom-call | tf_op jit(solution)/shard_map/high_copies/pallas_call | solution.py:38
  67.5 4.6 %all-to-all-start.2 = ((bf16[32,32,512]{2,1,0:T(8,128)(2,1)}), bf16[32,32,512]{2,1,0:T(8,128)(2,1)S(1)}, u32[]{:S(2)}, u32[]{:S(2)}) async-start(bf16[32,32,512]{2,1,0:T(8,128)(2,1)} %high_copies.1), calls=%async_computation.3 | async-start | bytes 2097152 | tf_op jit(solution)/shard_map/all_to_all | solution.py:206
  72.2 17.0 %all-to-all-done.2 = bf16[32,32,512]{2,1,0:T(8,128)(2,1)S(1)} async-done(((bf16[32,32,512]{2,1,0:T(8,128)(2,1)}), bf16[32,32,512]{2,1,0:T(8,128)(2,1)S(1)}, u32[]{:S(2)}, u32[]{:S(2)}) %all-to-all-start.2) | async-done | bytes 1048608 | tf_op jit(solution)/shard_map/all_to_all | solution.py:206
  89.2 3.4 %all-to-all-start.3 = ((bf16[8,16,128]{2,1,0:T(8,128)(2,1)}), bf16[8,16,128]{2,1,0:T(8,128)(2,1)S(1)}, u32[]{:S(2)}, u32[]{:S(2)}) async-start(bf16[8,16,128]{2,1,0:T(8,128)(2,1)} %bitcast.10), calls=%async_computation.4 | async-start | bytes 65536 | tf_op jit(solution)/shard_map/all_to_all | solution.py:208
  92.6 4.7 %all-to-all-done.3 = bf16[8,16,128]{2,1,0:T(8,128)(2,1)S(1)} async-done(((bf16[8,16,128]{2,1,0:T(8,128)(2,1)}), bf16[8,16,128]{2,1,0:T(8,128)(2,1)S(1)}, u32[]{:S(2)}, u32[]{:S(2)}) %all-to-all-start.3) | async-done | bytes 32800 | tf_op jit(solution)/shard_map/all_to_all | solution.py:208
  97.3 1.9 copy-done.1
  99.2 2.4 %term_half.3 = bf16[4,1024,128]{2,1,0:T(8,128)(2,1)S(1)} custom-call(s32[2]{0:T(128)S(1)} %pad_add_fusion.1.half_ref, bf16[528,512]{1,0:T(8,128)(2,1)S(1)} %pad_maximum_fusion.p0, bf16[528,512]{1,0:T(8,128)(2,1)S(1)} %collective-permute-done.p1, bf16[528,512]{1,0:T(8,128)(2,1)S(1)} %collective-permute-done.1.p2, ...), custom_call_target="tpu_custom_call" | custom-call | flops 1610612736 | bytes 6291456 | tf_op jit(solution)/shard_map/term_half/pallas_call | solution.py:63
  101.6 2.6 %collective-permute-start.3 = (bf16[4,1024,128]{2,1,0:T(8,128)(2,1)S(1)}, bf16[4,1024,128]{2,1,0:T(8,128)(2,1)S(1)}, u32[]{:S(2)}, u32[]{:S(2)}) collective-permute-start(bf16[4,1024,128]{2,1,0:T(8,128)(2,1)S(1)} %term_half.3), channel_id=1, source_target_pairs={{0,1},{1,0},{2,3},{3,2},{4,5},{5,4},{6,7},{7,6},{8,9},{9,8},{10,11... | collective-permute-start | bytes 3145736 | tf_op jit(solution)/shard_map/ppermute | solution.py:218
  104.3 2.4 %term_half.2 = bf16[4,1024,128]{2,1,0:T(8,128)(2,1)S(1)} custom-call(s32[2]{0:T(128)S(1)} %pad_add_fusion.half_ref, bf16[528,512]{1,0:T(8,128)(2,1)S(1)} %pad_maximum_fusion.p0, bf16[528,512]{1,0:T(8,128)(2,1)S(1)} %collective-permute-done.p1, bf16[528,512]{1,0:T(8,128)(2,1)S(1)} %collective-permute-done.1.p2, ...), custom_call_target="tpu_custom_call" | custom-call | flops 1610612736 | bytes 6291456 | tf_op jit(solution)/shard_map/term_half/pallas_call | solution.py:63
  106.7 0.3 add_convert_fusion
  107.0 17.3 %all_to_all.37.terms_ref = bf16[4,1024,128]{2,1,0:T(8,128)(2,1)S(1)} all-to-all(bf16[4,1024,128]{2,1,0:T(8,128)(2,1)S(1)} %add_convert_fusion), channel_id=1, replica_groups=mesh['z'=16,'x'=4,'y'=4,'c'=2] {'y'}, dimensions={0} | all-to-all | bytes 2097152 | tf_op jit(solution)/shard_map/all_to_all | solution.py:221
  124.2 0.7 spread.1
  125.0 38.7 %all_to_all.38 = bf16[64,32,128]{2,1,0:T(8,128)(2,1)} all-to-all(bf16[64,32,128]{2,1,0:T(8,128)(2,1)S(1)} %spread.1), channel_id=1, replica_groups=mesh['z'=16,'x'=4,'y'=4,'c'=2] {'z','x'}, dimensions={0} | all-to-all | bytes 1048576 | tf_op jit(solution)/shard_map/all_to_all | solution.py:223
  163.6 7.8 %all-to-all-start.6 = ((bf16[8,256,128]{2,1,0:T(8,128)(2,1)}), bf16[8,256,128]{2,1,0:T(8,128)(2,1)S(1)}, u32[]{:S(2)}, u32[]{:S(2)}) async-start(bf16[8,256,128]{2,1,0:T(8,128)(2,1)} %bitcast.15), calls=%async_computation.7 | async-start | bytes 1048576 | tf_op jit(solution)/shard_map/all_to_all | solution.py:224
  172.0 9.0 %all-to-all-done.6 = bf16[8,256,128]{2,1,0:T(8,128)(2,1)S(1)} async-done(((bf16[8,256,128]{2,1,0:T(8,128)(2,1)}), bf16[8,256,128]{2,1,0:T(8,128)(2,1)S(1)}, u32[]{:S(2)}, u32[]{:S(2)}) %all-to-all-start.6) | async-done | bytes 524320 | tf_op jit(solution)/shard_map/all_to_all | solution.py:224
  181.1 6.8 %chain.1 = (f32[64,4096]{1,0:T(8,128)}, bf16[64,4096]{1,0:T(8,128)(2,1)}) custom-call(bf16[8,8,32,128]{3,2,1,0:T(8,128)(2,1)S(1)} %bitcast.29, bf16[64,128]{1,0:T(8,128)(2,1)S(1)} %copy.27.goal_ref, bf16[64,128]{1,0:T(8,128)(2,1)S(1)} %broadcast_in_dim.43.left_ref, bf16[4096,128]{1,0:T(8,128)(2,1)S(1)} %copy-done.3, bf16[128,4096]{1,0:T(8,128)(2,1)S(1)} %copy-done.4), custom_call_target="tpu_custom_call" | custom-call | tf_op jit(solution)/shard_map/chain/pallas_call | solution.py:161
  (52 shorter events, 1.8 us)
Async XLA Ops:
  8.0 12.1 %copy-start = (bf16[256,128]{1,0:T(8,128)(2,1)S(1)}, bf16[256,128]{1,0:T(8,128)(2,1)}, u32[]{:S(2)}) copy-start(bf16[256,128]{1,0:T(8,128)(2,1)} %param.18) | copy-start | bytes 196612
  8.0 1.4 copy-start.8
  8.0 1.6 copy-start.6
  8.0 1.6 copy-start.7
  8.0 11.8 %copy-start.10 = (s32[1,8]{1,0:T(1,128)S(1)}, s32[1,8]{1,0:T(1,128)}, u32[]{:S(2)}) copy-start(s32[1,8]{1,0:T(1,128)} %param.19) | copy-start | bytes 100
  8.1 12.3 %copy-start.9 = (s32[256]{0:T(256)S(1)}, s32[256]{0:T(256)}, u32[]{:S(2)}) copy-start(s32[256]{0:T(256)} %param.20) | copy-start | bytes 3076
  8.1 43.8 %copy-start.5 = (bf16[256,512]{1,0:T(8,128)(2,1)S(1)}, bf16[256,512]{1,0:T(8,128)(2,1)}, u32[]{:S(2)}) copy-start(bf16[256,512]{1,0:T(8,128)(2,1)} %param.12) | copy-start | bytes 786436
  8.1 57.4 %reduce-scatter.2.cloned.1.call-start = ((), (), s32[]{:S(2)}) async-start(), calls=%async_computation.8 | async-start | bytes 2359296 | tf_op jit(solution)/shard_map/reduce_scatter | solution.py:183
  8.8 88.5 %all-gather.3.cloned.1.call-start = ((), (), s32[]{:S(2)}) async-start(), calls=%async_computation.9 | async-start | bytes 3342336 | tf_op jit(solution)/shard_map/all_gather | solution.py:182
  9.7 57.8 %collective-permute-start.2 = (bf16[528,512]{1,0:T(8,128)(2,1)S(1)}, bf16[528,512]{1,0:T(8,128)(2,1)S(1)}, u32[]{:S(2)}, u32[]{:S(2)}) collective-permute-start(bf16[528,512]{1,0:T(8,128)(2,1)S(1)} %pad_maximum_fusion.p0), channel_id=1, source_target_pairs={{0,24},{8,0},{16,8},{24,16},{1,25},{9,1},{17,9},{25,17},{2,26},{10... | collective-permute-start | bytes 1622024 | tf_op jit(solution)/shard_map/ppermute | solution.py:191
  14.9 52.6 %collective-permute-start.1 = (bf16[528,512]{1,0:T(8,128)(2,1)S(1)}, bf16[528,512]{1,0:T(8,128)(2,1)S(1)}, u32[]{:S(2)}, u32[]{:S(2)}) collective-permute-start(bf16[528,512]{1,0:T(8,128)(2,1)S(1)} %pad_maximum_fusion.p0), channel_id=1, source_target_pairs={{0,16},{8,24},{16,0},{24,8},{1,17},{9,25},{17,1},{25,9},{2,18},{10... | collective-permute-start | bytes 1622024 | tf_op jit(solution)/shard_map/ppermute | solution.py:191
  17.4 50.2 %collective-permute-start = (bf16[528,512]{1,0:T(8,128)(2,1)S(1)}, bf16[528,512]{1,0:T(8,128)(2,1)S(1)}, u32[]{:S(2)}, u32[]{:S(2)}) collective-permute-start(bf16[528,512]{1,0:T(8,128)(2,1)S(1)} %pad_maximum_fusion.p0), channel_id=1, source_target_pairs={{0,8},{8,16},{16,24},{24,0},{1,9},{9,17},{17,25},{25,1},{2,10},{10... | collective-permute-start | bytes 1622024 | tf_op jit(solution)/shard_map/ppermute | solution.py:191
  67.5 21.6 %all-to-all-start.2 = ((bf16[32,32,512]{2,1,0:T(8,128)(2,1)}), bf16[32,32,512]{2,1,0:T(8,128)(2,1)S(1)}, u32[]{:S(2)}, u32[]{:S(2)}) async-start(bf16[32,32,512]{2,1,0:T(8,128)(2,1)} %high_copies.1), calls=%async_computation.3 | async-start | bytes 2097152 | tf_op jit(solution)/shard_map/all_to_all | solution.py:206
  89.2 8.1 %all-to-all-start.3 = ((bf16[8,16,128]{2,1,0:T(8,128)(2,1)}), bf16[8,16,128]{2,1,0:T(8,128)(2,1)S(1)}, u32[]{:S(2)}, u32[]{:S(2)}) async-start(bf16[8,16,128]{2,1,0:T(8,128)(2,1)} %bitcast.10), calls=%async_computation.4 | async-start | bytes 65536 | tf_op jit(solution)/shard_map/all_to_all | solution.py:208
  97.3 1.9 copy-start.1
  99.2 5.1 %copy-start.2 = (bf16[48,64,512]{2,1,0:T(8,128)(2,1)S(1)}, bf16[48,64,512]{2,1,0:T(8,128)(2,1)}, u32[]{:S(2)}) copy-start(bf16[48,64,512]{2,1,0:T(8,128)(2,1)} %all-gather.3.cloned.1.call-done) | copy-start | bytes 9437188
  101.6 5.1 %collective-permute-start.3 = (bf16[4,1024,128]{2,1,0:T(8,128)(2,1)S(1)}, bf16[4,1024,128]{2,1,0:T(8,128)(2,1)S(1)}, u32[]{:S(2)}, u32[]{:S(2)}) collective-permute-start(bf16[4,1024,128]{2,1,0:T(8,128)(2,1)S(1)} %term_half.3), channel_id=1, source_target_pairs={{0,1},{1,0},{2,3},{3,2},{4,5},{5,4},{6,7},{7,6},{8,9},{9,8},{10,11... | collective-permute-start | bytes 3145736 | tf_op jit(solution)/shard_map/ppermute | solution.py:218
  125.0 56.1 %copy-start.3 = (bf16[4096,128]{1,0:T(8,128)(2,1)S(1)}, bf16[4096,128]{1,0:T(8,128)(2,1)}, u32[]{:S(2)}) copy-start(bf16[4096,128]{1,0:T(8,128)(2,1)} %in_ref.1) | copy-start | bytes 3145732
  125.0 56.1 %copy-start.4 = (bf16[128,4096]{1,0:T(8,128)(2,1)S(1)}, bf16[128,4096]{1,0:T(8,128)(2,1)}, u32[]{:S(2)}) copy-start(bf16[128,4096]{1,0:T(8,128)(2,1)} %out_ref.1) | copy-start | bytes 3145732
  163.6 17.3 %all-to-all-start.6 = ((bf16[8,256,128]{2,1,0:T(8,128)(2,1)}), bf16[8,256,128]{2,1,0:T(8,128)(2,1)S(1)}, u32[]{:S(2)}, u32[]{:S(2)}) async-start(bf16[8,256,128]{2,1,0:T(8,128)(2,1)} %bitcast.15), calls=%async_computation.7 | async-start | bytes 1048576 | tf_op jit(solution)/shard_map/all_to_all | solution.py:224
Sparse Core Ops, SparseCore 0:
  11.7 45.4 reduce-scatter.1
Sparse Core Ops, SparseCore 1:
  11.4 73.7 all-gather.2

commit v10 on v9

--- a/solution.py
+++ b/solution.py
@@ -197,21 +197,15 @@
     side = jnp.dot(slot.astype(BF), side, preferred_element_type=F32).astype(BF)
     side = lax.all_to_all(side.reshape(64, 2, 128), dp, split_axis=0, concat_axis=0, tiled=True)
 
-    resid, side = lax.optimization_barrier((resid, side))
-    resid = lax.all_to_all(
-        resid.reshape(8, 32, 512), tensor, split_axis=0, concat_axis=0, tiled=True
-    )
-    high = high_copies(summed, resid)
-    high, side, *pairs = lax.optimization_barrier((high, side, *pairs))
-    high = lax.all_to_all(high, ("x",) + tensor, split_axis=0, concat_axis=0, tiled=True)
-    high, side = lax.optimization_barrier((high, side))
-    side = lax.all_to_all(
-        side.reshape(8, 16, 128), tensor, split_axis=0, concat_axis=0, tiled=True
-    )
-    high, side = lax.optimization_barrier((high, side))
-    side = side.reshape(8, 64, 32)
+    side = jnp.concatenate([resid.reshape(8, 32, 512), side.reshape(8, 4, 512)], axis=1)
+    side = lax.all_to_all(side, tensor, split_axis=0, concat_axis=0, tiled=True)
+    resid, side = side[:, :32], side[:, 32:].reshape(8, 64, 32)
     goal = jnp.swapaxes(side[:, :, :16], 0, 1).reshape(64, 128)
     left = jnp.broadcast_to(side[0, :, 16:17], (64, 128))
+
+    high = high_copies(summed, resid)
+    high, *pairs = lax.optimization_barrier((high, *pairs))
+    high = lax.all_to_all(high, ("x",) + tensor, split_axis=0, concat_axis=0, tiled=True)
     high = high.reshape(4, 256, 512)
 
     other = term_half(jnp.stack([1 - core, along]).astype(jnp.int32), pairs, high, rows)

time: 196 us -> 195 us (level)
  waiting for transfers between devices: 31.8 us -> 26.2 us
  blocking collectives: 100 us -> 104 us
  local copies, waits for them, and re-layouts: 2.92 us -> 5.25 us
    all_to_all x1 -> x0, waiting for transfers between devices: 4.66 us -> none  [per_device(): lax.all_to_all(side.reshape(8, 16, 128), tensor, split_axis=0, concat_axi...]
    all_to_all x1 -> x0, starting transfers between devices: 3.37 us -> none  [per_device(): lax.all_to_all(side.reshape(8, 16, 128), tensor, split_axis=0, concat_axi...]
  transfers between devices with their start and end apart: 9 -> 8, of which waited for: 3 -> 2; matrix products, arithmetic and copies ran while one was open for 1% -> 2% of each run, Pallas kernels for 2% -> 2%
where the time goes in v10:
time: 195 us; the launch traced here: 194 us
  blocking collectives  104 us (53%)
  starting transfers between devices  26.8 us (14%)
  waiting for transfers between devices  26.2 us (13%)
  between operations  15.8 us (8%)
  Pallas kernels  14.4 us (7%)
  local copies, waits for them, and re-layouts  5.25 us (3%)
    all_to_all x1, blocking collectives, per_device(): moved = lax.all_to_all(moved, dp, split_axis=0, concat_axis=0, tiled=True)  39.7 us
    all_to_all x1, blocking collectives, per_device(): lax.all_to_all(side.reshape(64, 2, 128), dp, split_axis=0, concat_axis=0,...  30.8 us
    all_to_all x1, blocking collectives, per_device(): terms = lax.all_to_all(terms, 'y', split_axis=0, concat_axis=0, tiled=True)  19.2 us
    all_to_all x1, waiting for transfers between devices, per_device(): lax.all_to_all(high, ('x',) + tensor, split_axis=0, concat_axis=0, tiled=...  16.9 us
    all_to_all x1, blocking collectives, per_device(): side = lax.all_to_all(side, tensor, split_axis=0, concat_axis=0, tiled=True)  14.6 us
    ppermute x3, starting transfers between devices, per_device(): lax.ppermute(pair, 'x', ring(4, shift))  10.2 us
    all_to_all x1, waiting for transfers between devices, per_device(): lax.all_to_all(moved.reshape(8, 256, 128), tensor, split_axis=0, concat_a...  8.1 us
    all_to_all x1, starting transfers between devices, per_device(): lax.all_to_all(moved.reshape(8, 256, 128), tensor, split_axis=0, concat_a...  7.88 us
  transfers between devices with their start and end apart: 8, of which 2 were waited for; matrix products, arithmetic and copies ran while one was open for 2% of the time, Pallas kernels for 2%

profile of v10, /device:TPU:1, one launch (start us, length us, event | category | flops | bytes accessed | tf_op | source)
XLA Modules:
  0.0 194.0 jit_solution(16916268652612579634)
XLA Ops:
  8.1 0.7 reduce-scatter.2.cloned.1.call-update
  8.9 0.5 all-gather.3.cloned.1.call-update
  9.7 5.2 %collective-permute-start.2 = (bf16[528,512]{1,0:T(8,128)(2,1)S(1)}, bf16[528,512]{1,0:T(8,128)(2,1)S(1)}, u32[]{:S(2)}, u32[]{:S(2)}) collective-permute-start(bf16[528,512]{1,0:T(8,128)(2,1)S(1)} %pad_maximum_fusion.p0), channel_id=1, source_target_pairs={{0,24},{8,0},{16,8},{24,16},{1,25},{9,1},{17,9},{25,17},{2,26},{10... | collective-permute-start | bytes 1622024 | tf_op jit(solution)/shard_map/ppermute | solution.py:191
  14.9 2.4 %collective-permute-start.1 = (bf16[528,512]{1,0:T(8,128)(2,1)S(1)}, bf16[528,512]{1,0:T(8,128)(2,1)S(1)}, u32[]{:S(2)}, u32[]{:S(2)}) collective-permute-start(bf16[528,512]{1,0:T(8,128)(2,1)S(1)} %pad_maximum_fusion.p0), channel_id=1, source_target_pairs={{0,16},{8,24},{16,0},{24,8},{1,17},{9,25},{17,1},{25,9},{2,18},{10... | collective-permute-start | bytes 1622024 | tf_op jit(solution)/shard_map/ppermute | solution.py:191
  17.4 2.5 %collective-permute-start = (bf16[528,512]{1,0:T(8,128)(2,1)S(1)}, bf16[528,512]{1,0:T(8,128)(2,1)S(1)}, u32[]{:S(2)}, u32[]{:S(2)}) collective-permute-start(bf16[528,512]{1,0:T(8,128)(2,1)S(1)} %pad_maximum_fusion.p0), channel_id=1, source_target_pairs={{0,8},{8,16},{16,24},{24,0},{1,9},{9,17},{17,25},{25,1},{2,10},{10... | collective-permute-start | bytes 1622024 | tf_op jit(solution)/shard_map/ppermute | solution.py:191
  20.9 30.8 %all_to_all.30 = bf16[64,2,128]{2,1,0:T(2,128)(2,1)S(1)} all-to-all(bf16[64,2,128]{2,1,0:T(2,128)(2,1)S(1)} %reshape.87), channel_id=1, replica_groups=mesh['z'=16,'x'=4,'y'=4,'c'=2] {'z','x'}, dimensions={0} | all-to-all | bytes 65536 | tf_op jit(solution)/shard_map/all_to_all | solution.py:198
  51.8 14.6 %all_to_all.31 = bf16[8,36,512]{2,1,0:T(8,128)(2,1)S(1)} all-to-all(bf16[8,36,512]{2,1,0:T(8,128)(2,1)S(1)} %pad_maximum_fusion.1), channel_id=1, replica_groups=mesh['z'=16,'x'=4,'y'=4,'c'=2] {'y','c'}, dimensions={0} | all-to-all | bytes 589824 | tf_op jit(solution)/shard_map/all_to_all | solution.py:201
  66.4 0.7 copy-done.5
  67.1 0.7 slice.16.resid_ref
  67.8 2.1 %high_copies.1 = bf16[32,32,512]{2,1,0:T(8,128)(2,1)} custom-call(bf16[32,4096]{1,0:T(8,128)(2,1)} %reduce-scatter.2.cloned.1.call-done.summed_ref, bf16[8,32,512]{2,1,0:T(8,128)(2,1)} %slice.16.resid_ref), custom_call_target="tpu_custom_call" | custom-call | tf_op jit(solution)/shard_map/high_copies/pallas_call | solution.py:38
  69.9 4.3 %all-to-all-start.2 = ((bf16[32,32,512]{2,1,0:T(8,128)(2,1)}), bf16[32,32,512]{2,1,0:T(8,128)(2,1)S(1)}, u32[]{:S(2)}, u32[]{:S(2)}) async-start(bf16[32,32,512]{2,1,0:T(8,128)(2,1)} %high_copies.1), calls=%async_computation.3 | async-start | bytes 2097152 | tf_op jit(solution)/shard_map/all_to_all | solution.py:208
  74.4 16.9 %all-to-all-done.2 = bf16[32,32,512]{2,1,0:T(8,128)(2,1)S(1)} async-done(((bf16[32,32,512]{2,1,0:T(8,128)(2,1)}), bf16[32,32,512]{2,1,0:T(8,128)(2,1)S(1)}, u32[]{:S(2)}, u32[]{:S(2)}) %all-to-all-start.2) | async-done | bytes 1048608 | tf_op jit(solution)/shard_map/all_to_all | solution.py:208
  91.3 1.9 copy-done.1
  93.2 2.4 %term_half.3 = bf16[4,1024,128]{2,1,0:T(8,128)(2,1)S(1)} custom-call(s32[2]{0:T(128)S(1)} %pad_add_fusion.1.half_ref, bf16[528,512]{1,0:T(8,128)(2,1)S(1)} %pad_maximum_fusion.p0, bf16[528,512]{1,0:T(8,128)(2,1)S(1)} %collective-permute-done.p1, bf16[528,512]{1,0:T(8,128)(2,1)S(1)} %collective-permute-done.1.p2, ...), custom_call_target="tpu_custom_call" | custom-call | flops 1610612736 | bytes 6291456 | tf_op jit(solution)/shard_map/term_half/pallas_call | solution.py:63
  95.6 4.4 %collective-permute-start.3 = (bf16[4,1024,128]{2,1,0:T(8,128)(2,1)S(1)}, bf16[4,1024,128]{2,1,0:T(8,128)(2,1)S(1)}, u32[]{:S(2)}, u32[]{:S(2)}) collective-permute-start(bf16[4,1024,128]{2,1,0:T(8,128)(2,1)S(1)} %term_half.3), channel_id=1, source_target_pairs={{0,1},{1,0},{2,3},{3,2},{4,5},{5,4},{6,7},{7,6},{8,9},{9,8},{10,11... | collective-permute-start | bytes 3145736 | tf_op jit(solution)/shard_map/ppermute | solution.py:212
  100.0 2.4 %term_half.2 = bf16[4,1024,128]{2,1,0:T(8,128)(2,1)S(1)} custom-call(s32[2]{0:T(128)S(1)} %pad_add_fusion.half_ref, bf16[528,512]{1,0:T(8,128)(2,1)S(1)} %pad_maximum_fusion.p0, bf16[528,512]{1,0:T(8,128)(2,1)S(1)} %collective-permute-done.p1, bf16[528,512]{1,0:T(8,128)(2,1)S(1)} %collective-permute-done.1.p2, ...), custom_call_target="tpu_custom_call" | custom-call | flops 1610612736 | bytes 6291456 | tf_op jit(solution)/shard_map/term_half/pallas_call | solution.py:63
  102.4 0.3 add_convert_fusion
  102.7 19.2 %all_to_all.32.terms_ref = bf16[4,1024,128]{2,1,0:T(8,128)(2,1)S(1)} all-to-all(bf16[4,1024,128]{2,1,0:T(8,128)(2,1)S(1)} %add_convert_fusion), channel_id=1, replica_groups=mesh['z'=16,'x'=4,'y'=4,'c'=2] {'y'}, dimensions={0} | all-to-all | bytes 2097152 | tf_op jit(solution)/shard_map/all_to_all | solution.py:215
  121.8 0.7 spread.1
  122.6 39.7 %all_to_all.33 = bf16[64,32,128]{2,1,0:T(8,128)(2,1)} all-to-all(bf16[64,32,128]{2,1,0:T(8,128)(2,1)S(1)} %spread.1), channel_id=1, replica_groups=mesh['z'=16,'x'=4,'y'=4,'c'=2] {'z','x'}, dimensions={0} | all-to-all | bytes 1048576 | tf_op jit(solution)/shard_map/all_to_all | solution.py:217
  162.3 7.9 %all-to-all-start.5 = ((bf16[8,256,128]{2,1,0:T(8,128)(2,1)}), bf16[8,256,128]{2,1,0:T(8,128)(2,1)S(1)}, u32[]{:S(2)}, u32[]{:S(2)}) async-start(bf16[8,256,128]{2,1,0:T(8,128)(2,1)} %bitcast.14), calls=%async_computation.6 | async-start | bytes 1048576 | tf_op jit(solution)/shard_map/all_to_all | solution.py:218
  170.1 0.8 slice.17
  171.5 8.1 %all-to-all-done.5 = bf16[8,256,128]{2,1,0:T(8,128)(2,1)S(1)} async-done(((bf16[8,256,128]{2,1,0:T(8,128)(2,1)}), bf16[8,256,128]{2,1,0:T(8,128)(2,1)S(1)}, u32[]{:S(2)}, u32[]{:S(2)}) %all-to-all-start.5) | async-done | bytes 524320 | tf_op jit(solution)/shard_map/all_to_all | solution.py:218
  179.7 6.8 %chain.1 = (f32[64,4096]{1,0:T(8,128)}, bf16[64,4096]{1,0:T(8,128)(2,1)}) custom-call(bf16[8,8,32,128]{3,2,1,0:T(8,128)(2,1)S(1)} %bitcast.28, bf16[64,128]{1,0:T(8,128)(2,1)S(1)} %copy.28.goal_ref, bf16[64,128]{1,0:T(8,128)(2,1)S(1)} %broadcast_in_dim.43.left_ref, bf16[4096,128]{1,0:T(8,128)(2,1)S(1)} %copy-done.3, bf16[128,4096]{1,0:T(8,128)(2,1)S(1)} %copy-done.4), custom_call_target="tpu_custom_call" | custom-call | tf_op jit(solution)/shard_map/chain/pallas_call | solution.py:161
  (56 shorter events, 2.1 us)
Async XLA Ops:
  8.0 12.1 %copy-start = (bf16[256,128]{1,0:T(8,128)(2,1)S(1)}, bf16[256,128]{1,0:T(8,128)(2,1)}, u32[]{:S(2)}) copy-start(bf16[256,128]{1,0:T(8,128)(2,1)} %param.18) | copy-start | bytes 196612
  8.0 1.4 copy-start.9
  8.0 1.6 copy-start.7
  8.0 1.6 copy-start.8
  8.0 11.8 %copy-start.11 = (s32[1,8]{1,0:T(1,128)S(1)}, s32[1,8]{1,0:T(1,128)}, u32[]{:S(2)}) copy-start(s32[1,8]{1,0:T(1,128)} %param.19) | copy-start | bytes 100
  8.1 12.3 %copy-start.10 = (s32[256]{0:T(256)S(1)}, s32[256]{0:T(256)}, u32[]{:S(2)}) copy-start(s32[256]{0:T(256)} %param.20) | copy-start | bytes 3076
  8.1 43.7 %copy-start.6 = (bf16[256,512]{1,0:T(8,128)(2,1)S(1)}, bf16[256,512]{1,0:T(8,128)(2,1)}, u32[]{:S(2)}) copy-start(bf16[256,512]{1,0:T(8,128)(2,1)} %param.12) | copy-start | bytes 786436
  8.1 59.8 %reduce-scatter.2.cloned.1.call-start = ((), (), s32[]{:S(2)}) async-start(), calls=%async_computation.7 | async-start | bytes 2359296 | tf_op jit(solution)/shard_map/reduce_scatter | solution.py:183
  8.8 82.5 %all-gather.3.cloned.1.call-start = ((), (), s32[]{:S(2)}) async-start(), calls=%async_computation.8 | async-start | bytes 3342336 | tf_op jit(solution)/shard_map/all_gather | solution.py:182
  9.7 60.2 %collective-permute-start.2 = (bf16[528,512]{1,0:T(8,128)(2,1)S(1)}, bf16[528,512]{1,0:T(8,128)(2,1)S(1)}, u32[]{:S(2)}, u32[]{:S(2)}) collective-permute-start(bf16[528,512]{1,0:T(8,128)(2,1)S(1)} %pad_maximum_fusion.p0), channel_id=1, source_target_pairs={{0,24},{8,0},{16,8},{24,16},{1,25},{9,1},{17,9},{25,17},{2,26},{10... | collective-permute-start | bytes 1622024 | tf_op jit(solution)/shard_map/ppermute | solution.py:191
  14.9 55.0 %collective-permute-start.1 = (bf16[528,512]{1,0:T(8,128)(2,1)S(1)}, bf16[528,512]{1,0:T(8,128)(2,1)S(1)}, u32[]{:S(2)}, u32[]{:S(2)}) collective-permute-start(bf16[528,512]{1,0:T(8,128)(2,1)S(1)} %pad_maximum_fusion.p0), channel_id=1, source_target_pairs={{0,16},{8,24},{16,0},{24,8},{1,17},{9,25},{17,1},{25,9},{2,18},{10... | collective-permute-start | bytes 1622024 | tf_op jit(solution)/shard_map/ppermute | solution.py:191
  17.4 52.6 %collective-permute-start = (bf16[528,512]{1,0:T(8,128)(2,1)S(1)}, bf16[528,512]{1,0:T(8,128)(2,1)S(1)}, u32[]{:S(2)}, u32[]{:S(2)}) collective-permute-start(bf16[528,512]{1,0:T(8,128)(2,1)S(1)} %pad_maximum_fusion.p0), channel_id=1, source_target_pairs={{0,8},{8,16},{16,24},{24,0},{1,9},{9,17},{17,25},{25,1},{2,10},{10... | collective-permute-start | bytes 1622024 | tf_op jit(solution)/shard_map/ppermute | solution.py:191
  66.4 0.7 copy-start.5
  69.9 21.3 %all-to-all-start.2 = ((bf16[32,32,512]{2,1,0:T(8,128)(2,1)}), bf16[32,32,512]{2,1,0:T(8,128)(2,1)S(1)}, u32[]{:S(2)}, u32[]{:S(2)}) async-start(bf16[32,32,512]{2,1,0:T(8,128)(2,1)} %high_copies.1), calls=%async_computation.3 | async-start | bytes 2097152 | tf_op jit(solution)/shard_map/all_to_all | solution.py:208
  91.3 1.9 copy-start.1
  93.2 6.8 %copy-start.2 = (bf16[48,64,512]{2,1,0:T(8,128)(2,1)S(1)}, bf16[48,64,512]{2,1,0:T(8,128)(2,1)}, u32[]{:S(2)}) copy-start(bf16[48,64,512]{2,1,0:T(8,128)(2,1)} %all-gather.3.cloned.1.call-done) | copy-start | bytes 9437188
  95.6 6.8 %collective-permute-start.3 = (bf16[4,1024,128]{2,1,0:T(8,128)(2,1)S(1)}, bf16[4,1024,128]{2,1,0:T(8,128)(2,1)S(1)}, u32[]{:S(2)}, u32[]{:S(2)}) collective-permute-start(bf16[4,1024,128]{2,1,0:T(8,128)(2,1)S(1)} %term_half.3), channel_id=1, source_target_pairs={{0,1},{1,0},{2,3},{3,2},{4,5},{5,4},{6,7},{7,6},{8,9},{9,8},{10,11... | collective-permute-start | bytes 3145736 | tf_op jit(solution)/shard_map/ppermute | solution.py:212
  122.6 57.1 %copy-start.3 = (bf16[4096,128]{1,0:T(8,128)(2,1)S(1)}, bf16[4096,128]{1,0:T(8,128)(2,1)}, u32[]{:S(2)}) copy-start(bf16[4096,128]{1,0:T(8,128)(2,1)} %in_ref.1) | copy-start | bytes 3145732
  122.6 57.1 %copy-start.4 = (bf16[128,4096]{1,0:T(8,128)(2,1)S(1)}, bf16[128,4096]{1,0:T(8,128)(2,1)}, u32[]{:S(2)}) copy-start(bf16[128,4096]{1,0:T(8,128)(2,1)} %out_ref.1) | copy-start | bytes 3145732
  162.3 17.4 %all-to-all-start.5 = ((bf16[8,256,128]{2,1,0:T(8,128)(2,1)}), bf16[8,256,128]{2,1,0:T(8,128)(2,1)S(1)}, u32[]{:S(2)}, u32[]{:S(2)}) async-start(bf16[8,256,128]{2,1,0:T(8,128)(2,1)} %bitcast.14), calls=%async_computation.6 | async-start | bytes 1048576 | tf_op jit(solution)/shard_map/all_to_all | solution.py:218
Sparse Core Ops, SparseCore 0:
  11.7 45.4 reduce-scatter.1
Sparse Core Ops, SparseCore 1:
  11.4 73.4 all-gather.2

commit v11 on v10

--- a/solution.py
+++ b/solution.py
@@ -130,7 +130,7 @@
     for step in range(3):
         state = states[step][...]
         inv = lax.rsqrt(jnp.sum(state * state, axis=-1, keepdims=True) * (1.0 / 4096) + 1e-06)
-        pre = dot((state * inv).astype(BF), in_ref[...])
+        pre = inv * dot(state.astype(BF), in_ref[...])
         active = (pre * jax.nn.sigmoid(pre)).astype(BF)
         invs.append(inv)
         pres.append(pre)
@@ -143,15 +143,13 @@
         inv, pre = invs[step], pres[step]
         live = jnp.where(left > step, pre - goal, 0.0)
         if step == 2:
-            dpre = live.astype(BF)
+            dpre = live
         else:
             dact = dot(grad_ref[...].astype(BF), out_ref[...], NT)
             sig = jax.nn.sigmoid(pre)
-            dpre = (dact * (sig + pre * sig * (1.0 - sig)) + live).astype(BF)
-        dnorm = dot(dpre, in_ref[...], NT)
-        state = states[step][...]
-        mean = jnp.sum(dnorm * state, axis=-1, keepdims=True) * (1.0 / 4096)
-        back = inv * dnorm - state * (inv * inv * inv * mean)
+            dpre = dact * (sig + pre * sig * (1.0 - sig)) + live
+        mean = jnp.sum(dpre * pre, axis=-1, keepdims=True) * (1.0 / 4096)
+        back = dot((inv * dpre).astype(BF), in_ref[...], NT) - states[step][...] * (inv * inv * mean)
         if step < 2:
             back = grad_ref[...] + back
         grad_ref[...] = back

time: 195 us -> 193 us (0.990)
  no operation moved by 1% of the time
where the time goes in v11:
time: 193 us; the launch traced here: 192 us
  blocking collectives  104 us (54%)
  starting transfers between devices  26.8 us (14%)
  waiting for transfers between devices  26.2 us (14%)
  between operations  15.8 us (8%)
  Pallas kernels  12.5 us (6%)
  local copies, waits for them, and re-layouts  5.25 us (3%)
    all_to_all x1, blocking collectives, per_device(): moved = lax.all_to_all(moved, dp, split_axis=0, concat_axis=0, tiled=True)  39.6 us
    all_to_all x1, blocking collectives, per_device(): lax.all_to_all(side.reshape(64, 2, 128), dp, split_axis=0, concat_axis=0,...  30.8 us
    all_to_all x1, blocking collectives, per_device(): terms = lax.all_to_all(terms, 'y', split_axis=0, concat_axis=0, tiled=True)  19.2 us
    all_to_all x1, waiting for transfers between devices, per_device(): lax.all_to_all(high, ('x',) + tensor, split_axis=0, concat_axis=0, tiled=...  16.9 us
    all_to_all x1, blocking collectives, per_device(): side = lax.all_to_all(side, tensor, split_axis=0, concat_axis=0, tiled=True)  14.6 us
    ppermute x3, starting transfers between devices, per_device(): lax.ppermute(pair, 'x', ring(4, shift))  10.2 us
    all_to_all x1, waiting for transfers between devices, per_device(): lax.all_to_all(moved.reshape(8, 256, 128), tensor, split_axis=0, concat_a...  8.1 us
    all_to_all x1, starting transfers between devices, per_device(): lax.all_to_all(moved.reshape(8, 256, 128), tensor, split_axis=0, concat_a...  7.88 us
  transfers between devices with their start and end apart: 8, of which 2 were waited for; matrix products, arithmetic and copies ran while one was open for 2% of the time, Pallas kernels for 2%

profile of v11, /device:TPU:1, one launch (start us, length us, event | category | flops | bytes accessed | tf_op | source)
XLA Modules:
  0.0 192.1 jit_solution(14979061342444418362)
XLA Ops:
  8.1 0.7 reduce-scatter.2.cloned.1.call-update
  8.9 0.5 all-gather.3.cloned.1.call-update
  9.7 5.2 %collective-permute-start.2 = (bf16[528,512]{1,0:T(8,128)(2,1)S(1)}, bf16[528,512]{1,0:T(8,128)(2,1)S(1)}, u32[]{:S(2)}, u32[]{:S(2)}) collective-permute-start(bf16[528,512]{1,0:T(8,128)(2,1)S(1)} %pad_maximum_fusion.p0), channel_id=1, source_target_pairs={{0,24},{8,0},{16,8},{24,16},{1,25},{9,1},{17,9},{25,17},{2,26},{10... | collective-permute-start | bytes 1622024 | tf_op jit(solution)/shard_map/ppermute | solution.py:189
  14.9 2.4 %collective-permute-start.1 = (bf16[528,512]{1,0:T(8,128)(2,1)S(1)}, bf16[528,512]{1,0:T(8,128)(2,1)S(1)}, u32[]{:S(2)}, u32[]{:S(2)}) collective-permute-start(bf16[528,512]{1,0:T(8,128)(2,1)S(1)} %pad_maximum_fusion.p0), channel_id=1, source_target_pairs={{0,16},{8,24},{16,0},{24,8},{1,17},{9,25},{17,1},{25,9},{2,18},{10... | collective-permute-start | bytes 1622024 | tf_op jit(solution)/shard_map/ppermute | solution.py:189
  17.4 2.5 %collective-permute-start = (bf16[528,512]{1,0:T(8,128)(2,1)S(1)}, bf16[528,512]{1,0:T(8,128)(2,1)S(1)}, u32[]{:S(2)}, u32[]{:S(2)}) collective-permute-start(bf16[528,512]{1,0:T(8,128)(2,1)S(1)} %pad_maximum_fusion.p0), channel_id=1, source_target_pairs={{0,8},{8,16},{16,24},{24,0},{1,9},{9,17},{17,25},{25,1},{2,10},{10... | collective-permute-start | bytes 1622024 | tf_op jit(solution)/shard_map/ppermute | solution.py:189
  20.9 30.8 %all_to_all.30 = bf16[64,2,128]{2,1,0:T(2,128)(2,1)S(1)} all-to-all(bf16[64,2,128]{2,1,0:T(2,128)(2,1)S(1)} %reshape.87), channel_id=1, replica_groups=mesh['z'=16,'x'=4,'y'=4,'c'=2] {'z','x'}, dimensions={0} | all-to-all | bytes 65536 | tf_op jit(solution)/shard_map/all_to_all | solution.py:196
  51.8 14.6 %all_to_all.31 = bf16[8,36,512]{2,1,0:T(8,128)(2,1)S(1)} all-to-all(bf16[8,36,512]{2,1,0:T(8,128)(2,1)S(1)} %pad_maximum_fusion.1), channel_id=1, replica_groups=mesh['z'=16,'x'=4,'y'=4,'c'=2] {'y','c'}, dimensions={0} | all-to-all | bytes 589824 | tf_op jit(solution)/shard_map/all_to_all | solution.py:199
  66.4 0.7 copy-done.5
  67.1 0.7 slice.16.resid_ref
  67.8 2.1 %high_copies.1 = bf16[32,32,512]{2,1,0:T(8,128)(2,1)} custom-call(bf16[32,4096]{1,0:T(8,128)(2,1)} %reduce-scatter.2.cloned.1.call-done.summed_ref, bf16[8,32,512]{2,1,0:T(8,128)(2,1)} %slice.16.resid_ref), custom_call_target="tpu_custom_call" | custom-call | tf_op jit(solution)/shard_map/high_copies/pallas_call | solution.py:38
  69.9 4.3 %all-to-all-start.2 = ((bf16[32,32,512]{2,1,0:T(8,128)(2,1)}), bf16[32,32,512]{2,1,0:T(8,128)(2,1)S(1)}, u32[]{:S(2)}, u32[]{:S(2)}) async-start(bf16[32,32,512]{2,1,0:T(8,128)(2,1)} %high_copies.1), calls=%async_computation.3 | async-start | bytes 2097152 | tf_op jit(solution)/shard_map/all_to_all | solution.py:206
  74.4 16.9 %all-to-all-done.2 = bf16[32,32,512]{2,1,0:T(8,128)(2,1)S(1)} async-done(((bf16[32,32,512]{2,1,0:T(8,128)(2,1)}), bf16[32,32,512]{2,1,0:T(8,128)(2,1)S(1)}, u32[]{:S(2)}, u32[]{:S(2)}) %all-to-all-start.2) | async-done | bytes 1048608 | tf_op jit(solution)/shard_map/all_to_all | solution.py:206
  91.3 1.9 copy-done.1
  93.2 2.4 %term_half.3 = bf16[4,1024,128]{2,1,0:T(8,128)(2,1)S(1)} custom-call(s32[2]{0:T(128)S(1)} %pad_add_fusion.1.half_ref, bf16[528,512]{1,0:T(8,128)(2,1)S(1)} %pad_maximum_fusion.p0, bf16[528,512]{1,0:T(8,128)(2,1)S(1)} %collective-permute-done.p1, bf16[528,512]{1,0:T(8,128)(2,1)S(1)} %collective-permute-done.1.p2, ...), custom_call_target="tpu_custom_call" | custom-call | flops 1610612736 | bytes 6291456 | tf_op jit(solution)/shard_map/term_half/pallas_call | solution.py:63
  95.5 4.4 %collective-permute-start.3 = (bf16[4,1024,128]{2,1,0:T(8,128)(2,1)S(1)}, bf16[4,1024,128]{2,1,0:T(8,128)(2,1)S(1)}, u32[]{:S(2)}, u32[]{:S(2)}) collective-permute-start(bf16[4,1024,128]{2,1,0:T(8,128)(2,1)S(1)} %term_half.3), channel_id=1, source_target_pairs={{0,1},{1,0},{2,3},{3,2},{4,5},{5,4},{6,7},{7,6},{8,9},{9,8},{10,11... | collective-permute-start | bytes 3145736 | tf_op jit(solution)/shard_map/ppermute | solution.py:210
  100.0 2.4 %term_half.2 = bf16[4,1024,128]{2,1,0:T(8,128)(2,1)S(1)} custom-call(s32[2]{0:T(128)S(1)} %pad_add_fusion.half_ref, bf16[528,512]{1,0:T(8,128)(2,1)S(1)} %pad_maximum_fusion.p0, bf16[528,512]{1,0:T(8,128)(2,1)S(1)} %collective-permute-done.p1, bf16[528,512]{1,0:T(8,128)(2,1)S(1)} %collective-permute-done.1.p2, ...), custom_call_target="tpu_custom_call" | custom-call | flops 1610612736 | bytes 6291456 | tf_op jit(solution)/shard_map/term_half/pallas_call | solution.py:63
  102.4 0.3 add_convert_fusion
  102.7 19.2 %all_to_all.32.terms_ref = bf16[4,1024,128]{2,1,0:T(8,128)(2,1)S(1)} all-to-all(bf16[4,1024,128]{2,1,0:T(8,128)(2,1)S(1)} %add_convert_fusion), channel_id=1, replica_groups=mesh['z'=16,'x'=4,'y'=4,'c'=2] {'y'}, dimensions={0} | all-to-all | bytes 2097152 | tf_op jit(solution)/shard_map/all_to_all | solution.py:213
  121.8 0.7 spread.1
  122.6 39.6 %all_to_all.33 = bf16[64,32,128]{2,1,0:T(8,128)(2,1)} all-to-all(bf16[64,32,128]{2,1,0:T(8,128)(2,1)S(1)} %spread.1), channel_id=1, replica_groups=mesh['z'=16,'x'=4,'y'=4,'c'=2] {'z','x'}, dimensions={0} | all-to-all | bytes 1048576 | tf_op jit(solution)/shard_map/all_to_all | solution.py:215
  162.3 7.9 %all-to-all-start.5 = ((bf16[8,256,128]{2,1,0:T(8,128)(2,1)}), bf16[8,256,128]{2,1,0:T(8,128)(2,1)S(1)}, u32[]{:S(2)}, u32[]{:S(2)}) async-start(bf16[8,256,128]{2,1,0:T(8,128)(2,1)} %bitcast.14), calls=%async_computation.6 | async-start | bytes 1048576 | tf_op jit(solution)/shard_map/all_to_all | solution.py:216
  170.1 0.8 slice.17
  171.5 8.1 %all-to-all-done.5 = bf16[8,256,128]{2,1,0:T(8,128)(2,1)S(1)} async-done(((bf16[8,256,128]{2,1,0:T(8,128)(2,1)}), bf16[8,256,128]{2,1,0:T(8,128)(2,1)S(1)}, u32[]{:S(2)}, u32[]{:S(2)}) %all-to-all-start.5) | async-done | bytes 524320 | tf_op jit(solution)/shard_map/all_to_all | solution.py:216
  179.7 4.9 %chain.1 = (f32[64,4096]{1,0:T(8,128)}, bf16[64,4096]{1,0:T(8,128)(2,1)}) custom-call(bf16[8,8,32,128]{3,2,1,0:T(8,128)(2,1)S(1)} %bitcast.28, bf16[64,128]{1,0:T(8,128)(2,1)S(1)} %copy.28.goal_ref, bf16[64,128]{1,0:T(8,128)(2,1)S(1)} %broadcast_in_dim.43.left_ref, bf16[4096,128]{1,0:T(8,128)(2,1)S(1)} %copy-done.3, bf16[128,4096]{1,0:T(8,128)(2,1)S(1)} %copy-done.4), custom_call_target="tpu_custom_call" | custom-call | tf_op jit(solution)/shard_map/chain/pallas_call | solution.py:159
  (56 shorter events, 2.1 us)
Async XLA Ops:
  8.0 12.1 %copy-start = (bf16[256,128]{1,0:T(8,128)(2,1)S(1)}, bf16[256,128]{1,0:T(8,128)(2,1)}, u32[]{:S(2)}) copy-start(bf16[256,128]{1,0:T(8,128)(2,1)} %param.18) | copy-start | bytes 196612
  8.0 1.4 copy-start.9
  8.0 1.6 copy-start.7
  8.0 1.6 copy-start.8
  8.0 11.8 %copy-start.11 = (s32[1,8]{1,0:T(1,128)S(1)}, s32[1,8]{1,0:T(1,128)}, u32[]{:S(2)}) copy-start(s32[1,8]{1,0:T(1,128)} %param.19) | copy-start | bytes 100
  8.1 12.3 %copy-start.10 = (s32[256]{0:T(256)S(1)}, s32[256]{0:T(256)}, u32[]{:S(2)}) copy-start(s32[256]{0:T(256)} %param.20) | copy-start | bytes 3076
  8.1 43.7 %copy-start.6 = (bf16[256,512]{1,0:T(8,128)(2,1)S(1)}, bf16[256,512]{1,0:T(8,128)(2,1)}, u32[]{:S(2)}) copy-start(bf16[256,512]{1,0:T(8,128)(2,1)} %param.12) | copy-start | bytes 786436
  8.1 59.8 %reduce-scatter.2.cloned.1.call-start = ((), (), s32[]{:S(2)}) async-start(), calls=%async_computation.7 | async-start | bytes 2359296 | tf_op jit(solution)/shard_map/reduce_scatter | solution.py:181
  8.8 82.5 %all-gather.3.cloned.1.call-start = ((), (), s32[]{:S(2)}) async-start(), calls=%async_computation.8 | async-start | bytes 3342336 | tf_op jit(solution)/shard_map/all_gather | solution.py:180
  9.7 60.2 %collective-permute-start.2 = (bf16[528,512]{1,0:T(8,128)(2,1)S(1)}, bf16[528,512]{1,0:T(8,128)(2,1)S(1)}, u32[]{:S(2)}, u32[]{:S(2)}) collective-permute-start(bf16[528,512]{1,0:T(8,128)(2,1)S(1)} %pad_maximum_fusion.p0), channel_id=1, source_target_pairs={{0,24},{8,0},{16,8},{24,16},{1,25},{9,1},{17,9},{25,17},{2,26},{10... | collective-permute-start | bytes 1622024 | tf_op jit(solution)/shard_map/ppermute | solution.py:189
  14.9 55.0 %collective-permute-start.1 = (bf16[528,512]{1,0:T(8,128)(2,1)S(1)}, bf16[528,512]{1,0:T(8,128)(2,1)S(1)}, u32[]{:S(2)}, u32[]{:S(2)}) collective-permute-start(bf16[528,512]{1,0:T(8,128)(2,1)S(1)} %pad_maximum_fusion.p0), channel_id=1, source_target_pairs={{0,16},{8,24},{16,0},{24,8},{1,17},{9,25},{17,1},{25,9},{2,18},{10... | collective-permute-start | bytes 1622024 | tf_op jit(solution)/shard_map/ppermute | solution.py:189
  17.4 52.6 %collective-permute-start = (bf16[528,512]{1,0:T(8,128)(2,1)S(1)}, bf16[528,512]{1,0:T(8,128)(2,1)S(1)}, u32[]{:S(2)}, u32[]{:S(2)}) collective-permute-start(bf16[528,512]{1,0:T(8,128)(2,1)S(1)} %pad_maximum_fusion.p0), channel_id=1, source_target_pairs={{0,8},{8,16},{16,24},{24,0},{1,9},{9,17},{17,25},{25,1},{2,10},{10... | collective-permute-start | bytes 1622024 | tf_op jit(solution)/shard_map/ppermute | solution.py:189
  66.4 0.7 copy-start.5
  69.9 21.3 %all-to-all-start.2 = ((bf16[32,32,512]{2,1,0:T(8,128)(2,1)}), bf16[32,32,512]{2,1,0:T(8,128)(2,1)S(1)}, u32[]{:S(2)}, u32[]{:S(2)}) async-start(bf16[32,32,512]{2,1,0:T(8,128)(2,1)} %high_copies.1), calls=%async_computation.3 | async-start | bytes 2097152 | tf_op jit(solution)/shard_map/all_to_all | solution.py:206
  91.3 1.9 copy-start.1
  93.2 6.8 %copy-start.2 = (bf16[48,64,512]{2,1,0:T(8,128)(2,1)S(1)}, bf16[48,64,512]{2,1,0:T(8,128)(2,1)}, u32[]{:S(2)}) copy-start(bf16[48,64,512]{2,1,0:T(8,128)(2,1)} %all-gather.3.cloned.1.call-done) | copy-start | bytes 9437188
  95.5 6.8 %collective-permute-start.3 = (bf16[4,1024,128]{2,1,0:T(8,128)(2,1)S(1)}, bf16[4,1024,128]{2,1,0:T(8,128)(2,1)S(1)}, u32[]{:S(2)}, u32[]{:S(2)}) collective-permute-start(bf16[4,1024,128]{2,1,0:T(8,128)(2,1)S(1)} %term_half.3), channel_id=1, source_target_pairs={{0,1},{1,0},{2,3},{3,2},{4,5},{5,4},{6,7},{7,6},{8,9},{9,8},{10,11... | collective-permute-start | bytes 3145736 | tf_op jit(solution)/shard_map/ppermute | solution.py:210
  122.6 57.1 %copy-start.3 = (bf16[4096,128]{1,0:T(8,128)(2,1)S(1)}, bf16[4096,128]{1,0:T(8,128)(2,1)}, u32[]{:S(2)}) copy-start(bf16[4096,128]{1,0:T(8,128)(2,1)} %in_ref.1) | copy-start | bytes 3145732
  122.6 57.1 %copy-start.4 = (bf16[128,4096]{1,0:T(8,128)(2,1)S(1)}, bf16[128,4096]{1,0:T(8,128)(2,1)}, u32[]{:S(2)}) copy-start(bf16[128,4096]{1,0:T(8,128)(2,1)} %out_ref.1) | copy-start | bytes 3145732
  162.3 17.4 %all-to-all-start.5 = ((bf16[8,256,128]{2,1,0:T(8,128)(2,1)}), bf16[8,256,128]{2,1,0:T(8,128)(2,1)S(1)}, u32[]{:S(2)}, u32[]{:S(2)}) async-start(bf16[8,256,128]{2,1,0:T(8,128)(2,1)} %bitcast.14), calls=%async_computation.6 | async-start | bytes 1048576 | tf_op jit(solution)/shard_map/all_to_all | solution.py:216
Sparse Core Ops, SparseCore 0:
  11.7 45.4 reduce-scatter.1
Sparse Core Ops, SparseCore 1:
  11.4 73.4 all-gather.2

commit v12 on v11

--- a/solution.py
+++ b/solution.py
@@ -83,8 +83,8 @@
         moved = None
         for odd, pair_ref in enumerate(((p0, p1), (p2, p3))[two]):
             group = 2 * two + odd
-            shard = pair_ref[512:513, 0:256].astype(jnp.int32)
-            rank = pair_ref[512:513, 256:512].astype(jnp.int32)
+            extra = pair_ref[512:528].astype(F32)[0:1].astype(jnp.int32)
+            shard, rank = extra[:, 0:256], extra[:, 256:512]
             slot = shard * 16 + (odd * 8 + rank)
             hot = jnp.where(row == slot, 1.0, 0.0).astype(BF)
             part = dot(hot, joined[group * 256 : (group + 1) * 256])

time: 193 us -> 193 us (level)
  no operation moved by 1% of the time
where the time goes in v12:
time: 193 us; the launch traced here: 192 us
  blocking collectives  104 us (54%)
  starting transfers between devices  26.8 us (14%)
  waiting for transfers between devices  26.2 us (14%)
  between operations  15.8 us (8%)
  Pallas kernels  12.5 us (6%)
  local copies, waits for them, and re-layouts  5.25 us (3%)
    all_to_all x1, blocking collectives, per_device(): moved = lax.all_to_all(moved, dp, split_axis=0, concat_axis=0, tiled=True)  39.6 us
    all_to_all x1, blocking collectives, per_device(): lax.all_to_all(side.reshape(64, 2, 128), dp, split_axis=0, concat_axis=0,...  30.8 us
    all_to_all x1, blocking collectives, per_device(): terms = lax.all_to_all(terms, 'y', split_axis=0, concat_axis=0, tiled=True)  19.2 us
    all_to_all x1, waiting for transfers between devices, per_device(): lax.all_to_all(high, ('x',) + tensor, split_axis=0, concat_axis=0, tiled=...  16.9 us
    all_to_all x1, blocking collectives, per_device(): side = lax.all_to_all(side, tensor, split_axis=0, concat_axis=0, tiled=True)  14.6 us
    ppermute x3, starting transfers between devices, per_device(): lax.ppermute(pair, 'x', ring(4, shift))  10.2 us
    all_to_all x1, waiting for transfers between devices, per_device(): lax.all_to_all(moved.reshape(8, 256, 128), tensor, split_axis=0, concat_a...  8.1 us
    all_to_all x1, starting transfers between devices, per_device(): lax.all_to_all(moved.reshape(8, 256, 128), tensor, split_axis=0, concat_a...  7.88 us
  transfers between devices with their start and end apart: 8, of which 2 were waited for; matrix products, arithmetic and copies ran while one was open for 2% of the time, Pallas kernels for 2%

profile of v12, /device:TPU:1, one launch (start us, length us, event | category | flops | bytes accessed | tf_op | source)
XLA Modules:
  0.0 192.1 jit_solution(3013078898665610926)
XLA Ops:
  8.1 0.7 reduce-scatter.2.cloned.1.call-update
  8.9 0.5 all-gather.3.cloned.1.call-update
  9.7 5.2 %collective-permute-start.2 = (bf16[528,512]{1,0:T(8,128)(2,1)S(1)}, bf16[528,512]{1,0:T(8,128)(2,1)S(1)}, u32[]{:S(2)}, u32[]{:S(2)}) collective-permute-start(bf16[528,512]{1,0:T(8,128)(2,1)S(1)} %pad_maximum_fusion.p0), channel_id=1, source_target_pairs={{0,24},{8,0},{16,8},{24,16},{1,25},{9,1},{17,9},{25,17},{2,26},{10... | collective-permute-start | bytes 1622024 | tf_op jit(solution)/shard_map/ppermute | solution.py:189
  14.9 2.4 %collective-permute-start.1 = (bf16[528,512]{1,0:T(8,128)(2,1)S(1)}, bf16[528,512]{1,0:T(8,128)(2,1)S(1)}, u32[]{:S(2)}, u32[]{:S(2)}) collective-permute-start(bf16[528,512]{1,0:T(8,128)(2,1)S(1)} %pad_maximum_fusion.p0), channel_id=1, source_target_pairs={{0,16},{8,24},{16,0},{24,8},{1,17},{9,25},{17,1},{25,9},{2,18},{10... | collective-permute-start | bytes 1622024 | tf_op jit(solution)/shard_map/ppermute | solution.py:189
  17.4 2.5 %collective-permute-start = (bf16[528,512]{1,0:T(8,128)(2,1)S(1)}, bf16[528,512]{1,0:T(8,128)(2,1)S(1)}, u32[]{:S(2)}, u32[]{:S(2)}) collective-permute-start(bf16[528,512]{1,0:T(8,128)(2,1)S(1)} %pad_maximum_fusion.p0), channel_id=1, source_target_pairs={{0,8},{8,16},{16,24},{24,0},{1,9},{9,17},{17,25},{25,1},{2,10},{10... | collective-permute-start | bytes 1622024 | tf_op jit(solution)/shard_map/ppermute | solution.py:189
  20.9 30.8 %all_to_all.30 = bf16[64,2,128]{2,1,0:T(2,128)(2,1)S(1)} all-to-all(bf16[64,2,128]{2,1,0:T(2,128)(2,1)S(1)} %reshape.87), channel_id=1, replica_groups=mesh['z'=16,'x'=4,'y'=4,'c'=2] {'z','x'}, dimensions={0} | all-to-all | bytes 65536 | tf_op jit(solution)/shard_map/all_to_all | solution.py:196
  51.8 14.6 %all_to_all.31 = bf16[8,36,512]{2,1,0:T(8,128)(2,1)S(1)} all-to-all(bf16[8,36,512]{2,1,0:T(8,128)(2,1)S(1)} %pad_maximum_fusion.1), channel_id=1, replica_groups=mesh['z'=16,'x'=4,'y'=4,'c'=2] {'y','c'}, dimensions={0} | all-to-all | bytes 589824 | tf_op jit(solution)/shard_map/all_to_all | solution.py:199
  66.4 0.7 copy-done.5
  67.1 0.7 slice.16.resid_ref
  67.8 2.1 %high_copies.1 = bf16[32,32,512]{2,1,0:T(8,128)(2,1)} custom-call(bf16[32,4096]{1,0:T(8,128)(2,1)} %reduce-scatter.2.cloned.1.call-done.summed_ref, bf16[8,32,512]{2,1,0:T(8,128)(2,1)} %slice.16.resid_ref), custom_call_target="tpu_custom_call" | custom-call | tf_op jit(solution)/shard_map/high_copies/pallas_call | solution.py:38
  69.9 4.3 %all-to-all-start.2 = ((bf16[32,32,512]{2,1,0:T(8,128)(2,1)}), bf16[32,32,512]{2,1,0:T(8,128)(2,1)S(1)}, u32[]{:S(2)}, u32[]{:S(2)}) async-start(bf16[32,32,512]{2,1,0:T(8,128)(2,1)} %high_copies.1), calls=%async_computation.3 | async-start | bytes 2097152 | tf_op jit(solution)/shard_map/all_to_all | solution.py:206
  74.4 16.9 %all-to-all-done.2 = bf16[32,32,512]{2,1,0:T(8,128)(2,1)S(1)} async-done(((bf16[32,32,512]{2,1,0:T(8,128)(2,1)}), bf16[32,32,512]{2,1,0:T(8,128)(2,1)S(1)}, u32[]{:S(2)}, u32[]{:S(2)}) %all-to-all-start.2) | async-done | bytes 1048608 | tf_op jit(solution)/shard_map/all_to_all | solution.py:206
  91.3 1.9 copy-done.1
  93.2 2.4 %term_half.3 = bf16[4,1024,128]{2,1,0:T(8,128)(2,1)S(1)} custom-call(s32[2]{0:T(128)S(1)} %pad_add_fusion.1.half_ref, bf16[528,512]{1,0:T(8,128)(2,1)S(1)} %pad_maximum_fusion.p0, bf16[528,512]{1,0:T(8,128)(2,1)S(1)} %collective-permute-done.p1, bf16[528,512]{1,0:T(8,128)(2,1)S(1)} %collective-permute-done.1.p2, ...), custom_call_target="tpu_custom_call" | custom-call | flops 1610612736 | bytes 6291456 | tf_op jit(solution)/shard_map/term_half/pallas_call | solution.py:63
  95.5 4.4 %collective-permute-start.3 = (bf16[4,1024,128]{2,1,0:T(8,128)(2,1)S(1)}, bf16[4,1024,128]{2,1,0:T(8,128)(2,1)S(1)}, u32[]{:S(2)}, u32[]{:S(2)}) collective-permute-start(bf16[4,1024,128]{2,1,0:T(8,128)(2,1)S(1)} %term_half.3), channel_id=1, source_target_pairs={{0,1},{1,0},{2,3},{3,2},{4,5},{5,4},{6,7},{7,6},{8,9},{9,8},{10,11... | collective-permute-start | bytes 3145736 | tf_op jit(solution)/shard_map/ppermute | solution.py:210
  100.0 2.4 %term_half.2 = bf16[4,1024,128]{2,1,0:T(8,128)(2,1)S(1)} custom-call(s32[2]{0:T(128)S(1)} %pad_add_fusion.half_ref, bf16[528,512]{1,0:T(8,128)(2,1)S(1)} %pad_maximum_fusion.p0, bf16[528,512]{1,0:T(8,128)(2,1)S(1)} %collective-permute-done.p1, bf16[528,512]{1,0:T(8,128)(2,1)S(1)} %collective-permute-done.1.p2, ...), custom_call_target="tpu_custom_call" | custom-call | flops 1610612736 | bytes 6291456 | tf_op jit(solution)/shard_map/term_half/pallas_call | solution.py:63
  102.4 0.3 add_convert_fusion
  102.7 19.2 %all_to_all.32.terms_ref = bf16[4,1024,128]{2,1,0:T(8,128)(2,1)S(1)} all-to-all(bf16[4,1024,128]{2,1,0:T(8,128)(2,1)S(1)} %add_convert_fusion), channel_id=1, replica_groups=mesh['z'=16,'x'=4,'y'=4,'c'=2] {'y'}, dimensions={0} | all-to-all | bytes 2097152 | tf_op jit(solution)/shard_map/all_to_all | solution.py:213
  121.8 0.7 spread.1
  122.6 39.6 %all_to_all.33 = bf16[64,32,128]{2,1,0:T(8,128)(2,1)} all-to-all(bf16[64,32,128]{2,1,0:T(8,128)(2,1)S(1)} %spread.1), channel_id=1, replica_groups=mesh['z'=16,'x'=4,'y'=4,'c'=2] {'z','x'}, dimensions={0} | all-to-all | bytes 1048576 | tf_op jit(solution)/shard_map/all_to_all | solution.py:215
  162.3 7.9 %all-to-all-start.5 = ((bf16[8,256,128]{2,1,0:T(8,128)(2,1)}), bf16[8,256,128]{2,1,0:T(8,128)(2,1)S(1)}, u32[]{:S(2)}, u32[]{:S(2)}) async-start(bf16[8,256,128]{2,1,0:T(8,128)(2,1)} %bitcast.14), calls=%async_computation.6 | async-start | bytes 1048576 | tf_op jit(solution)/shard_map/all_to_all | solution.py:216
  170.1 0.8 slice.17
  171.5 8.1 %all-to-all-done.5 = bf16[8,256,128]{2,1,0:T(8,128)(2,1)S(1)} async-done(((bf16[8,256,128]{2,1,0:T(8,128)(2,1)}), bf16[8,256,128]{2,1,0:T(8,128)(2,1)S(1)}, u32[]{:S(2)}, u32[]{:S(2)}) %all-to-all-start.5) | async-done | bytes 524320 | tf_op jit(solution)/shard_map/all_to_all | solution.py:216
  179.7 4.9 %chain.1 = (f32[64,4096]{1,0:T(8,128)}, bf16[64,4096]{1,0:T(8,128)(2,1)}) custom-call(bf16[8,8,32,128]{3,2,1,0:T(8,128)(2,1)S(1)} %bitcast.28, bf16[64,128]{1,0:T(8,128)(2,1)S(1)} %copy.28.goal_ref, bf16[64,128]{1,0:T(8,128)(2,1)S(1)} %broadcast_in_dim.43.left_ref, bf16[4096,128]{1,0:T(8,128)(2,1)S(1)} %copy-done.3, bf16[128,4096]{1,0:T(8,128)(2,1)S(1)} %copy-done.4), custom_call_target="tpu_custom_call" | custom-call | tf_op jit(solution)/shard_map/chain/pallas_call | solution.py:159
  (56 shorter events, 2.1 us)
Async XLA Ops:
  8.0 12.1 %copy-start = (bf16[256,128]{1,0:T(8,128)(2,1)S(1)}, bf16[256,128]{1,0:T(8,128)(2,1)}, u32[]{:S(2)}) copy-start(bf16[256,128]{1,0:T(8,128)(2,1)} %param.18) | copy-start | bytes 196612
  8.0 1.4 copy-start.9
  8.0 1.6 copy-start.7
  8.0 1.6 copy-start.8
  8.0 11.8 %copy-start.11 = (s32[1,8]{1,0:T(1,128)S(1)}, s32[1,8]{1,0:T(1,128)}, u32[]{:S(2)}) copy-start(s32[1,8]{1,0:T(1,128)} %param.19) | copy-start | bytes 100
  8.1 12.3 %copy-start.10 = (s32[256]{0:T(256)S(1)}, s32[256]{0:T(256)}, u32[]{:S(2)}) copy-start(s32[256]{0:T(256)} %param.20) | copy-start | bytes 3076
  8.1 43.7 %copy-start.6 = (bf16[256,512]{1,0:T(8,128)(2,1)S(1)}, bf16[256,512]{1,0:T(8,128)(2,1)}, u32[]{:S(2)}) copy-start(bf16[256,512]{1,0:T(8,128)(2,1)} %param.12) | copy-start | bytes 786436
  8.1 59.8 %reduce-scatter.2.cloned.1.call-start = ((), (), s32[]{:S(2)}) async-start(), calls=%async_computation.7 | async-start | bytes 2359296 | tf_op jit(solution)/shard_map/reduce_scatter | solution.py:181
  8.8 82.5 %all-gather.3.cloned.1.call-start = ((), (), s32[]{:S(2)}) async-start(), calls=%async_computation.8 | async-start | bytes 3342336 | tf_op jit(solution)/shard_map/all_gather | solution.py:180
  9.7 60.2 %collective-permute-start.2 = (bf16[528,512]{1,0:T(8,128)(2,1)S(1)}, bf16[528,512]{1,0:T(8,128)(2,1)S(1)}, u32[]{:S(2)}, u32[]{:S(2)}) collective-permute-start(bf16[528,512]{1,0:T(8,128)(2,1)S(1)} %pad_maximum_fusion.p0), channel_id=1, source_target_pairs={{0,24},{8,0},{16,8},{24,16},{1,25},{9,1},{17,9},{25,17},{2,26},{10... | collective-permute-start | bytes 1622024 | tf_op jit(solution)/shard_map/ppermute | solution.py:189
  14.9 55.0 %collective-permute-start.1 = (bf16[528,512]{1,0:T(8,128)(2,1)S(1)}, bf16[528,512]{1,0:T(8,128)(2,1)S(1)}, u32[]{:S(2)}, u32[]{:S(2)}) collective-permute-start(bf16[528,512]{1,0:T(8,128)(2,1)S(1)} %pad_maximum_fusion.p0), channel_id=1, source_target_pairs={{0,16},{8,24},{16,0},{24,8},{1,17},{9,25},{17,1},{25,9},{2,18},{10... | collective-permute-start | bytes 1622024 | tf_op jit(solution)/shard_map/ppermute | solution.py:189
  17.4 52.6 %collective-permute-start = (bf16[528,512]{1,0:T(8,128)(2,1)S(1)}, bf16[528,512]{1,0:T(8,128)(2,1)S(1)}, u32[]{:S(2)}, u32[]{:S(2)}) collective-permute-start(bf16[528,512]{1,0:T(8,128)(2,1)S(1)} %pad_maximum_fusion.p0), channel_id=1, source_target_pairs={{0,8},{8,16},{16,24},{24,0},{1,9},{9,17},{17,25},{25,1},{2,10},{10... | collective-permute-start | bytes 1622024 | tf_op jit(solution)/shard_map/ppermute | solution.py:189
  66.4 0.7 copy-start.5
  69.9 21.3 %all-to-all-start.2 = ((bf16[32,32,512]{2,1,0:T(8,128)(2,1)}), bf16[32,32,512]{2,1,0:T(8,128)(2,1)S(1)}, u32[]{:S(2)}, u32[]{:S(2)}) async-start(bf16[32,32,512]{2,1,0:T(8,128)(2,1)} %high_copies.1), calls=%async_computation.3 | async-start | bytes 2097152 | tf_op jit(solution)/shard_map/all_to_all | solution.py:206
  91.3 1.9 copy-start.1
  93.2 6.8 %copy-start.2 = (bf16[48,64,512]{2,1,0:T(8,128)(2,1)S(1)}, bf16[48,64,512]{2,1,0:T(8,128)(2,1)}, u32[]{:S(2)}) copy-start(bf16[48,64,512]{2,1,0:T(8,128)(2,1)} %all-gather.3.cloned.1.call-done) | copy-start | bytes 9437188
  95.5 6.8 %collective-permute-start.3 = (bf16[4,1024,128]{2,1,0:T(8,128)(2,1)S(1)}, bf16[4,1024,128]{2,1,0:T(8,128)(2,1)S(1)}, u32[]{:S(2)}, u32[]{:S(2)}) collective-permute-start(bf16[4,1024,128]{2,1,0:T(8,128)(2,1)S(1)} %term_half.3), channel_id=1, source_target_pairs={{0,1},{1,0},{2,3},{3,2},{4,5},{5,4},{6,7},{7,6},{8,9},{9,8},{10,11... | collective-permute-start | bytes 3145736 | tf_op jit(solution)/shard_map/ppermute | solution.py:210
  122.6 57.1 %copy-start.3 = (bf16[4096,128]{1,0:T(8,128)(2,1)S(1)}, bf16[4096,128]{1,0:T(8,128)(2,1)}, u32[]{:S(2)}) copy-start(bf16[4096,128]{1,0:T(8,128)(2,1)} %in_ref.1) | copy-start | bytes 3145732
  122.6 57.1 %copy-start.4 = (bf16[128,4096]{1,0:T(8,128)(2,1)S(1)}, bf16[128,4096]{1,0:T(8,128)(2,1)}, u32[]{:S(2)}) copy-start(bf16[128,4096]{1,0:T(8,128)(2,1)} %out_ref.1) | copy-start | bytes 3145732
  162.3 17.4 %all-to-all-start.5 = ((bf16[8,256,128]{2,1,0:T(8,128)(2,1)}), bf16[8,256,128]{2,1,0:T(8,128)(2,1)S(1)}, u32[]{:S(2)}, u32[]{:S(2)}) async-start(bf16[8,256,128]{2,1,0:T(8,128)(2,1)} %bitcast.14), calls=%async_computation.6 | async-start | bytes 1048576 | tf_op jit(solution)/shard_map/all_to_all | solution.py:216
Sparse Core Ops, SparseCore 0:
  11.7 45.4 reduce-scatter.1
Sparse Core Ops, SparseCore 1:
  11.4 73.4 all-gather.2

commit v13 on v12

--- a/solution.py
+++ b/solution.py
@@ -46,17 +46,20 @@
 
 def term_kernel(half_ref, p0, p1, p2, p3, high_ref, rows_ref, out_ref):
     half = half_ref[0]
+    pairs = (p0, p1, p2, p3)
+    lows = jnp.concatenate([pair_ref[0:256] for pair_ref in pairs], axis=0)
+    mids = jnp.concatenate([pair_ref[256:512] for pair_ref in pairs], axis=0)
+    highs = jnp.concatenate(
+        [high_ref[lax.rem(half_ref[1] + (4 - group), 4)] for group in range(4)], axis=0
+    )
     for i in range(2):
         weights = [rows_ref[i, :, half, :, piece].reshape(256, 512) for piece in range(3)]
-        for group, pair_ref in enumerate((p0, p1, p2, p3)):
-            total = dot(pair_ref[0:256], weights[0], NT)
-            total += dot(pair_ref[256:512], weights[1], NT)
-            total += dot(high_ref[lax.rem(half_ref[1] + (4 - group), 4)], weights[2], NT)
-            total = total.astype(BF)
-            for part in range(2):
-                out_ref[2 * i + part, group * 256 : (group + 1) * 256, :] = total[
-                    :, part * 128 : (part + 1) * 128
-                ]
+        total = dot(lows, weights[0], NT)
+        total += dot(mids, weights[1], NT)
+        total += dot(highs, weights[2], NT)
+        total = total.astype(BF)
+        for part in range(2):
+            out_ref[2 * i + part] = total[:, part * 128 : (part + 1) * 128]
 
 
 def term_half(half, pairs, high, rows):

time: 193 us -> 193 us (level)
  no operation moved by 1% of the time
where the time goes in v13:
time: 193 us; the launch traced here: 192 us
  blocking collectives  104 us (54%)
  starting transfers between devices  26.8 us (14%)
  waiting for transfers between devices  26.2 us (14%)
  between operations  15.8 us (8%)
  Pallas kernels  12.5 us (6%)
  local copies, waits for them, and re-layouts  5.25 us (3%)
    all_to_all x1, blocking collectives, per_device(): moved = lax.all_to_all(moved, dp, split_axis=0, concat_axis=0, tiled=True)  39.7 us
    all_to_all x1, blocking collectives, per_device(): lax.all_to_all(side.reshape(64, 2, 128), dp, split_axis=0, concat_axis=0,...  30.8 us
    all_to_all x1, blocking collectives, per_device(): terms = lax.all_to_all(terms, 'y', split_axis=0, concat_axis=0, tiled=True)  19.2 us
    all_to_all x1, waiting for transfers between devices, per_device(): lax.all_to_all(high, ('x',) + tensor, split_axis=0, concat_axis=0, tiled=...  16.9 us
    all_to_all x1, blocking collectives, per_device(): side = lax.all_to_all(side, tensor, split_axis=0, concat_axis=0, tiled=True)  14.6 us
    ppermute x3, starting transfers between devices, per_device(): lax.ppermute(pair, 'x', ring(4, shift))  10.2 us
    all_to_all x1, waiting for transfers between devices, per_device(): lax.all_to_all(moved.reshape(8, 256, 128), tensor, split_axis=0, concat_a...  8.1 us
    all_to_all x1, starting transfers between devices, per_device(): lax.all_to_all(moved.reshape(8, 256, 128), tensor, split_axis=0, concat_a...  7.88 us
  transfers between devices with their start and end apart: 8, of which 2 were waited for; matrix products, arithmetic and copies ran while one was open for 2% of the time, Pallas kernels for 2%

profile of v13, /device:TPU:1, one launch (start us, length us, event | category | flops | bytes accessed | tf_op | source)
XLA Modules:
  0.0 192.1 jit_solution(16675452726333039670)
XLA Ops:
  8.1 0.7 reduce-scatter.2.cloned.1.call-update
  8.9 0.5 all-gather.3.cloned.1.call-update
  9.7 5.2 %collective-permute-start.2 = (bf16[528,512]{1,0:T(8,128)(2,1)S(1)}, bf16[528,512]{1,0:T(8,128)(2,1)S(1)}, u32[]{:S(2)}, u32[]{:S(2)}) collective-permute-start(bf16[528,512]{1,0:T(8,128)(2,1)S(1)} %pad_maximum_fusion.p0), channel_id=1, source_target_pairs={{0,24},{8,0},{16,8},{24,16},{1,25},{9,1},{17,9},{25,17},{2,26},{10... | collective-permute-start | bytes 1622024 | tf_op jit(solution)/shard_map/ppermute | solution.py:192
  14.9 2.4 %collective-permute-start.1 = (bf16[528,512]{1,0:T(8,128)(2,1)S(1)}, bf16[528,512]{1,0:T(8,128)(2,1)S(1)}, u32[]{:S(2)}, u32[]{:S(2)}) collective-permute-start(bf16[528,512]{1,0:T(8,128)(2,1)S(1)} %pad_maximum_fusion.p0), channel_id=1, source_target_pairs={{0,16},{8,24},{16,0},{24,8},{1,17},{9,25},{17,1},{25,9},{2,18},{10... | collective-permute-start | bytes 1622024 | tf_op jit(solution)/shard_map/ppermute | solution.py:192
  17.4 2.5 %collective-permute-start = (bf16[528,512]{1,0:T(8,128)(2,1)S(1)}, bf16[528,512]{1,0:T(8,128)(2,1)S(1)}, u32[]{:S(2)}, u32[]{:S(2)}) collective-permute-start(bf16[528,512]{1,0:T(8,128)(2,1)S(1)} %pad_maximum_fusion.p0), channel_id=1, source_target_pairs={{0,8},{8,16},{16,24},{24,0},{1,9},{9,17},{17,25},{25,1},{2,10},{10... | collective-permute-start | bytes 1622024 | tf_op jit(solution)/shard_map/ppermute | solution.py:192
  20.9 30.8 %all_to_all.30 = bf16[64,2,128]{2,1,0:T(2,128)(2,1)S(1)} all-to-all(bf16[64,2,128]{2,1,0:T(2,128)(2,1)S(1)} %reshape.87), channel_id=1, replica_groups=mesh['z'=16,'x'=4,'y'=4,'c'=2] {'z','x'}, dimensions={0} | all-to-all | bytes 65536 | tf_op jit(solution)/shard_map/all_to_all | solution.py:199
  51.8 14.6 %all_to_all.31 = bf16[8,36,512]{2,1,0:T(8,128)(2,1)S(1)} all-to-all(bf16[8,36,512]{2,1,0:T(8,128)(2,1)S(1)} %pad_maximum_fusion.1), channel_id=1, replica_groups=mesh['z'=16,'x'=4,'y'=4,'c'=2] {'y','c'}, dimensions={0} | all-to-all | bytes 589824 | tf_op jit(solution)/shard_map/all_to_all | solution.py:202
  66.4 0.7 copy-done.5
  67.1 0.7 slice.16.resid_ref
  67.8 2.1 %high_copies.1 = bf16[32,32,512]{2,1,0:T(8,128)(2,1)} custom-call(bf16[32,4096]{1,0:T(8,128)(2,1)} %reduce-scatter.2.cloned.1.call-done.summed_ref, bf16[8,32,512]{2,1,0:T(8,128)(2,1)} %slice.16.resid_ref), custom_call_target="tpu_custom_call" | custom-call | tf_op jit(solution)/shard_map/high_copies/pallas_call | solution.py:38
  69.9 4.3 %all-to-all-start.2 = ((bf16[32,32,512]{2,1,0:T(8,128)(2,1)}), bf16[32,32,512]{2,1,0:T(8,128)(2,1)S(1)}, u32[]{:S(2)}, u32[]{:S(2)}) async-start(bf16[32,32,512]{2,1,0:T(8,128)(2,1)} %high_copies.1), calls=%async_computation.3 | async-start | bytes 2097152 | tf_op jit(solution)/shard_map/all_to_all | solution.py:209
  74.4 16.9 %all-to-all-done.2 = bf16[32,32,512]{2,1,0:T(8,128)(2,1)S(1)} async-done(((bf16[32,32,512]{2,1,0:T(8,128)(2,1)}), bf16[32,32,512]{2,1,0:T(8,128)(2,1)S(1)}, u32[]{:S(2)}, u32[]{:S(2)}) %all-to-all-start.2) | async-done | bytes 1048608 | tf_op jit(solution)/shard_map/all_to_all | solution.py:209
  91.3 1.9 copy-done.1
  93.2 2.4 %term_half.3 = bf16[4,1024,128]{2,1,0:T(8,128)(2,1)S(1)} custom-call(s32[2]{0:T(128)S(1)} %pad_add_fusion.1.half_ref, bf16[528,512]{1,0:T(8,128)(2,1)S(1)} %pad_maximum_fusion.p0, bf16[528,512]{1,0:T(8,128)(2,1)S(1)} %collective-permute-done.p1, bf16[528,512]{1,0:T(8,128)(2,1)S(1)} %collective-permute-done.1.p2, ...), custom_call_target="tpu_custom_call" | custom-call | flops 1610612736 | bytes 6291456 | tf_op jit(solution)/shard_map/term_half/pallas_call | solution.py:66
  95.5 4.4 %collective-permute-start.3 = (bf16[4,1024,128]{2,1,0:T(8,128)(2,1)S(1)}, bf16[4,1024,128]{2,1,0:T(8,128)(2,1)S(1)}, u32[]{:S(2)}, u32[]{:S(2)}) collective-permute-start(bf16[4,1024,128]{2,1,0:T(8,128)(2,1)S(1)} %term_half.3), channel_id=1, source_target_pairs={{0,1},{1,0},{2,3},{3,2},{4,5},{5,4},{6,7},{7,6},{8,9},{9,8},{10,11... | collective-permute-start | bytes 3145736 | tf_op jit(solution)/shard_map/ppermute | solution.py:213
  100.0 2.4 %term_half.2 = bf16[4,1024,128]{2,1,0:T(8,128)(2,1)S(1)} custom-call(s32[2]{0:T(128)S(1)} %pad_add_fusion.half_ref, bf16[528,512]{1,0:T(8,128)(2,1)S(1)} %pad_maximum_fusion.p0, bf16[528,512]{1,0:T(8,128)(2,1)S(1)} %collective-permute-done.p1, bf16[528,512]{1,0:T(8,128)(2,1)S(1)} %collective-permute-done.1.p2, ...), custom_call_target="tpu_custom_call" | custom-call | flops 1610612736 | bytes 6291456 | tf_op jit(solution)/shard_map/term_half/pallas_call | solution.py:66
  102.4 0.3 add_convert_fusion
  102.7 19.2 %all_to_all.32.terms_ref = bf16[4,1024,128]{2,1,0:T(8,128)(2,1)S(1)} all-to-all(bf16[4,1024,128]{2,1,0:T(8,128)(2,1)S(1)} %add_convert_fusion), channel_id=1, replica_groups=mesh['z'=16,'x'=4,'y'=4,'c'=2] {'y'}, dimensions={0} | all-to-all | bytes 2097152 | tf_op jit(solution)/shard_map/all_to_all | solution.py:216
  121.8 0.7 spread.1
  122.6 39.7 %all_to_all.33 = bf16[64,32,128]{2,1,0:T(8,128)(2,1)} all-to-all(bf16[64,32,128]{2,1,0:T(8,128)(2,1)S(1)} %spread.1), channel_id=1, replica_groups=mesh['z'=16,'x'=4,'y'=4,'c'=2] {'z','x'}, dimensions={0} | all-to-all | bytes 1048576 | tf_op jit(solution)/shard_map/all_to_all | solution.py:218
  162.3 7.9 %all-to-all-start.5 = ((bf16[8,256,128]{2,1,0:T(8,128)(2,1)}), bf16[8,256,128]{2,1,0:T(8,128)(2,1)S(1)}, u32[]{:S(2)}, u32[]{:S(2)}) async-start(bf16[8,256,128]{2,1,0:T(8,128)(2,1)} %bitcast.14), calls=%async_computation.6 | async-start | bytes 1048576 | tf_op jit(solution)/shard_map/all_to_all | solution.py:219
  170.1 0.8 slice.17
  171.5 8.1 %all-to-all-done.5 = bf16[8,256,128]{2,1,0:T(8,128)(2,1)S(1)} async-done(((bf16[8,256,128]{2,1,0:T(8,128)(2,1)}), bf16[8,256,128]{2,1,0:T(8,128)(2,1)S(1)}, u32[]{:S(2)}, u32[]{:S(2)}) %all-to-all-start.5) | async-done | bytes 524320 | tf_op jit(solution)/shard_map/all_to_all | solution.py:219
  179.7 4.9 %chain.1 = (f32[64,4096]{1,0:T(8,128)}, bf16[64,4096]{1,0:T(8,128)(2,1)}) custom-call(bf16[8,8,32,128]{3,2,1,0:T(8,128)(2,1)S(1)} %bitcast.28, bf16[64,128]{1,0:T(8,128)(2,1)S(1)} %copy.28.goal_ref, bf16[64,128]{1,0:T(8,128)(2,1)S(1)} %broadcast_in_dim.43.left_ref, bf16[4096,128]{1,0:T(8,128)(2,1)S(1)} %copy-done.3, bf16[128,4096]{1,0:T(8,128)(2,1)S(1)} %copy-done.4), custom_call_target="tpu_custom_call" | custom-call | tf_op jit(solution)/shard_map/chain/pallas_call | solution.py:162
  (56 shorter events, 2.1 us)
Async XLA Ops:
  8.0 12.1 %copy-start = (bf16[256,128]{1,0:T(8,128)(2,1)S(1)}, bf16[256,128]{1,0:T(8,128)(2,1)}, u32[]{:S(2)}) copy-start(bf16[256,128]{1,0:T(8,128)(2,1)} %param.18) | copy-start | bytes 196612
  8.0 1.4 copy-start.9
  8.0 1.6 copy-start.7
  8.0 1.6 copy-start.8
  8.0 11.8 %copy-start.11 = (s32[1,8]{1,0:T(1,128)S(1)}, s32[1,8]{1,0:T(1,128)}, u32[]{:S(2)}) copy-start(s32[1,8]{1,0:T(1,128)} %param.19) | copy-start | bytes 100
  8.1 12.3 %copy-start.10 = (s32[256]{0:T(256)S(1)}, s32[256]{0:T(256)}, u32[]{:S(2)}) copy-start(s32[256]{0:T(256)} %param.20) | copy-start | bytes 3076
  8.1 43.7 %copy-start.6 = (bf16[256,512]{1,0:T(8,128)(2,1)S(1)}, bf16[256,512]{1,0:T(8,128)(2,1)}, u32[]{:S(2)}) copy-start(bf16[256,512]{1,0:T(8,128)(2,1)} %param.12) | copy-start | bytes 786436
  8.1 59.8 %reduce-scatter.2.cloned.1.call-start = ((), (), s32[]{:S(2)}) async-start(), calls=%async_computation.7 | async-start | bytes 2359296 | tf_op jit(solution)/shard_map/reduce_scatter | solution.py:184
  8.8 82.5 %all-gather.3.cloned.1.call-start = ((), (), s32[]{:S(2)}) async-start(), calls=%async_computation.8 | async-start | bytes 3342336 | tf_op jit(solution)/shard_map/all_gather | solution.py:183
  9.7 60.2 %collective-permute-start.2 = (bf16[528,512]{1,0:T(8,128)(2,1)S(1)}, bf16[528,512]{1,0:T(8,128)(2,1)S(1)}, u32[]{:S(2)}, u32[]{:S(2)}) collective-permute-start(bf16[528,512]{1,0:T(8,128)(2,1)S(1)} %pad_maximum_fusion.p0), channel_id=1, source_target_pairs={{0,24},{8,0},{16,8},{24,16},{1,25},{9,1},{17,9},{25,17},{2,26},{10... | collective-permute-start | bytes 1622024 | tf_op jit(solution)/shard_map/ppermute | solution.py:192
  14.9 55.0 %collective-permute-start.1 = (bf16[528,512]{1,0:T(8,128)(2,1)S(1)}, bf16[528,512]{1,0:T(8,128)(2,1)S(1)}, u32[]{:S(2)}, u32[]{:S(2)}) collective-permute-start(bf16[528,512]{1,0:T(8,128)(2,1)S(1)} %pad_maximum_fusion.p0), channel_id=1, source_target_pairs={{0,16},{8,24},{16,0},{24,8},{1,17},{9,25},{17,1},{25,9},{2,18},{10... | collective-permute-start | bytes 1622024 | tf_op jit(solution)/shard_map/ppermute | solution.py:192
  17.4 52.6 %collective-permute-start = (bf16[528,512]{1,0:T(8,128)(2,1)S(1)}, bf16[528,512]{1,0:T(8,128)(2,1)S(1)}, u32[]{:S(2)}, u32[]{:S(2)}) collective-permute-start(bf16[528,512]{1,0:T(8,128)(2,1)S(1)} %pad_maximum_fusion.p0), channel_id=1, source_target_pairs={{0,8},{8,16},{16,24},{24,0},{1,9},{9,17},{17,25},{25,1},{2,10},{10... | collective-permute-start | bytes 1622024 | tf_op jit(solution)/shard_map/ppermute | solution.py:192
  66.4 0.7 copy-start.5
  69.9 21.3 %all-to-all-start.2 = ((bf16[32,32,512]{2,1,0:T(8,128)(2,1)}), bf16[32,32,512]{2,1,0:T(8,128)(2,1)S(1)}, u32[]{:S(2)}, u32[]{:S(2)}) async-start(bf16[32,32,512]{2,1,0:T(8,128)(2,1)} %high_copies.1), calls=%async_computation.3 | async-start | bytes 2097152 | tf_op jit(solution)/shard_map/all_to_all | solution.py:209
  91.3 1.9 copy-start.1
  93.2 6.8 %copy-start.2 = (bf16[48,64,512]{2,1,0:T(8,128)(2,1)S(1)}, bf16[48,64,512]{2,1,0:T(8,128)(2,1)}, u32[]{:S(2)}) copy-start(bf16[48,64,512]{2,1,0:T(8,128)(2,1)} %all-gather.3.cloned.1.call-done) | copy-start | bytes 9437188
  95.5 6.8 %collective-permute-start.3 = (bf16[4,1024,128]{2,1,0:T(8,128)(2,1)S(1)}, bf16[4,1024,128]{2,1,0:T(8,128)(2,1)S(1)}, u32[]{:S(2)}, u32[]{:S(2)}) collective-permute-start(bf16[4,1024,128]{2,1,0:T(8,128)(2,1)S(1)} %term_half.3), channel_id=1, source_target_pairs={{0,1},{1,0},{2,3},{3,2},{4,5},{5,4},{6,7},{7,6},{8,9},{9,8},{10,11... | collective-permute-start | bytes 3145736 | tf_op jit(solution)/shard_map/ppermute | solution.py:213
  122.6 57.1 %copy-start.3 = (bf16[4096,128]{1,0:T(8,128)(2,1)S(1)}, bf16[4096,128]{1,0:T(8,128)(2,1)}, u32[]{:S(2)}) copy-start(bf16[4096,128]{1,0:T(8,128)(2,1)} %in_ref.1) | copy-start | bytes 3145732
  122.6 57.1 %copy-start.4 = (bf16[128,4096]{1,0:T(8,128)(2,1)S(1)}, bf16[128,4096]{1,0:T(8,128)(2,1)}, u32[]{:S(2)}) copy-start(bf16[128,4096]{1,0:T(8,128)(2,1)} %out_ref.1) | copy-start | bytes 3145732
  162.3 17.4 %all-to-all-start.5 = ((bf16[8,256,128]{2,1,0:T(8,128)(2,1)}), bf16[8,256,128]{2,1,0:T(8,128)(2,1)S(1)}, u32[]{:S(2)}, u32[]{:S(2)}) async-start(bf16[8,256,128]{2,1,0:T(8,128)(2,1)} %bitcast.14), calls=%async_computation.6 | async-start | bytes 1048576 | tf_op jit(solution)/shard_map/all_to_all | solution.py:219
Sparse Core Ops, SparseCore 0:
  11.7 45.4 reduce-scatter.1
Sparse Core Ops, SparseCore 1:
  11.4 73.4 all-gather.2
